TPU v7x, 32 devices: a whole 2x2x4 slice. The times are simulated.
32 devices in a mesh: parts: 2 (over y), replica: 4 (over x, core), tensor: 4 (over z).
Axes of the slice: x: 2, y: 2, z: 4, core: 2. Of those that a mesh axis runs over, the one named last changes fastest.
Arguments:
- act_codes: bfloat16 [256, 8192], P(('parts', 'replica'), 'tensor'), parts along dimension 0, may hold values from -128 to 127, as said below
- act_scale: float32 [256], P('parts'), parts along dimension 0, may hold values from 0.006 to 0.02
- adapter_ids: int32 [256], P(('parts', 'replica')), parts along dimension 0, may hold values from 0 to 7, as said below
- seg_starts: int32 [8, 4], P('parts'), parts along dimension 0, may hold values from 0 to 32, as said below
- pool_index: int32 [16], P('parts'), parts along dimension 0, may hold values from 0 to 7, as said below
- gate_levels: bfloat16 [8192, 32768], P(None, ('replica', 'tensor')), may hold values from -8 to 7, as said below
- gate_scale: float32 [64, 32768], P(None, ('replica', 'tensor')), may hold values from 0.0008 to 0.0035
- up_levels: bfloat16 [8192, 32768], P(None, ('replica', 'tensor')), may hold values from -8 to 7, as said below
- up_scale: float32 [64, 32768], P(None, ('replica', 'tensor')), may hold values from 0.0008 to 0.0035
- down_levels: bfloat16 [32768, 8192], P(('replica', 'tensor')), may hold values from -8 to 7, as said below
- down_scale: float32 [256, 8192], P(('replica', 'tensor')), may hold values from 0.0006 to 0.0024
- shrink_weight: bfloat16 [32768, 512], P(('replica', 'tensor')), may hold values from -0.03125 to 0.03125
- expand_matrix_rows: bfloat16 [8, 64, 8192], P('replica', None, 'tensor'), may hold values from -1.5 to 1.5
Outputs:
- mixed: bfloat16 [256, 8192], P(('parts', 'replica'), 'tensor'), parts along dimension 0
There are 2 independent parts, one for each index of `parts`. A program takes and returns all parts, laid end to end along the dimension named above; an argument that names none is the same for every part. Nothing has to cross between parts.
Inputs may be any that keep to these rules, and one draw needn't show every extreme that they name: `act_codes`: whole numbers. `gate_levels`: whole numbers. `up_levels`: whole numbers. `down_levels`: whole numbers. `pool_index`: each adapter's pool row; every pool row is used once. Pool rows a * 2 to a * 2 + 1 are held by replica a. `seg_starts`: row r starts with 0 and rises strictly over its live slots; the unused slots after them hold 32. Some replica uses all 4 slots. The segments of one replica name distinct adapters, at most 1 of them held by any one replica; some replica takes exactly 1 from every replica. `adapter_ids`: equal within each segment of a replica.
All inputs are finite; a program needn't handle non-finite values.
Results may differ from a plain program's by a relative error of at most 0.0095.
Values may be sent and summed in bfloat16 or wider, within the bound.
No kernel may reach another device: no remote copies, remote signals or barrier semaphores. Data moves between devices by JAX's collectives and lax.ppermute only.
A program may use at most 384 MiB of HBM per device.

v0:
```python
import jax
import jax.numpy as jnp
from jax import lax
from jax.sharding import PartitionSpec as P


def dequantize(levels, scales):
    values = levels.astype(jnp.float32)
    rows = values.shape[0]
    groups = scales.shape[0]
    scaled = values.reshape(groups, rows // groups, values.shape[1]) * scales[:, None, :]
    return scaled.reshape(rows, values.shape[1]).astype(jnp.bfloat16)


def segment_tables(all_ids, seg_starts, pool_index, rows_dev):
    replicas = seg_starts.shape[0]
    positions = jnp.arange(rows_dev, dtype=jnp.int32)
    row_slot = jnp.sum(
        (seg_starts[:, None, 1:] <= positions[None, :, None]).astype(jnp.int32), axis=2
    )
    clipped = jnp.minimum(seg_starts, rows_dev - 1)
    flat_rows = clipped + (jnp.arange(replicas, dtype=jnp.int32) * rows_dev)[:, None]
    slot_adapter = jnp.take(all_ids, flat_rows)
    slot_pool = jnp.take(pool_index, slot_adapter)
    following = jnp.concatenate(
        [seg_starts[:, 1:], jnp.full((replicas, 1), rows_dev, jnp.int32)], axis=1
    )
    live = following > seg_starts
    row_pool = jnp.take_along_axis(slot_pool, row_slot, axis=1)
    return (row_slot, slot_pool, live, row_pool)


def spread_rows(onehot, low):
    widened = onehot[:, :, None] * low[:, None, :].astype(jnp.float32)
    return widened.reshape(onehot.shape[0], onehot.shape[1] * low.shape[1]).astype(jnp.bfloat16)


def local(
    act_codes,
    act_scale,
    adapter_ids,
    seg_starts,
    pool_index,
    gate_levels,
    gate_scale,
    up_levels,
    up_scale,
    down_levels,
    down_scale,
    shrink_weight,
    expand_matrix_rows,
):
    my_replica = lax.axis_index("replica")
    rows_dev = adapter_ids.shape[0]
    adapters = pool_index.shape[0]
    rank = expand_matrix_rows.shape[1]
    columns = expand_matrix_rows.shape[2]
    feature_codes = lax.all_gather(act_codes, "tensor", axis=1, tiled=True)
    inputs, all_ids = (
        lax.all_gather(feature_codes, "replica", axis=0, tiled=True),
        lax.all_gather(adapter_ids, "replica", axis=0, tiled=True),
    )
    row_slot, slot_pool, live, row_pool = segment_tables(all_ids, seg_starts, pool_index, rows_dev)
    gate = act_scale[:, None] * jnp.dot(
        inputs, dequantize(gate_levels, gate_scale), preferred_element_type=jnp.float32
    )
    up = act_scale[:, None] * jnp.dot(
        inputs, dequantize(up_levels, up_scale), preferred_element_type=jnp.float32
    )
    hidden = (jax.nn.silu(gate) * up).astype(jnp.bfloat16)
    w_down = dequantize(down_levels, down_scale)
    flat_pool = row_pool.reshape(-1)
    choose = (flat_pool[:, None] == jnp.arange(adapters, dtype=jnp.int32)[None, :]).astype(
        jnp.float32
    )
    project = jnp.dot(hidden, shrink_weight, preferred_element_type=jnp.float32)
    partial_value = jnp.sum(
        project.reshape(flat_pool.shape[0], adapters, rank) * choose[:, :, None], axis=1
    )
    total = lax.psum(partial_value, ("replica", "tensor"))
    mine = lax.dynamic_slice_in_dim(total, my_replica * rows_dev, rows_dev, 0)
    low = mine.astype(jnp.bfloat16)
    whole_pool = lax.all_gather(expand_matrix_rows, "replica", axis=0, tiled=True)
    my_pool = jnp.take(row_pool, my_replica, axis=0)
    onehot = (my_pool[:, None] == jnp.arange(adapters, dtype=jnp.int32)[None, :]).astype(
        jnp.float32
    )
    adapter_delta = jnp.dot(
        spread_rows(onehot, low),
        whole_pool.reshape(adapters * rank, columns),
        preferred_element_type=jnp.float32,
    )
    base_output = lax.psum_scatter(
        jnp.dot(hidden, w_down, preferred_element_type=jnp.float32).astype(jnp.bfloat16),
        "replica",
        scatter_dimension=0,
        tiled=True,
    ).astype(jnp.float32)
    base_output = lax.psum_scatter(
        base_output.astype(jnp.bfloat16), "tensor", scatter_dimension=1, tiled=True
    ).astype(jnp.float32)
    return (base_output + adapter_delta).astype(jnp.bfloat16)


def solution(mesh):
    placed = (
        P(("parts", "replica"), "tensor"),
        P("parts"),
        P(("parts", "replica")),
        P("parts", None),
        P("parts"),
        P(None, ("replica", "tensor")),
        P(None, ("replica", "tensor")),
        P(None, ("replica", "tensor")),
        P(None, ("replica", "tensor")),
        P(("replica", "tensor"), None),
        P(("replica", "tensor"), None),
        P(("replica", "tensor"), None),
        P("replica", None, "tensor"),
    )
    return jax.shard_map(
        local,
        mesh=mesh,
        in_specs=placed,
        out_specs=P(("parts", "replica"), "tensor"),
        check_vma=False,
    )
```

profile of v0, /device:TPU:0, one launch (start us, length us, event | category | flops | bytes accessed | tf_op | source)
XLA Modules:
  0.0 248.1 jit_solution(3836526410395391556)
XLA Ops:
  6.5 0.0 copy-start
  6.5 19.5 %all_gather.12 = bf16[32,8192]{1,0:T(8,128)(2,1)} all-gather(bf16[32,2048]{1,0:T(8,128)(2,1)} %param.13), channel_id=1, replica_groups=mesh['parts'=2,'replica'=4,'tensor'=4] {'tensor'}, dimensions={1}, use_global_device_ids=true | all-gather | bytes 655360 | tf_op jit(solution)/shard_map/all_gather | solution.py:58
  26.0 0.0 all-gather.3.cloned.1.call-update
  26.0 0.0 copy-start.2
  26.0 0.0 reduce-scatter.3.cloned.1.call-start
  26.1 23.7 %fusion.2 = bf16[8192,2048]{1,0:T(8,128)(2,1)} fusion(bf16[8192,2048]{1,0:T(8,128)(2,1)} %param.18, f32[64,2048]{1,0:T(8,128)} %param.19), kind=kLoop, calls=%fused_computation.8 | loop fusion | flops 50331648 | bytes 67633152 | tf_op jit(solution)/shard_map/convert_element_type | solution.py:12
  49.8 0.0 copy-start.3
  49.9 23.3 %fusion.1 = bf16[8192,2048]{1,0:T(8,128)(2,1)} fusion(bf16[8192,2048]{1,0:T(8,128)(2,1)} %param.20, f32[64,2048]{1,0:T(8,128)S(1)} %copy-done.2), kind=kLoop, calls=%fused_computation.6 | loop fusion | flops 50331648 | bytes 67633152 | tf_op jit(solution)/shard_map/convert_element_type | solution.py:12
  73.1 0.0 copy-start.6
  73.1 23.4 %fusion = bf16[2048,8192]{1,0:T(8,128)(2,1)} fusion(bf16[2048,8192]{1,0:T(8,128)(2,1)} %param.22, f32[16,8192]{1,0:T(8,128)S(1)} %copy-done.3), kind=kLoop, calls=%fused_computation.4 | loop fusion | flops 50331648 | bytes 67633152 | tf_op jit(solution)/shard_map/convert_element_type | solution.py:12
  96.5 15.8 %fusion.5 = f32[128,2048]{0,1:T(8,128)S(1)} fusion(bf16[8192,2048]{1,0:T(8,128)(2,1)} %fusion.2, bf16[128,8192]{1,0:T(8,128)(2,1)} %all-gather.3.cloned.1.call-done, f32[128]{0:T(128)S(1)} %copy-done.6), kind=kOutput, calls=%fused_computation.14 | convolution fusion | flops 4295229440 | bytes 36700672 | tf_op jit(solution)/shard_map/dot_general | solution.py:64
  112.4 0.0 copy-start.4
  112.4 0.0 copy-start.8
  112.4 0.0 copy-start.7
  112.4 0.0 copy-start.1
  112.4 15.7 %fusion.6 = bf16[128,2048]{0,1:T(8,128)(2,1)S(1)} fusion(bf16[8192,2048]{1,0:T(8,128)(2,1)} %fusion.1, bf16[128,8192]{1,0:T(8,128)(2,1)S(1)} %copy-done.5, f32[128,2048]{0,1:T(8,128)S(1)} %fusion.5, f32[128]{0:T(128)S(1)} %copy-done.6), kind=kOutput, calls=%fused_computation.15 | convolution fusion | flops 4296802304 | bytes 37224960 | tf_op jit(solution)/shard_map/dot_general | solution.py:67
  128.1 16.7 %convolution_convert_fusion = bf16[128,8192]{1,0:T(8,128)(2,1)} fusion(bf16[128,2048]{0,1:T(8,128)(2,1)S(1)} %fusion.6, bf16[2048,8192]{1,0:T(8,128)(2,1)} %fusion), kind=kOutput, calls=%fused_computation.9 | convolution fusion | flops 4296015872 | bytes 36175872 | tf_op jit(solution)/shard_map/dot_general | solution.py:94
  144.8 0.0 reduce-scatter.3.cloned.1.call-update
  144.9 0.0 all-gather.5.cloned.1.call-start
  144.9 0.7 all-gather.5.cloned.1.call-update
  145.6 0.0 reduce-scatter.5.cloned.1.call-start
  145.7 0.1 slice.3
  145.7 0.1 compare_select_fusion.2
  145.8 0.1 reshape.162
  145.9 0.6 dynamic-slice.4
  147.2 0.2 dynamic-update-slice.1
  147.4 4.9 %all-reduce = s32[128]{0:T(128)S(1)} all-reduce(s32[128]{0:T(128)S(1)} %dynamic-update-slice.1), channel_id=1, replica_groups=mesh['parts'=2,'replica'=4,'tensor'=4] {'replica'}, use_global_device_ids=true, to_apply=%add | all-reduce | flops 128 | bytes 1024
  152.3 0.7 gather_fusion
  153.0 0.1 reshape.161
  153.1 0.1 compare_select_fusion.1
  153.1 0.1 reshape.170
  153.2 0.0 copy-done.1
  153.2 0.7 gather_fusion.1
  153.9 0.1 reshape.169
  154.0 0.1 copy.20
  154.1 0.1 convert_reduce_fusion
  154.2 0.1 reduce_sum.24
  154.3 0.1 reshape.176
  154.4 1.5 gather_fusion.2
  155.9 0.1 reshape.179
  156.0 20.2 %reduce-scatter.3.cloned.1.call-done = bf16[32,8192]{1,0:T(8,128)(2,1)} async-done(((bf16[128,8192]{1,0:T(8,128)(2,1)}), bf16[32,8192]{1,0:T(8,128)(2,1)}) %reduce-scatter.3.cloned.1.call-update) | async-done | bytes 524304 | tf_op jit(solution)/shard_map/reduce_scatter | solution.py:93
  176.2 0.0 reduce-scatter.5.cloned.1.call-update
  176.3 0.9 fusion.18
  177.2 0.1 copy.22
  177.3 61.4 %psum.7 = bf16[128,64]{1,0:T(8,128)(2,1)S(1)} all-reduce(f32[128,64]{1,0:T(8,128)S(1)} %copy.22), channel_id=1, replica_groups=mesh['parts'=2,'replica'=4,'tensor'=4] {'replica','tensor'}, use_global_device_ids=true, to_apply=%region_4.5 | all-reduce | flops 8192 | bytes 49152 | tf_op jit(solution)/shard_map/psum | solution.py:80
  238.7 0.0 all-gather.5.cloned.1.call-done
  238.7 0.0 reduce-scatter.5.cloned.1.call-done
  238.8 2.8 %fusion.8 = bf16[32,2048]{1,0:T(8,128)(2,1)} fusion(bf16[8,64,2048]{2,1,0:T(8,128)(2,1)} %all-gather.5.cloned.1.call-done, bf16[32,2048]{1,0:T(8,128)(2,1)} %reduce-scatter.5.cloned.1.call-done, f32[32,64]{1,0:T(8,128)S(1)} %fusion.11, f32[32,8]{0,1:T(8,128)S(1)} %fusion.12), kind=kOutput, calls=%fused_computation.18 | convolution fusion | flops 67338240 | bytes 2368512 | tf_op jit(solution)/shard_map/dot_general | solution.py:88
  (24 shorter events, 0.1 us)
Async XLA Ops:
  6.5 169.7 %copy-start = (bf16[2048,512]{1,0:T(8,128)(2,1)S(1)}, bf16[2048,512]{1,0:T(8,128)(2,1)}, u32[]{:S(2)}) copy-start(bf16[2048,512]{1,0:T(8,128)(2,1)} %param.24) | copy-start | bytes 6291460
  6.5 90.0 %all-gather.3.cloned.1.call-start = ((), (), s32[]{:S(2)}) async-start(), calls=%async_computation.2 | async-start | bytes 2621440 | tf_op jit(solution)/shard_map/all_gather | solution.py:60
  26.0 23.8 %copy-start.2 = (f32[64,2048]{1,0:T(8,128)S(1)}, f32[64,2048]{1,0:T(8,128)}, u32[]{:S(2)}) copy-start(f32[64,2048]{1,0:T(8,128)} %param.21) | copy-start | bytes 1572868
  26.0 150.1 %reduce-scatter.3.cloned.1.call-start = ((), (), s32[]{:S(2)}) async-start(), calls=%async_computation.3 | async-start | bytes 2621440 | tf_op jit(solution)/shard_map/reduce_scatter | solution.py:93
  49.8 23.3 %copy-start.3 = (f32[16,8192]{1,0:T(8,128)S(1)}, f32[16,8192]{1,0:T(8,128)}, u32[]{:S(2)}) copy-start(f32[16,8192]{1,0:T(8,128)} %param.23) | copy-start | bytes 1572868
  73.1 23.4 %copy-start.6 = (f32[128]{0:T(128)S(1)}, f32[128]{0:T(128)}, u32[]{:S(2)}) copy-start(f32[128]{0:T(128)} %param.14) | copy-start | bytes 1540
  96.5 15.8 %copy-start.5 = (bf16[128,8192]{1,0:T(8,128)(2,1)S(1)}, bf16[128,8192]{1,0:T(8,128)(2,1)}, u32[]{:S(2)}) copy-start(bf16[128,8192]{1,0:T(8,128)(2,1)} %all-gather.3.cloned.1.call-done) | copy-start | bytes 6291460
  112.4 33.3 %copy-start.4 = (s32[4,4]{1,0:T(4,128)S(1)}, s32[4,4]{1,0:T(4,128)}, u32[]{:S(2)}) copy-start(s32[4,4]{1,0:T(4,128)} %param.16) | copy-start | bytes 196
  112.4 33.5 %copy-start.8 = (u32[32]{0:T(128)S(1)}, u32[32]{0:T(128)}, u32[]{:S(2)}) copy-start(u32[32]{0:T(128)} %constant.112) | copy-start | bytes 388
  112.4 34.8 %copy-start.7 = (s32[32]{0:T(128)S(1)}, s32[32]{0:T(128)}, u32[]{:S(2)}) copy-start(s32[32]{0:T(128)} %param.15) | copy-start | bytes 388
  112.4 40.8 %copy-start.1 = (s32[8]{0:T(128)S(1)}, s32[8]{0:T(128)}, u32[]{:S(2)}) copy-start(s32[8]{0:T(128)} %param.17) | copy-start | bytes 100
  144.9 93.9 %all-gather.5.cloned.1.call-start = ((), (), s32[]{:S(2)}) async-start(), calls=%async_computation.5 | async-start | bytes 2621440 | tf_op jit(solution)/shard_map/all_gather | solution.py:83
  145.6 93.2 %reduce-scatter.5.cloned.1.call-start = ((), (), s32[]{:S(2)}) async-start(), calls=%async_computation.4 | async-start | bytes 655360 | tf_op jit(solution)/shard_map/reduce_scatter | solution.py:99
Sparse Core Ops, SparseCore 0:
  26.2 22.3 all-gather.2
  145.0 31.1 reduce-scatter.2
  177.8 22.7 all-gather.4
  202.9 21.5 reduce-scatter.4
where the time goes:
time: 248 us
  blocking collectives  85.8 us (35%)
  other arithmetic  70.7 us (29%)
  matrix products  52 us (21%)
  waiting for transfers between devices  21 us (8%)
  between operations  14 us (6%)
  local copies, waits for them, and re-layouts  4.57 us (2%)
    convert_element_type x3, other arithmetic, dequantize(): return scaled.reshape(rows, values.shape[1]).astype(jnp.bfloat16)  70.4 us
    psum x1, blocking collectives, local(): total = lax.psum(partial_value, ('replica', 'tensor'))  61.4 us
    reduce_scatter x1, waiting for transfers between devices, local(): lax.psum_scatter(jnp.dot(hidden, w_down, preferred_element_type=jnp.float...  20.2 us
    all_gather x1, blocking collectives, local(): feature_codes = lax.all_gather(act_codes, 'tensor', axis=1, tiled=True)  19.5 us
    dot_general x1, matrix products, local(): jnp.dot(hidden, w_down, preferred_element_type=jnp.float32)  16.7 us
    dot_general x1, matrix products, local(): jnp.dot(inputs, dequantize(gate_levels, gate_scale), preferred_element_ty...  15.8 us
    dot_general x1, matrix products, local(): jnp.dot(inputs, dequantize(up_levels, up_scale), preferred_element_type=j...  15.7 us
  transfers between devices with their start and end apart: 4, of which 1 were waited for; matrix products, arithmetic and copies ran while one was open for 31% of the time, Pallas kernels for 0%

commit v1 on v0

v1 whole, which is shorter than its diff:
```python
import functools
import jax
import jax.numpy as jnp
from jax import lax
from jax.experimental import pallas as pl
from jax.experimental.pallas import tpu as pltpu
from jax.sharding import PartitionSpec as P

GROUP = 128
LANES = 128
MIB = 1024 * 1024


def vmem():
    return pl.BlockSpec(memory_space=pltpu.VMEM)


def smem():
    return pl.BlockSpec(memory_space=pltpu.SMEM)


def hbm():
    return pl.BlockSpec(memory_space=pltpu.HBM)


def scaled(levels, scales, first_group, groups):
    parts = []
    for g in range(groups):
        row = scales[pl.ds(first_group + g, 1), :].astype(jnp.bfloat16)
        parts.append(levels[g * GROUP : (g + 1) * GROUP, :] * row)
    return jnp.concatenate(parts, axis=0) if groups > 1 else parts[0]


def gate_up_kernel(pieces, blocks, first, last, kb, slots, offsets, *refs):
    rows_in = refs[: pieces * blocks]
    refs = refs[pieces * blocks :]
    gl, gs, ul, us = refs[:4]
    refs = refs[4:]
    if not first:
        gate_in, up_in = refs[:2]
        refs = refs[2:]
    if last:
        act_scale, hidden = refs[:2]
        refs = refs[2:]
        gate, up = refs[:2]
        refs = refs[2:]
    else:
        gate, up = refs[:2]
        refs = refs[2:]
    xs, gbuf, ubuf, sems = refs
    rows = rows_in[0].shape[0]
    depth = rows_in[0].shape[1]
    per_block = depth // kb
    steps = blocks * per_block

    def copies(step, slot):
        k = pl.multiple_of(offsets[step // per_block] + (step % per_block) * kb, kb)
        return (
            pltpu.make_async_copy(gl.at[pl.ds(k, kb), :], gbuf.at[slot], sems.at[0, slot]),
            pltpu.make_async_copy(ul.at[pl.ds(k, kb), :], ubuf.at[slot], sems.at[1, slot]),
        )

    for s in range(min(slots, steps)):
        for c in copies(s, s):
            c.start()
    for b in range(blocks):
        for p in range(pieces):
            for k in range(per_block):
                xs[b * per_block + k, p * rows : (p + 1) * rows, :] = rows_in[b * pieces + p][
                    :, k * kb : (k + 1) * kb
                ]
    if first:
        gate[...] = jnp.zeros_like(gate)
        up[...] = jnp.zeros_like(up)
    else:
        gate[...] = gate_in[...]
        up[...] = up_in[...]

    def body(step, carry):
        slot = lax.rem(step, slots)
        group = (offsets[step // per_block] + (step % per_block) * kb) // GROUP
        cg, cu = copies(step, slot)
        x = xs[step]
        cg.wait()
        gate[...] += jnp.dot(
            x, scaled(gbuf.at[slot], gs, group, kb // GROUP), preferred_element_type=jnp.float32
        )
        cu.wait()
        up[...] += jnp.dot(
            x, scaled(ubuf.at[slot], us, group, kb // GROUP), preferred_element_type=jnp.float32
        )

        @pl.when(step + slots < steps)
        def _():
            for c in copies(step + slots, slot):
                c.start()

        return carry

    lax.fori_loop(0, steps, body, 0)
    if last:
        g = gate[...] * act_scale[...]
        u = up[...] * act_scale[...]
        hidden[...] = (g / (1.0 + jnp.exp(-g)) * u).astype(jnp.bfloat16)


def gate_up(offsets, blocks_in, gl, gs, ul, us, acc, act_scale):
    first, last = acc is None, act_scale is not None
    blocks, pieces = len(blocks_in), len(blocks_in[0])
    rows, depth = blocks_in[0][0].shape
    width = gl.shape[1]
    kb = min(256, depth)
    slots = 6
    ins = [offsets] + [p for b in blocks_in for p in b] + [gl, gs, ul, us]
    specs = [smem()] + [vmem()] * (blocks * pieces) + [hbm(), vmem(), hbm(), vmem()]
    if not first:
        ins += list(acc)
        specs += [vmem(), vmem()]
    total = jax.ShapeDtypeStruct((rows * pieces, width), jnp.float32)
    scratch = []
    if last:
        ins.append(act_scale)
        specs.append(vmem())
        out_shape = [jax.ShapeDtypeStruct((rows * pieces, width), jnp.bfloat16)]
        scratch += [pltpu.VMEM(total.shape, jnp.float32)] * 2
    else:
        out_shape = [total, total]
    steps = blocks * depth // kb
    scratch += [
        pltpu.VMEM((steps, rows * pieces, kb), jnp.bfloat16),
        pltpu.VMEM((slots, kb, width), jnp.bfloat16),
        pltpu.VMEM((slots, kb, width), jnp.bfloat16),
        pltpu.SemaphoreType.DMA((2, slots)),
    ]
    return pl.pallas_call(
        functools.partial(gate_up_kernel, pieces, blocks, first, last, kb, slots),
        out_shape=out_shape,
        in_specs=specs,
        out_specs=[vmem()] * len(out_shape),
        scratch_shapes=scratch,
        compiler_params=pltpu.CompilerParams(vmem_limit_bytes=40 * MIB),
        cost_estimate=pl.CostEstimate(
            flops=4 * rows * pieces * blocks * depth * width,
            bytes_accessed=4 * blocks * depth * width,
            transcendentals=0,
        ),
        name="gate_up",
    )(*ins)


def down_kernel(kb, slots, shrink_too, offset, hidden, dl, ds, *refs):
    if shrink_too:
        shrink = refs[0]
        refs = refs[1:]
    mine, theirs, acc, scales, hs, buf, sems, scale_sem = refs
    depth, width = hidden.shape[1], acc.shape[1]
    half = mine.shape[0]
    steps = depth // kb
    col = pl.multiple_of(offset[0], width)

    def copy(step, slot):
        return pltpu.make_async_copy(
            dl.at[pl.ds(pl.multiple_of(step * kb, kb), kb), pl.ds(col, width)],
            buf.at[slot],
            sems.at[slot],
        )

    scale_copy = pltpu.make_async_copy(ds.at[:, pl.ds(col, width)], scales, scale_sem)
    scale_copy.start()
    for s in range(min(slots, steps)):
        copy(s, s).start()
    for s in range(steps):
        hs[s, :, :] = hidden[:, s * kb : (s + 1) * kb]
    acc[...] = jnp.zeros_like(acc)
    if shrink_too:
        project = jnp.dot(hidden[...], shrink[...], preferred_element_type=jnp.float32)
        project = project.astype(jnp.bfloat16)
        mine[:, width:] = project[:half]
        theirs[:, width:] = project[half:]
    scale_copy.wait()

    def body(step, carry):
        slot = lax.rem(step, slots)
        copy(step, slot).wait()
        acc[...] += jnp.dot(
            hs[step],
            scaled(buf.at[slot], scales, step * (kb // GROUP), kb // GROUP),
            preferred_element_type=jnp.float32,
        )

        @pl.when(step + slots < steps)
        def _():
            copy(step + slots, slot).start()

        return carry

    lax.fori_loop(0, steps, body, 0)
    mine[:, :width] = acc[:half, :].astype(jnp.bfloat16)
    theirs[:, :width] = acc[half:, :].astype(jnp.bfloat16)


def down(offset, hidden, dl, ds, width, shrink):
    rows, depth = hidden.shape
    kb = min(256, depth)
    slots = min(8, depth // kb)
    wide = width + (0 if shrink is None else shrink.shape[1])
    ins = [offset, hidden, dl, ds]
    specs = [smem(), vmem(), hbm(), hbm()]
    if shrink is not None:
        ins.append(shrink)
        specs.append(vmem())
    half = jax.ShapeDtypeStruct((rows // 2, wide), jnp.bfloat16)
    return pl.pallas_call(
        functools.partial(down_kernel, kb, slots, shrink is not None),
        out_shape=[half, half],
        in_specs=specs,
        out_specs=[vmem(), vmem()],
        scratch_shapes=[
            pltpu.VMEM((rows, width), jnp.float32),
            pltpu.VMEM((depth // GROUP, width), jnp.float32),
            pltpu.VMEM((depth // kb, rows, kb), jnp.bfloat16),
            pltpu.VMEM((slots, kb, width), jnp.bfloat16),
            pltpu.SemaphoreType.DMA((slots,)),
            pltpu.SemaphoreType.DMA,
        ],
        compiler_params=pltpu.CompilerParams(vmem_limit_bytes=24 * MIB),
        cost_estimate=pl.CostEstimate(
            flops=2 * rows * depth * width, bytes_accessed=2 * depth * width, transcendentals=0
        ),
        name="down",
    )(*ins)


def fold_matrix(pool_width, rank, lanes, transposed):
    shape = (lanes, pool_width) if transposed else (pool_width, lanes)
    wide = lax.broadcasted_iota(jnp.int32, shape, 1 if transposed else 0)
    slim = lax.broadcasted_iota(jnp.int32, shape, 0 if transposed else 1)
    return (lax.rem(wide, rank) == slim).astype(jnp.float32).astype(jnp.bfloat16)


def pool_mask(pool_row, rows, pool_width, rank):
    column = lax.broadcasted_iota(jnp.int32, (rows, pool_width), 1)
    start = pool_row[...] * rank
    return (column >= start) & (column < start + rank)


def message_kernel(count, width, rank, pool_row, *refs):
    parts, (out, low) = refs[:count], refs[count:]
    total = parts[0][...].astype(jnp.float32)
    for p in parts[1:]:
        total = total + p[...].astype(jnp.float32)
    rows, wide = total.shape
    mask = pool_mask(pool_row, rows, wide - width, rank)
    chosen = jnp.where(mask, total[:, width:], 0.0).astype(jnp.bfloat16)
    part = jnp.dot(
        chosen,
        fold_matrix(wide - width, rank, low.shape[1], False),
        preferred_element_type=jnp.float32,
    ).astype(jnp.bfloat16)
    low[...] = part
    out[:, :width] = total[:, :width].astype(jnp.bfloat16)
    out[:, width:] = part


def message(parts, pool_row, width, rank):
    rows = parts[0].shape[0]
    lanes = max(LANES, rank)
    return pl.pallas_call(
        functools.partial(message_kernel, len(parts), width, rank),
        out_shape=[
            jax.ShapeDtypeStruct((rows, width + lanes), jnp.bfloat16),
            jax.ShapeDtypeStruct((rows, lanes), jnp.bfloat16),
        ],
        in_specs=[vmem()] * (1 + len(parts)),
        out_specs=[vmem()] * 2,
        name="message",
    )(pool_row, *parts)


def final_kernel(count, wides, rank, pool_row, low, pool, *refs):
    parts, wide, out = refs[:count], refs[count : count + wides], refs[count + wides]
    rows, width = out.shape
    total_low = low[...].astype(jnp.float32)
    for w in wide:
        total_low = total_low + w[:, width:].astype(jnp.float32)
    total_low = total_low.astype(jnp.bfloat16)
    pool_width = pool.shape[0]
    spread = jnp.dot(
        total_low,
        fold_matrix(pool_width, rank, total_low.shape[1], True),
        preferred_element_type=jnp.float32,
    )
    mask = pool_mask(pool_row, rows, pool_width, rank)
    spread = jnp.where(mask, spread, 0.0).astype(jnp.bfloat16)
    total = jnp.dot(spread, pool[...], preferred_element_type=jnp.float32)
    for p in parts:
        total = total + p[...].astype(jnp.float32)
    for w in wide:
        total = total + w[:, :width].astype(jnp.float32)
    out[...] = total.astype(jnp.bfloat16)


def final(parts, wide, pool_row, low, pool, rank):
    rows, width = parts[0].shape
    return pl.pallas_call(
        functools.partial(final_kernel, len(parts), len(wide), rank),
        out_shape=jax.ShapeDtypeStruct((rows, width), jnp.bfloat16),
        in_specs=[vmem()] * (3 + len(parts) + len(wide)),
        out_specs=vmem(),
        compiler_params=pltpu.CompilerParams(vmem_limit_bytes=16 * MIB),
        name="final",
    )(pool_row, low, pool, *parts, *wide)


def add_bf16(a, b):
    return (a.astype(jnp.float32) + b.astype(jnp.float32)).astype(jnp.bfloat16)


def nearest_first(count):
    return sorted(range(1, count), key=lambda d: (d.bit_length(), -d))


def local(replicas, tensors, *args):
    (
        act_codes,
        act_scale,
        adapter_ids,
        seg_starts,
        pool_index,
        gate_levels,
        gate_scale,
        up_levels,
        up_scale,
        down_levels,
        down_scale,
        shrink_weight,
        expand_rows,
    ) = args
    replica = lax.axis_index("replica")
    tensor = lax.axis_index("tensor")
    cores = 2
    chips = replicas // cores
    rows, depth = act_codes.shape
    rank, width = expand_rows.shape[1], expand_rows.shape[2]

    def core_swap(v):
        return lax.ppermute(v, "replica", [(r, r ^ 1) for r in range(replicas)])

    def chip_swap(v, s):
        return lax.ppermute(v, "replica", [(r, r ^ (s * cores)) for r in range(replicas)])

    def tensor_swap(v, d):
        return lax.ppermute(v, "tensor", [(t, t ^ d) for t in range(tensors)])

    order = [s * cores for s in range(chips)] + [s * cores + 1 for s in range(chips)]

    def spread_block(v):
        same = [v] + [chip_swap(v, s) for s in range(1, chips)]
        return same + [core_swap(p) for p in same]

    distances = [0] + nearest_first(tensors)
    offsets = jnp.stack([(tensor ^ d) for d in distances]).astype(jnp.int32)
    row_scale = jnp.concatenate(
        [
            lax.dynamic_slice_in_dim(act_scale, (replica ^ o) * rows, rows, 0)
            for o in order
        ]
    )[:, None]
    own_choice = adapter_ids[:, None] == jnp.arange(pool_index.shape[0], dtype=jnp.int32)[None, :]
    pool_row = jnp.sum(jnp.where(own_choice, pool_index[None, :], 0), axis=1, keepdims=True)
    whole_pool = lax.all_gather(expand_rows, "replica", axis=0, tiled=True)
    whole_pool = whole_pool.reshape(-1, width)

    arrived = {0: spread_block(act_codes)}
    moved = {d: tensor_swap(act_codes, d) for d in distances[1:]}
    for d in distances[1:]:
        arrived[d] = spread_block(moved[d])
    groups = [distances[:1]]
    rest = distances[1:]
    if len(rest) <= 3:
        groups += [[d] for d in rest]
    else:
        groups += [rest[: len(rest) // 2], rest[len(rest) // 2 :]]
    acc = None
    at = 0
    for i, g in enumerate(groups):
        acc = gate_up(
            offsets[at : at + len(g)] * depth,
            [arrived[d] for d in g],
            gate_levels,
            gate_scale,
            up_levels,
            up_scale,
            acc,
            row_scale if i == len(groups) - 1 else None,
        )
        at += len(g)
    hidden = acc[0]

    low = None
    received = []
    for d in distances[1:][::-1] + [0]:
        i = distances.index(d)
        first = low is None
        mine, theirs = down(
            offsets[i : i + 1] * width,
            hidden,
            down_levels,
            down_scale,
            width,
            shrink_weight if first else None,
        )
        pair = add_bf16(mine, core_swap(theirs))
        parts = [pair[:rows]] + [
            chip_swap(pair[s * rows : (s + 1) * rows], s) for s in range(1, chips)
        ]
        if first:
            out, low = message(parts, pool_row, width, rank)
            received.append(tensor_swap(out, d))
        elif d:
            total = parts[0].astype(jnp.float32)
            for p in parts[1:]:
                total = total + p.astype(jnp.float32)
            out = jnp.concatenate([total.astype(jnp.bfloat16), low], axis=1)
            received.append(tensor_swap(out, d))
        else:
            own = parts
    return final(own, received, pool_row, low, whole_pool, rank)


def solution(mesh):
    placed = (
        P(("parts", "replica"), "tensor"),
        P("parts"),
        P(("parts", "replica")),
        P("parts", None),
        P("parts"),
        P(None, ("replica", "tensor")),
        P(None, ("replica", "tensor")),
        P(None, ("replica", "tensor")),
        P(None, ("replica", "tensor")),
        P(("replica", "tensor"), None),
        P(("replica", "tensor"), None),
        P(("replica", "tensor"), None),
        P("replica", None, "tensor"),
    )
    return jax.shard_map(
        functools.partial(local, mesh.shape["replica"], mesh.shape["tensor"]),
        mesh=mesh,
        in_specs=placed,
        out_specs=P(("parts", "replica"), "tensor"),
        check_vma=False,
    )
```

time: 248 us -> 117 us (0.47)
  blocking collectives: 85.8 us -> 0 us
  other arithmetic: 70.7 us -> 1.89 us
  matrix products: 52 us -> 0 us
  Pallas kernels: 0 us -> 46.7 us
  starting transfers between devices: 0.12 us -> 21 us
  waiting for transfers between devices: 21 us -> 25.3 us
  local copies, waits for them, and re-layouts: 4.57 us -> 8.4 us
    convert_element_type x6, other arithmetic: 70.4 us -> 0.34 us  [the longest x4 0.27 us: add_bf16(): return (a.astype(jnp.float32) + b.astype(jnp.float32)).astype(jnp.bfloat16)]
    psum x1 -> x0, blocking collectives: 61.4 us -> none  [local(): total = lax.psum(partial_value, ('replica', 'tensor'))]
    dot_general x5 -> x0, matrix products: 52 us -> none  [the longest x1 16.7 us: local(): jnp.dot(hidden, w_down, preferred_element_type=jnp.float32)]
    pallas_call x0 -> x10, Pallas kernels: none -> 46.7 us  [the longest x4 27 us: gate_up(): pl.pallas_call(functools.partial(gate_up_kernel, pieces, blocks, first, l...]
    ppermute x0 -> x26, waiting for transfers between devices: none -> 25.3 us  [the longest x6 14.4 us: tensor_swap(): return lax.ppermute(v, 'tensor', [(t, t ^ d) for t in range(tensors)])]
    ppermute x0 -> x26, starting transfers between devices: none -> 21 us  [the longest x8 9.73 us: chip_swap(): lax.ppermute(v, 'replica', [(r, r ^ s * cores) for r in range(replicas)])]
    reduce_scatter x2 -> x0, waiting for transfers between devices: 20.2 us -> none  [the longest x1 20.2 us: local(): lax.psum_scatter(jnp.dot(hidden, w_down, preferred_element_type=jnp.float...]
    all_gather x1 -> x0, blocking collectives: 19.5 us -> none  [local(): feature_codes = lax.all_gather(act_codes, 'tensor', axis=1, tiled=True)]
  transfers between devices with their start and end apart: 4 -> 27, of which waited for: 1 -> 8; matrix products, arithmetic and copies ran while one was open for 31% -> 4% of each run, Pallas kernels for 0% -> 39%
where the time goes in v1:
time: 117 us
  Pallas kernels  46.7 us (40%)
  waiting for transfers between devices  25.3 us (22%)
  starting transfers between devices  21 us (18%)
  between operations  13.7 us (12%)
  local copies, waits for them, and re-layouts  8.4 us (7%)
  other arithmetic  1.89 us (2%)
    pallas_call x4, Pallas kernels, gate_up(): pl.pallas_call(functools.partial(gate_up_kernel, pieces, blocks, first, l...  27 us
    pallas_call x4, Pallas kernels, down(): pl.pallas_call(functools.partial(down_kernel, kb, slots, shrink is not No...  16.6 us
    ppermute x6, waiting for transfers between devices, tensor_swap(): return lax.ppermute(v, 'tensor', [(t, t ^ d) for t in range(tensors)])  14.4 us
    ppermute x8, waiting for transfers between devices, chip_swap(): lax.ppermute(v, 'replica', [(r, r ^ s * cores) for r in range(replicas)])  10.8 us
    ppermute x8, starting transfers between devices, chip_swap(): lax.ppermute(v, 'replica', [(r, r ^ s * cores) for r in range(replicas)])  9.73 us
    ppermute x6, starting transfers between devices, tensor_swap(): return lax.ppermute(v, 'tensor', [(t, t ^ d) for t in range(tensors)])  8.62 us
    unnamed x22, local copies, waits for them, and re-layouts  5.97 us
    ppermute x12, starting transfers between devices, core_swap(): return lax.ppermute(v, 'replica', [(r, r ^ 1) for r in range(replicas)])  2.64 us
  transfers between devices with their start and end apart: 27, of which 8 were waited for; matrix products, arithmetic and copies ran while one was open for 4% of the time, Pallas kernels for 39%

profile of v1, /device:TPU:0, one launch (start us, length us, event | category | flops | bytes accessed | tf_op | source)
XLA Modules:
  0.0 116.9 jit_solution(2856912206471533225)
XLA Ops:
  6.5 2.9 %collective-permute-start.12 = (bf16[32,2048]{1,0:T(8,128)(2,1)}, bf16[32,2048]{1,0:T(8,128)(2,1)S(1)}, u32[]{:S(2)}, u32[]{:S(2)}) collective-permute-start(bf16[32,2048]{1,0:T(8,128)(2,1)} %refs_0_.2), channel_id=1, source_target_pairs={{0,8},{4,12},{8,0},{12,4},{1,9},{5,13},{9,1},{13,5},{2,10},{6,14},... | collective-permute-start | bytes 393224 | tf_op jit(solution)/shard_map/ppermute | solution.py:350
  9.5 1.6 %collective-permute-start.8 = (bf16[32,2048]{1,0:T(8,128)(2,1)}, bf16[32,2048]{1,0:T(8,128)(2,1)S(1)}, u32[]{:S(2)}, u32[]{:S(2)}) collective-permute-start(bf16[32,2048]{1,0:T(8,128)(2,1)} %refs_0_.2), channel_id=1, source_target_pairs={{0,1},{1,0},{2,3},{3,2},{4,5},{5,4},{6,7},{7,6},{8,9},{9,8},{10,11... | collective-permute-start | bytes 393224 | tf_op jit(solution)/shard_map/ppermute | solution.py:353
  11.1 2.5 %collective-permute-start.4 = (bf16[32,2048]{1,0:T(8,128)(2,1)}, bf16[32,2048]{1,0:T(8,128)(2,1)S(1)}, u32[]{:S(2)}, u32[]{:S(2)}) collective-permute-start(bf16[32,2048]{1,0:T(8,128)(2,1)} %refs_0_.2), channel_id=1, source_target_pairs={{0,3},{1,2},{2,1},{3,0},{4,7},{5,6},{6,5},{7,4},{8,11},{9,10},{10,... | collective-permute-start | bytes 393224 | tf_op jit(solution)/shard_map/ppermute | solution.py:353
  13.7 0.9 fusion.2
  14.6 0.2 collective-permute-start.14
  14.8 0.5 collective-permute-start.9
  15.6 0.8 select_reduce_fusion
  16.3 0.7 copy.21.pool_row
  17.0 3.0 %collective-permute-done.4.refs_0_ = bf16[32,2048]{1,0:T(8,128)(2,1)S(1)} collective-permute-done((bf16[32,2048]{1,0:T(8,128)(2,1)}, bf16[32,2048]{1,0:T(8,128)(2,1)S(1)}, u32[]{:S(2)}, u32[]{:S(2)}) %collective-permute-start.4) | collective-permute-done | bytes 131104 | tf_op jit(solution)/shard_map/ppermute | solution.py:353
  20.1 0.5 collective-permute-start.5
  20.6 5.8 %collective-permute-done.refs_0_ = bf16[32,2048]{1,0:T(8,128)(2,1)S(1)} collective-permute-done((bf16[32,2048]{1,0:T(8,128)(2,1)}, bf16[32,2048]{1,0:T(8,128)(2,1)S(1)}, u32[]{:S(2)}, u32[]{:S(2)}) %collective-permute-start) | collective-permute-done | bytes 131104 | tf_op jit(solution)/shard_map/ppermute | solution.py:353
  26.5 0.5 collective-permute-start.1
  27.2 1.0 copy-done
  28.3 1.0 copy-done.2
  29.3 0.9 copy-done.8
  30.2 6.7 %gate_up.4 = (f32[128,2048]{1,0:T(8,128)S(1)}, f32[128,2048]{1,0:T(8,128)S(1)}) custom-call(s32[1]{0:T(128)} %bitcast.4.offsets.offset, bf16[32,2048]{1,0:T(8,128)(2,1)S(1)} %copy-done.8, bf16[32,2048]{1,0:T(8,128)(2,1)S(1)} %collective-permute-done.12.refs_1_, bf16[32,2048]{1,0:T(8,128)(2,1)S(1)} %collective-permute-done.13.refs_2_, ...), custom_call_target="tpu_custom_call" | custom-call | flops 2147483648 | bytes 16777216 | tf_op jit(solution)/shard_map/gate_up/pallas_call | solution.py:135
  36.9 0.4 collective-permute-start.2
  37.5 0.3 collective-permute-start.3
  37.8 6.6 %gate_up.5 = (f32[128,2048]{1,0:T(8,128)S(1)}, f32[128,2048]{1,0:T(8,128)S(1)}) custom-call(s32[1]{0:T(128)} %bitcast.3.offsets.offset, bf16[32,2048]{1,0:T(8,128)(2,1)S(1)} %collective-permute-done.8.refs_0_, bf16[32,2048]{1,0:T(8,128)(2,1)S(1)} %collective-permute-done.9.refs_1_, bf16[32,2048]{1,0:T(8,128)(2,1)S(1)} %collective-permute-done.10.refs_2_, ...), custom_call_target="tpu_custom_call" | custom-call | flops 2147483648 | bytes 16777216 | tf_op jit(solution)/shard_map/gate_up/pallas_call | solution.py:135
  44.4 6.6 %gate_up.6 = (f32[128,2048]{1,0:T(8,128)S(1)}, f32[128,2048]{1,0:T(8,128)S(1)}) custom-call(s32[1]{0:T(128)} %bitcast.2.offsets.offset, bf16[32,2048]{1,0:T(8,128)(2,1)S(1)} %collective-permute-done.4.refs_0_, bf16[32,2048]{1,0:T(8,128)(2,1)S(1)} %collective-permute-done.5.refs_1_, bf16[32,2048]{1,0:T(8,128)(2,1)S(1)} %collective-permute-done.6.refs_2_, ...), custom_call_target="tpu_custom_call" | custom-call | flops 2147483648 | bytes 16777216 | tf_op jit(solution)/shard_map/gate_up/pallas_call | solution.py:135
  51.0 7.2 %gate_up.7.hidden = bf16[128,2048]{1,0:T(8,128)(2,1)S(1)} custom-call(s32[1]{0:T(128)} %bitcast.1.offsets.offset, bf16[32,2048]{1,0:T(8,128)(2,1)S(1)} %collective-permute-done.refs_0_, bf16[32,2048]{1,0:T(8,128)(2,1)S(1)} %collective-permute-done.1.refs_1_, bf16[32,2048]{1,0:T(8,128)(2,1)S(1)} %collective-permute-done.2.refs_2_, ...), custom_call_target="tpu_custom_call" | custom-call | flops 2147483648 | bytes 16777216 | tf_op jit(solution)/shard_map/gate_up/pallas_call | solution.py:135
  58.2 4.2 %down.6 = (bf16[64,2048]{1,0:T(8,128)(2,1)S(1)}, bf16[64,2048]{1,0:T(8,128)(2,1)S(1)}) custom-call(s32[1]{0:T(128)} %bitcast.2.offsets.offset, bf16[128,2048]{1,0:T(8,128)(2,1)S(1)} %gate_up.7.hidden, bf16[2048,8192]{1,0:T(8,128)(2,1)} %dl.7, f32[16,8192]{1,0:T(8,128)S(1)} %copy-done.4), custom_call_target="tpu_custom_call" | custom-call | flops 1073741824 | bytes 8388608 | tf_op jit(solution)/shard_map/down/pallas_call | solution.py:213
  62.7 4.0 %down.7 = (bf16[64,2048]{1,0:T(8,128)(2,1)S(1)}, bf16[64,2048]{1,0:T(8,128)(2,1)S(1)}) custom-call(s32[1]{0:T(128)} %bitcast.3.offsets.offset, bf16[128,2048]{1,0:T(8,128)(2,1)S(1)} %gate_up.7.hidden, bf16[2048,8192]{1,0:T(8,128)(2,1)} %dl.7, f32[16,8192]{1,0:T(8,128)S(1)} %copy-done.4), custom_call_target="tpu_custom_call" | custom-call | flops 1073741824 | bytes 8388608 | tf_op jit(solution)/shard_map/down/pallas_call | solution.py:213
  66.7 0.4 collective-permute-start.23
  67.1 4.4 %down.4 = (bf16[64,2560]{1,0:T(8,128)(2,1)S(1)}, bf16[64,2560]{1,0:T(8,128)(2,1)S(1)}) custom-call(s32[1]{0:T(128)} %bitcast.1.offsets.offset, bf16[128,2048]{1,0:T(8,128)(2,1)S(1)} %gate_up.7.hidden, bf16[2048,8192]{1,0:T(8,128)(2,1)} %dl.7, f32[16,8192]{1,0:T(8,128)S(1)} %copy-done.4, bf16[2048,512]{1,0:T(8,128)(2,1)S(1)} %copy-done.5), custom_call_target="tpu_custom_call" | custom-call | flops 1073741824 | bytes 8388608 | tf_op jit(solution)/shard_map/down/pallas_call | solution.py:213
  71.5 0.3 collective-permute-start.15
  71.7 4.0 %down.5 = (bf16[64,2048]{1,0:T(8,128)(2,1)S(1)}, bf16[64,2048]{1,0:T(8,128)(2,1)S(1)}) custom-call(s32[1]{0:T(128)} %bitcast.4.offsets.offset, bf16[128,2048]{1,0:T(8,128)(2,1)S(1)} %gate_up.7.hidden, bf16[2048,8192]{1,0:T(8,128)(2,1)} %dl.7, f32[16,8192]{1,0:T(8,128)S(1)} %copy-done.4), custom_call_target="tpu_custom_call" | custom-call | flops 1073741824 | bytes 8388608 | tf_op jit(solution)/shard_map/down/pallas_call | solution.py:213
  75.7 0.4 collective-permute-start.17
  76.2 1.5 %collective-permute-start.21 = (bf16[32,2048]{1,0:T(8,128)(2,1)S(1)}, bf16[32,2048]{1,0:T(8,128)(2,1)S(1)}, u32[]{:S(2)}, u32[]{:S(2)}) collective-permute-start(bf16[32,2048]{1,0:T(8,128)(2,1)S(1)} %slice.37), channel_id=1, source_target_pairs={{0,8},{4,12},{8,0},{12,4},{1,9},{5,13},{9,1},{13,5},{2,10},{6,14},... | collective-permute-start | bytes 393224 | tf_op jit(solution)/shard_map/ppermute | solution.py:350
  77.8 0.6 collective-permute-start.24
  78.6 0.7 fusion
  79.3 1.5 %collective-permute-start.16 = (bf16[32,2560]{1,0:T(8,128)(2,1)S(1)}, bf16[32,2560]{1,0:T(8,128)(2,1)S(1)}, u32[]{:S(2)}, u32[]{:S(2)}) collective-permute-start(bf16[32,2560]{1,0:T(8,128)(2,1)S(1)} %get-tuple-element.37), channel_id=1, source_target_pairs={{0,8},{4,12},{8,0},{12,4},{1,9},{5,13},{9,1},{13,5},{2,10},{6,14},... | collective-permute-start | bytes 491528 | tf_op jit(solution)/shard_map/ppermute | solution.py:350
  80.8 1.8 %collective-permute-done.21 = bf16[32,2048]{1,0:T(8,128)(2,1)S(1)} collective-permute-done((bf16[32,2048]{1,0:T(8,128)(2,1)S(1)}, bf16[32,2048]{1,0:T(8,128)(2,1)S(1)}, u32[]{:S(2)}, u32[]{:S(2)}) %collective-permute-start.21) | collective-permute-done | bytes 131104 | tf_op jit(solution)/shard_map/ppermute | solution.py:350
  82.7 2.8 %collective-permute-done.24 = bf16[32,2048]{1,0:T(8,128)(2,1)S(1)} collective-permute-done((bf16[32,2048]{1,0:T(8,128)(2,1)S(1)}, bf16[32,2048]{1,0:T(8,128)(2,1)S(1)}, u32[]{:S(2)}, u32[]{:S(2)}) %collective-permute-start.24) | collective-permute-done | bytes 131104 | tf_op jit(solution)/shard_map/ppermute | solution.py:350
  85.5 2.7 %collective-permute-done.16.refs_1_ = bf16[32,2560]{1,0:T(8,128)(2,1)S(1)} collective-permute-done((bf16[32,2560]{1,0:T(8,128)(2,1)S(1)}, bf16[32,2560]{1,0:T(8,128)(2,1)S(1)}, u32[]{:S(2)}, u32[]{:S(2)}) %collective-permute-start.16) | collective-permute-done | bytes 163872 | tf_op jit(solution)/shard_map/ppermute | solution.py:350
  88.2 0.7 copy-done.10
  88.9 1.9 %message.1 = (bf16[32,2176]{1,0:T(8,128)(2,1)}, bf16[32,128]{1,0:T(8,128)(2,1)}) custom-call(s32[32,1]{1,0:T(8,128)} %copy.21.pool_row, bf16[32,2560]{1,0:T(8,128)(2,1)} %get-tuple-element.38.refs_0_, bf16[32,2560]{1,0:T(8,128)(2,1)} %copy-done.10), custom_call_target="tpu_custom_call" | custom-call | tf_op jit(solution)/shard_map/message/pallas_call | solution.py:268
  90.7 0.7 pad_maximum_fusion
  91.5 2.7 %collective-permute-start.22 = (bf16[32,2176]{1,0:T(8,128)(2,1)S(1)}, bf16[32,2176]{1,0:T(8,128)(2,1)S(1)}, u32[]{:S(2)}, u32[]{:S(2)}) collective-permute-start(bf16[32,2176]{1,0:T(8,128)(2,1)S(1)} %get-tuple-element.42), channel_id=1, source_target_pairs={{0,3},{1,2},{2,1},{3,0},{4,7},{5,6},{6,5},{7,4},{8,11},{9,10},{10,... | collective-permute-start | bytes 417800 | tf_op jit(solution)/shard_map/ppermute | solution.py:353
  94.2 0.4 collective-permute-start.25
  94.6 1.3 %collective-permute-start.19 = (bf16[32,2176]{1,0:T(8,128)(2,1)}, bf16[32,2176]{1,0:T(8,128)(2,1)S(1)}, u32[]{:S(2)}, u32[]{:S(2)}) collective-permute-start(bf16[32,2176]{1,0:T(8,128)(2,1)} %get-tuple-element.32), channel_id=1, source_target_pairs={{0,2},{1,3},{2,0},{3,1},{4,6},{5,7},{6,4},{7,5},{8,10},{9,11},{10,... | collective-permute-start | bytes 417800 | tf_op jit(solution)/shard_map/ppermute | solution.py:353
  95.9 1.6 %collective-permute-start.18 = (bf16[32,2048]{1,0:T(8,128)(2,1)S(1)}, bf16[32,2048]{1,0:T(8,128)(2,1)S(1)}, u32[]{:S(2)}, u32[]{:S(2)}) collective-permute-start(bf16[32,2048]{1,0:T(8,128)(2,1)S(1)} %get-tuple-element.39), channel_id=1, source_target_pairs={{0,8},{4,12},{8,0},{12,4},{1,9},{5,13},{9,1},{13,5},{2,10},{6,14},... | collective-permute-start | bytes 393224 | tf_op jit(solution)/shard_map/ppermute | solution.py:350
  97.5 3.5 %collective-permute-done.18.refs_1_ = bf16[32,2048]{1,0:T(8,128)(2,1)S(1)} collective-permute-done((bf16[32,2048]{1,0:T(8,128)(2,1)S(1)}, bf16[32,2048]{1,0:T(8,128)(2,1)S(1)}, u32[]{:S(2)}, u32[]{:S(2)}) %collective-permute-start.18) | collective-permute-done | bytes 131104 | tf_op jit(solution)/shard_map/ppermute | solution.py:350
  101.0 0.9 collective-permute-done.25.refs_4_
  101.9 4.6 %collective-permute-done.19.refs_2_ = bf16[32,2176]{1,0:T(8,128)(2,1)S(1)} collective-permute-done((bf16[32,2176]{1,0:T(8,128)(2,1)}, bf16[32,2176]{1,0:T(8,128)(2,1)S(1)}, u32[]{:S(2)}, u32[]{:S(2)}) %collective-permute-start.19) | collective-permute-done | bytes 139296 | tf_op jit(solution)/shard_map/ppermute | solution.py:353
  106.5 1.6 %copy-done.6 = bf16[8,64,2048]{2,1,0:T(8,128)(2,1)S(1)} copy-done((bf16[8,64,2048]{2,1,0:T(8,128)(2,1)S(1)}, bf16[8,64,2048]{2,1,0:T(8,128)(2,1)}, u32[]{:S(2)}) %copy-start.6) | copy-done | bytes 2097176
  108.1 0.7 copy-done.9
  108.8 1.3 %final.1 = bf16[32,2048]{1,0:T(8,128)(2,1)} custom-call(s32[32,1]{1,0:T(8,128)S(1)} %copy-done.7, bf16[32,128]{1,0:T(8,128)(2,1)S(1)} %copy-done.9, bf16[512,2048]{1,0:T(8,128)(2,1)S(1)} %bitcast.8, bf16[32,2048]{1,0:T(8,128)(2,1)S(1)} %get-tuple-element.40.refs_0_, bf16[32,2048]{1,0:T(8,128)(2,1)S(1)} %collective-permute-done.18.refs_1_, ...), custom_call_target="tpu_custom_call" | custom-call | tf_op jit(solution)/shard_map/final/pallas_call | solution.py:305
  (55 shorter events, 1.5 us)
Async XLA Ops:
  6.5 100.0 %all-gather.2.cloned.1.call-start = ((), (), s32[]{:S(2)}) async-start(), calls=%async_computation | async-start | bytes 2621440 | tf_op jit(solution)/shard_map/all_gather | solution.py:371
  6.5 8.1 %collective-permute-start.12 = (bf16[32,2048]{1,0:T(8,128)(2,1)}, bf16[32,2048]{1,0:T(8,128)(2,1)S(1)}, u32[]{:S(2)}, u32[]{:S(2)}) collective-permute-start(bf16[32,2048]{1,0:T(8,128)(2,1)} %refs_0_.2), channel_id=1, source_target_pairs={{0,8},{4,12},{8,0},{12,4},{1,9},{5,13},{9,1},{13,5},{2,10},{6,14},... | collective-permute-start | bytes 393224 | tf_op jit(solution)/shard_map/ppermute | solution.py:350
  9.5 5.4 %collective-permute-start.8 = (bf16[32,2048]{1,0:T(8,128)(2,1)}, bf16[32,2048]{1,0:T(8,128)(2,1)S(1)}, u32[]{:S(2)}, u32[]{:S(2)}) collective-permute-start(bf16[32,2048]{1,0:T(8,128)(2,1)} %refs_0_.2), channel_id=1, source_target_pairs={{0,1},{1,0},{2,3},{3,2},{4,5},{5,4},{6,7},{7,6},{8,9},{9,8},{10,11... | collective-permute-start | bytes 393224 | tf_op jit(solution)/shard_map/ppermute | solution.py:353
  11.1 6.0 %collective-permute-start.13 = (bf16[32,2048]{1,0:T(8,128)(2,1)}, bf16[32,2048]{1,0:T(8,128)(2,1)S(1)}, u32[]{:S(2)}, u32[]{:S(2)}) collective-permute-start(bf16[32,2048]{1,0:T(8,128)(2,1)} %refs_0_.2), channel_id=1, source_target_pairs={{0,4},{4,0},{8,12},{12,8},{1,5},{5,1},{9,13},{13,9},{2,6},{6,2},{1... | collective-permute-start | bytes 393224 | tf_op jit(solution)/shard_map/ppermute | solution.py:347
  11.1 9.0 %collective-permute-start.4 = (bf16[32,2048]{1,0:T(8,128)(2,1)}, bf16[32,2048]{1,0:T(8,128)(2,1)S(1)}, u32[]{:S(2)}, u32[]{:S(2)}) collective-permute-start(bf16[32,2048]{1,0:T(8,128)(2,1)} %refs_0_.2), channel_id=1, source_target_pairs={{0,3},{1,2},{2,1},{3,0},{4,7},{5,6},{6,5},{7,4},{8,11},{9,10},{10,... | collective-permute-start | bytes 393224 | tf_op jit(solution)/shard_map/ppermute | solution.py:353
  13.5 12.9 %collective-permute-start = (bf16[32,2048]{1,0:T(8,128)(2,1)}, bf16[32,2048]{1,0:T(8,128)(2,1)S(1)}, u32[]{:S(2)}, u32[]{:S(2)}) collective-permute-start(bf16[32,2048]{1,0:T(8,128)(2,1)} %refs_0_.2), channel_id=1, source_target_pairs={{0,2},{1,3},{2,0},{3,1},{4,6},{5,7},{6,4},{7,5},{8,10},{9,11},{10,... | collective-permute-start | bytes 393224 | tf_op jit(solution)/shard_map/ppermute | solution.py:353
  14.6 11.9 %collective-permute-start.14 = (bf16[32,2048]{1,0:T(8,128)(2,1)S(1)}, bf16[32,2048]{1,0:T(8,128)(2,1)S(1)}, u32[]{:S(2)}, u32[]{:S(2)}) collective-permute-start(bf16[32,2048]{1,0:T(8,128)(2,1)S(1)} %collective-permute-done.12.refs_1_), channel_id=1, source_target_pairs={{0,4},{4,0},{8,12},{12,8},{1,5},{5,1},{9,13},{13,9},{2,6},{6,2},{1... | collective-permute-start | bytes 393224 | tf_op jit(solution)/shard_map/ppermute | solution.py:347
  14.8 12.2 %collective-permute-start.9 = (bf16[32,2048]{1,0:T(8,128)(2,1)S(1)}, bf16[32,2048]{1,0:T(8,128)(2,1)S(1)}, u32[]{:S(2)}, u32[]{:S(2)}) collective-permute-start(bf16[32,2048]{1,0:T(8,128)(2,1)S(1)} %collective-permute-done.8.refs_0_), channel_id=1, source_target_pairs={{0,8},{4,12},{8,0},{12,4},{1,9},{5,13},{9,1},{13,5},{2,10},{6,14},... | collective-permute-start | bytes 393224 | tf_op jit(solution)/shard_map/ppermute | solution.py:350
  17.0 19.9 %collective-permute-start.10 = (bf16[32,2048]{1,0:T(8,128)(2,1)S(1)}, bf16[32,2048]{1,0:T(8,128)(2,1)S(1)}, u32[]{:S(2)}, u32[]{:S(2)}) collective-permute-start(bf16[32,2048]{1,0:T(8,128)(2,1)S(1)} %collective-permute-done.8.refs_0_), channel_id=1, source_target_pairs={{0,4},{4,0},{8,12},{12,8},{1,5},{5,1},{9,13},{13,9},{2,6},{6,2},{1... | collective-permute-start | bytes 393224 | tf_op jit(solution)/shard_map/ppermute | solution.py:347
  20.1 17.2 %collective-permute-start.5 = (bf16[32,2048]{1,0:T(8,128)(2,1)S(1)}, bf16[32,2048]{1,0:T(8,128)(2,1)S(1)}, u32[]{:S(2)}, u32[]{:S(2)}) collective-permute-start(bf16[32,2048]{1,0:T(8,128)(2,1)S(1)} %collective-permute-done.4.refs_0_), channel_id=1, source_target_pairs={{0,8},{4,12},{8,0},{12,4},{1,9},{5,13},{9,1},{13,5},{2,10},{6,14},... | collective-permute-start | bytes 393224 | tf_op jit(solution)/shard_map/ppermute | solution.py:350
  26.4 18.0 %collective-permute-start.6 = (bf16[32,2048]{1,0:T(8,128)(2,1)S(1)}, bf16[32,2048]{1,0:T(8,128)(2,1)S(1)}, u32[]{:S(2)}, u32[]{:S(2)}) collective-permute-start(bf16[32,2048]{1,0:T(8,128)(2,1)S(1)} %collective-permute-done.4.refs_0_), channel_id=1, source_target_pairs={{0,4},{4,0},{8,12},{12,8},{1,5},{5,1},{9,13},{13,9},{2,6},{6,2},{1... | collective-permute-start | bytes 393224 | tf_op jit(solution)/shard_map/ppermute | solution.py:347
  26.5 11.0 %collective-permute-start.1 = (bf16[32,2048]{1,0:T(8,128)(2,1)S(1)}, bf16[32,2048]{1,0:T(8,128)(2,1)S(1)}, u32[]{:S(2)}, u32[]{:S(2)}) collective-permute-start(bf16[32,2048]{1,0:T(8,128)(2,1)S(1)} %collective-permute-done.refs_0_), channel_id=1, source_target_pairs={{0,8},{4,12},{8,0},{12,4},{1,9},{5,13},{9,1},{13,5},{2,10},{6,14},... | collective-permute-start | bytes 393224 | tf_op jit(solution)/shard_map/ppermute | solution.py:350
  27.0 10.8 %collective-permute-start.11 = (bf16[32,2048]{1,0:T(8,128)(2,1)S(1)}, bf16[32,2048]{1,0:T(8,128)(2,1)S(1)}, u32[]{:S(2)}, u32[]{:S(2)}) collective-permute-start(bf16[32,2048]{1,0:T(8,128)(2,1)S(1)} %collective-permute-done.9.refs_1_), channel_id=1, source_target_pairs={{0,4},{4,0},{8,12},{12,8},{1,5},{5,1},{9,13},{13,9},{2,6},{6,2},{1... | collective-permute-start | bytes 393224 | tf_op jit(solution)/shard_map/ppermute | solution.py:347
  27.2 1.0 copy-start
  28.3 1.0 copy-start.2
  29.3 0.9 copy-start.8
  30.2 7.6 %copy-start.1 = (f32[64,2048]{1,0:T(8,128)S(1)}, f32[64,2048]{1,0:T(8,128)}, u32[]{:S(2)}) copy-start(f32[64,2048]{1,0:T(8,128)} %refs_5_.7) | copy-start | bytes 1572868
  30.2 7.6 %copy-start.3 = (f32[64,2048]{1,0:T(8,128)S(1)}, f32[64,2048]{1,0:T(8,128)}, u32[]{:S(2)}) copy-start(f32[64,2048]{1,0:T(8,128)} %refs_7_.7) | copy-start | bytes 1572868
  36.9 14.1 %collective-permute-start.2 = (bf16[32,2048]{1,0:T(8,128)(2,1)S(1)}, bf16[32,2048]{1,0:T(8,128)(2,1)S(1)}, u32[]{:S(2)}, u32[]{:S(2)}) collective-permute-start(bf16[32,2048]{1,0:T(8,128)(2,1)S(1)} %collective-permute-done.refs_0_), channel_id=1, source_target_pairs={{0,4},{4,0},{8,12},{12,8},{1,5},{5,1},{9,13},{13,9},{2,6},{6,2},{1... | collective-permute-start | bytes 393224 | tf_op jit(solution)/shard_map/ppermute | solution.py:347
  37.3 7.1 %collective-permute-start.7 = (bf16[32,2048]{1,0:T(8,128)(2,1)S(1)}, bf16[32,2048]{1,0:T(8,128)(2,1)S(1)}, u32[]{:S(2)}, u32[]{:S(2)}) collective-permute-start(bf16[32,2048]{1,0:T(8,128)(2,1)S(1)} %collective-permute-done.5.refs_1_), channel_id=1, source_target_pairs={{0,4},{4,0},{8,12},{12,8},{1,5},{5,1},{9,13},{13,9},{2,6},{6,2},{1... | collective-permute-start | bytes 393224 | tf_op jit(solution)/shard_map/ppermute | solution.py:347
  37.5 13.5 %collective-permute-start.3 = (bf16[32,2048]{1,0:T(8,128)(2,1)S(1)}, bf16[32,2048]{1,0:T(8,128)(2,1)S(1)}, u32[]{:S(2)}, u32[]{:S(2)}) collective-permute-start(bf16[32,2048]{1,0:T(8,128)(2,1)S(1)} %collective-permute-done.1.refs_1_), channel_id=1, source_target_pairs={{0,4},{4,0},{8,12},{12,8},{1,5},{5,1},{9,13},{13,9},{2,6},{6,2},{1... | collective-permute-start | bytes 393224 | tf_op jit(solution)/shard_map/ppermute | solution.py:347
  51.0 7.2 %copy-start.4 = (f32[16,8192]{1,0:T(8,128)S(1)}, f32[16,8192]{1,0:T(8,128)}, u32[]{:S(2)}) copy-start(f32[16,8192]{1,0:T(8,128)} %ds.7) | copy-start | bytes 1572868
  58.2 8.8 %copy-start.5 = (bf16[2048,512]{1,0:T(8,128)(2,1)S(1)}, bf16[2048,512]{1,0:T(8,128)(2,1)}, u32[]{:S(2)}) copy-start(bf16[2048,512]{1,0:T(8,128)(2,1)} %refs_0_.3) | copy-start | bytes 6291460
  62.4 13.7 %collective-permute-start.20 = (bf16[64,2048]{1,0:T(8,128)(2,1)S(1)}, bf16[64,2048]{1,0:T(8,128)(2,1)S(1)}, u32[]{:S(2)}, u32[]{:S(2)}) collective-permute-start(bf16[64,2048]{1,0:T(8,128)(2,1)S(1)} %get-tuple-element.34), channel_id=1, source_target_pairs={{0,4},{4,0},{8,12},{12,8},{1,5},{5,1},{9,13},{13,9},{2,6},{6,2},{1... | collective-permute-start | bytes 786440 | tf_op jit(solution)/shard_map/ppermute | solution.py:347
  66.7 39.8 %copy-start.7 = (s32[32,1]{1,0:T(8,128)S(1)}, s32[32,1]{1,0:T(8,128)}, u32[]{:S(2)}) copy-start(s32[32,1]{1,0:T(8,128)} %copy.21.pool_row) | copy-start | bytes 388
  66.7 11.1 %collective-permute-start.23 = (bf16[64,2048]{1,0:T(8,128)(2,1)S(1)}, bf16[64,2048]{1,0:T(8,128)(2,1)S(1)}, u32[]{:S(2)}, u32[]{:S(2)}) collective-permute-start(bf16[64,2048]{1,0:T(8,128)(2,1)S(1)} %get-tuple-element.36), channel_id=1, source_target_pairs={{0,4},{4,0},{8,12},{12,8},{1,5},{5,1},{9,13},{13,9},{2,6},{6,2},{1... | collective-permute-start | bytes 786440 | tf_op jit(solution)/shard_map/ppermute | solution.py:347
  71.5 7.1 %collective-permute-start.15 = (bf16[64,2560]{1,0:T(8,128)(2,1)S(1)}, bf16[64,2560]{1,0:T(8,128)(2,1)S(1)}, u32[]{:S(2)}, u32[]{:S(2)}) collective-permute-start(bf16[64,2560]{1,0:T(8,128)(2,1)S(1)} %get-tuple-element.28), channel_id=1, source_target_pairs={{0,4},{4,0},{8,12},{12,8},{1,5},{5,1},{9,13},{13,9},{2,6},{6,2},{1... | collective-permute-start | bytes 983048 | tf_op jit(solution)/shard_map/ppermute | solution.py:347
  75.7 2.7 %collective-permute-start.17 = (bf16[64,2048]{1,0:T(8,128)(2,1)S(1)}, bf16[64,2048]{1,0:T(8,128)(2,1)S(1)}, u32[]{:S(2)}, u32[]{:S(2)}) collective-permute-start(bf16[64,2048]{1,0:T(8,128)(2,1)S(1)} %get-tuple-element.31), channel_id=1, source_target_pairs={{0,4},{4,0},{8,12},{12,8},{1,5},{5,1},{9,13},{13,9},{2,6},{6,2},{1... | collective-permute-start | bytes 786440 | tf_op jit(solution)/shard_map/ppermute | solution.py:347
  76.2 6.4 %collective-permute-start.21 = (bf16[32,2048]{1,0:T(8,128)(2,1)S(1)}, bf16[32,2048]{1,0:T(8,128)(2,1)S(1)}, u32[]{:S(2)}, u32[]{:S(2)}) collective-permute-start(bf16[32,2048]{1,0:T(8,128)(2,1)S(1)} %slice.37), channel_id=1, source_target_pairs={{0,8},{4,12},{8,0},{12,4},{1,9},{5,13},{9,1},{13,5},{2,10},{6,14},... | collective-permute-start | bytes 393224 | tf_op jit(solution)/shard_map/ppermute | solution.py:350
  77.8 7.6 %collective-permute-start.24 = (bf16[32,2048]{1,0:T(8,128)(2,1)S(1)}, bf16[32,2048]{1,0:T(8,128)(2,1)S(1)}, u32[]{:S(2)}, u32[]{:S(2)}) collective-permute-start(bf16[32,2048]{1,0:T(8,128)(2,1)S(1)} %slice.39), channel_id=1, source_target_pairs={{0,8},{4,12},{8,0},{12,4},{1,9},{5,13},{9,1},{13,5},{2,10},{6,14},... | collective-permute-start | bytes 393224 | tf_op jit(solution)/shard_map/ppermute | solution.py:350
  79.3 8.9 %collective-permute-start.16 = (bf16[32,2560]{1,0:T(8,128)(2,1)S(1)}, bf16[32,2560]{1,0:T(8,128)(2,1)S(1)}, u32[]{:S(2)}, u32[]{:S(2)}) collective-permute-start(bf16[32,2560]{1,0:T(8,128)(2,1)S(1)} %get-tuple-element.37), channel_id=1, source_target_pairs={{0,8},{4,12},{8,0},{12,4},{1,9},{5,13},{9,1},{13,5},{2,10},{6,14},... | collective-permute-start | bytes 491528 | tf_op jit(solution)/shard_map/ppermute | solution.py:350
  88.2 0.7 copy-start.10
  91.5 9.5 %collective-permute-start.22 = (bf16[32,2176]{1,0:T(8,128)(2,1)S(1)}, bf16[32,2176]{1,0:T(8,128)(2,1)S(1)}, u32[]{:S(2)}, u32[]{:S(2)}) collective-permute-start(bf16[32,2176]{1,0:T(8,128)(2,1)S(1)} %get-tuple-element.42), channel_id=1, source_target_pairs={{0,3},{1,2},{2,1},{3,0},{4,7},{5,6},{6,5},{7,4},{8,11},{9,10},{10,... | collective-permute-start | bytes 417800 | tf_op jit(solution)/shard_map/ppermute | solution.py:353
  94.2 7.7 %collective-permute-start.25 = (bf16[32,2176]{1,0:T(8,128)(2,1)S(1)}, bf16[32,2176]{1,0:T(8,128)(2,1)S(1)}, u32[]{:S(2)}, u32[]{:S(2)}) collective-permute-start(bf16[32,2176]{1,0:T(8,128)(2,1)S(1)} %get-tuple-element.41), channel_id=1, source_target_pairs={{0,1},{1,0},{2,3},{3,2},{4,5},{5,4},{6,7},{7,6},{8,9},{9,8},{10,11... | collective-permute-start | bytes 417800 | tf_op jit(solution)/shard_map/ppermute | solution.py:353
  94.6 11.9 %collective-permute-start.19 = (bf16[32,2176]{1,0:T(8,128)(2,1)}, bf16[32,2176]{1,0:T(8,128)(2,1)S(1)}, u32[]{:S(2)}, u32[]{:S(2)}) collective-permute-start(bf16[32,2176]{1,0:T(8,128)(2,1)} %get-tuple-element.32), channel_id=1, source_target_pairs={{0,2},{1,3},{2,0},{3,1},{4,6},{5,7},{6,4},{7,5},{8,10},{9,11},{10,... | collective-permute-start | bytes 417800 | tf_op jit(solution)/shard_map/ppermute | solution.py:353
  95.9 5.0 %collective-permute-start.18 = (bf16[32,2048]{1,0:T(8,128)(2,1)S(1)}, bf16[32,2048]{1,0:T(8,128)(2,1)S(1)}, u32[]{:S(2)}, u32[]{:S(2)}) collective-permute-start(bf16[32,2048]{1,0:T(8,128)(2,1)S(1)} %get-tuple-element.39), channel_id=1, source_target_pairs={{0,8},{4,12},{8,0},{12,4},{1,9},{5,13},{9,1},{13,5},{2,10},{6,14},... | collective-permute-start | bytes 393224 | tf_op jit(solution)/shard_map/ppermute | solution.py:350
  106.5 1.6 %copy-start.6 = (bf16[8,64,2048]{2,1,0:T(8,128)(2,1)S(1)}, bf16[8,64,2048]{2,1,0:T(8,128)(2,1)}, u32[]{:S(2)}) copy-start(bf16[8,64,2048]{2,1,0:T(8,128)(2,1)} %all-gather.2.cloned.1.call-done) | copy-start | bytes 6291460
  108.1 0.7 copy-start.9
Sparse Core Ops, SparseCore 0:
  13.8 26.4 all-gather.1

commit v2 on v1

v2 whole, which is shorter than its diff:
```python
import functools
import jax
import jax.numpy as jnp
from jax import lax
from jax.experimental import pallas as pl
from jax.experimental.pallas import tpu as pltpu
from jax.sharding import PartitionSpec as P

GROUP = 128
LANES = 128
MIB = 1024 * 1024
BLOCK = 512


def vmem():
    return pl.BlockSpec(memory_space=pltpu.VMEM)


def smem():
    return pl.BlockSpec(memory_space=pltpu.SMEM)


def hbm():
    return pl.BlockSpec(memory_space=pltpu.HBM)


def anywhere():
    return pl.BlockSpec(memory_space=pl.ANY)


def after(value, *earlier):
    return lax.optimization_barrier((value,) + earlier)[0]


def scaled(levels, scales, first_group, groups):
    parts = []
    for g in range(groups):
        row = scales[pl.ds(first_group + g, 1), :].astype(jnp.bfloat16)
        parts.append(levels[g * GROUP : (g + 1) * GROUP, :] * row)
    return jnp.concatenate(parts, axis=0) if groups > 1 else parts[0]


def as_column(row):
    rows = row.shape[1]
    place = lax.broadcasted_iota(jnp.int32, (rows, rows), 0)
    same = place == lax.broadcasted_iota(jnp.int32, (rows, rows), 1)
    return jnp.sum(jnp.where(same, row, jnp.zeros_like(row)), axis=1, keepdims=True)


def fill_kernel(
    kb, count, depth, order, where, pool_index, act_scale, ids,
    gl, gs, ul, us, ds, gbuf, ubuf, gs_out, us_out, ds_out, row_scale, pool_row,
    pool_held, act_held, ids_held, act_column, small_sems, sems,
):
    k = pl.multiple_of(where[1] * depth, kb)
    small = [(pool_index, pool_held), (act_scale, act_held), (ids, ids_held)]
    small = [pltpu.make_async_copy(a, b, small_sems.at[i]) for i, (a, b) in enumerate(small)]
    for c in small:
        c.start()
    moves = [(gs, gs_out), (us, us_out), (ds, ds_out)]
    for j in range(count):
        rows = pl.ds(k + j * kb, kb)
        moves += [(gl.at[rows, :], gbuf.at[j]), (ul.at[rows, :], ubuf.at[j])]
    made = [pltpu.make_async_copy(a, b, sems.at[i]) for i, (a, b) in enumerate(moves)]
    for c in made:
        c.start()
    for c in small:
        c.wait()
    rows = ids.shape[1]
    act_column[...] = as_column(act_held[...])
    for p, o in enumerate(order):
        at = pl.multiple_of((where[0] ^ o) * rows, rows)
        row_scale[p * rows : (p + 1) * rows, :] = act_column[pl.ds(at, rows), :]
    column = as_column(ids_held[...].astype(jnp.float32)).astype(jnp.int32)
    named = lax.broadcasted_iota(jnp.int32, (rows, pool_held.shape[1]), 1) == column
    chosen = jnp.where(named, pool_held[...].astype(jnp.float32), 0.0)
    pool_row[...] = jnp.sum(chosen, axis=1, keepdims=True).astype(jnp.int32)
    for c in made:
        c.wait()


def fill(where, pool_index, act_scale, ids, order, depth, gl, gs, ul, us, ds, kb, count):
    block = pltpu.VMEM((count, kb, gl.shape[1]), gl.dtype)
    out_shape = [block, block] + [jax.ShapeDtypeStruct(v.shape, v.dtype) for v in (gs, us, ds)]
    rows = ids.shape[1]
    out_shape += [
        jax.ShapeDtypeStruct((rows * len(order), 1), jnp.float32),
        jax.ShapeDtypeStruct((rows, 1), jnp.int32),
    ]
    return pl.pallas_call(
        functools.partial(fill_kernel, kb, count, depth, order),
        out_shape=out_shape,
        in_specs=[smem()] + [anywhere()] * 3 + [hbm()] * 5,
        out_specs=[vmem()] * 7,
        scratch_shapes=[
            pltpu.VMEM(pool_index.shape, jnp.int32),
            pltpu.VMEM(act_scale.shape, jnp.float32),
            pltpu.VMEM(ids.shape, jnp.int32),
            pltpu.VMEM((act_scale.shape[1], 1), jnp.float32),
            pltpu.SemaphoreType.DMA((3,)),
            pltpu.SemaphoreType.DMA((3 + 2 * count,)),
        ],
        compiler_params=pltpu.CompilerParams(vmem_limit_bytes=4 * MIB),
        cost_estimate=pl.CostEstimate(
            flops=0, bytes_accessed=4 * count * kb * gl.shape[1], transcendentals=0
        ),
        name="fill",
    )(where, pool_index, act_scale, ids, gl, gs, ul, us, ds)


def run(steps, stage, ahead):
    for c in ahead:
        c.start()

    def body(step, carry):
        stage(step)
        return carry

    lax.fori_loop(0, steps, body, 0)
    for c in ahead:
        c.wait()


def gate_up_kernel(pieces, distances, coming, first, last, kb, ahead, where, *refs):
    blocks = len(distances)
    rows_in = refs[: pieces * blocks]
    refs = refs[pieces * blocks :]
    gl, gs, ul, us, g_held, u_held = refs[:6]
    refs = refs[6:]
    if not first:
        gate_in, up_in = refs[:2]
        refs = refs[2:]
    if last:
        act_scale, dl, hidden, d_next = refs[:4]
        refs = refs[4:]
        gate, up = refs[:2]
        refs = refs[2:]
    else:
        gate, up, g_next, u_next = refs[:4]
        refs = refs[4:]
    xs, row_sems, ahead_sems = refs
    rows = rows_in[0].shape[0]
    depth = rows_in[0].shape[1]
    per_block = depth // kb
    steps = blocks * per_block

    row_copies = [
        pltpu.make_async_copy(
            rows_in[b * pieces + p],
            xs.at[p * rows : (p + 1) * rows, b * depth : (b + 1) * depth],
            row_sems.at[b * pieces + p],
        )
        for b in range(blocks)
        for p in range(pieces)
    ]
    for c in row_copies:
        c.start()

    def place(step):
        block = where[1] ^ distances[0]
        for b in range(1, blocks):
            block = jnp.where(step // per_block == b, where[1] ^ distances[b], block)
        return pl.multiple_of(block * depth + (step % per_block) * kb, kb)

    following = []
    for j in range(ahead):
        if last:
            down_kb, width = d_next.shape[1:]
            col = pl.multiple_of((where[1] ^ coming[0]) * width, width)
            source = dl.at[j * down_kb : (j + 1) * down_kb, pl.ds(col, width)]
            following.append(pltpu.make_async_copy(source, d_next.at[j], ahead_sems.at[j]))
        else:
            k = (where[1] ^ coming[j // per_block]) * depth + (j % per_block) * kb
            k = pl.multiple_of(k, kb)
            for i, (a, b) in enumerate(((gl, g_next), (ul, u_next))):
                following.append(
                    pltpu.make_async_copy(
                        a.at[pl.ds(k, kb), :], b.at[j], ahead_sems.at[2 * j + i]
                    )
                )

    def add(total, given, scales, step):
        block = given.at[step]
        group = place(step) // GROUP
        total[...] += jnp.dot(
            xs[:, pl.ds(pl.multiple_of(step * kb, kb), kb)],
            scaled(block, scales, group, kb // GROUP),
            preferred_element_type=jnp.float32,
        )

    if first:
        gate[...] = jnp.zeros_like(gate)
        up[...] = jnp.zeros_like(up)
    else:
        gate[...] = gate_in[...]
        up[...] = up_in[...]
    for c in row_copies:
        c.wait()
    def both(step):
        add(gate, g_held, gs, step)
        add(up, u_held, us, step)

    run(steps, both, following)
    if last:
        g = gate[...] * act_scale[...]
        u = up[...] * act_scale[...]
        hidden[...] = (g / (1.0 + jnp.exp(-g)) * u).astype(jnp.bfloat16)


def gate_up(where, distances, coming, blocks_in, gl, gs, ul, us, carried, acc, act_scale, dl, kb, down_kb, ahead):
    first, last = acc is None, act_scale is not None
    blocks, pieces = len(blocks_in), len(blocks_in[0])
    rows, depth = blocks_in[0][0].shape
    width = gl.shape[1]
    ins = [where] + [p for b in blocks_in for p in b] + [gl, gs, ul, us] + list(carried)
    specs = [smem()] + [anywhere()] * (blocks * pieces) + [hbm(), vmem(), hbm(), vmem()]
    specs += [vmem(), vmem()]
    if not first:
        ins += list(acc)
        specs += [vmem(), vmem()]
    total = jax.ShapeDtypeStruct((rows * pieces, width), jnp.float32)
    scratch = []
    if last:
        ins += [act_scale, dl]
        specs += [vmem(), hbm()]
        out_shape = [jax.ShapeDtypeStruct((rows * pieces, width), jnp.bfloat16)]
        out_shape += [pltpu.VMEM((ahead, down_kb, depth), jnp.bfloat16)]
        scratch += [pltpu.VMEM(total.shape, jnp.float32)] * 2
    else:
        out_shape = [total, total] + [pltpu.VMEM((ahead, kb, width), jnp.bfloat16)] * 2
    scratch += [
        pltpu.VMEM((rows * pieces, blocks * depth), jnp.bfloat16),
        pltpu.SemaphoreType.DMA((blocks * pieces,)),
        pltpu.SemaphoreType.DMA((2 * ahead,)),
    ]
    return pl.pallas_call(
        functools.partial(gate_up_kernel, pieces, distances, coming, first, last, kb, ahead),
        out_shape=out_shape,
        in_specs=specs,
        out_specs=[vmem()] * len(out_shape),
        scratch_shapes=scratch,
        compiler_params=pltpu.CompilerParams(vmem_limit_bytes=8 * MIB),
        cost_estimate=pl.CostEstimate(
            flops=4 * rows * pieces * blocks * depth * width,
            bytes_accessed=4 * blocks * depth * width,
            transcendentals=0,
        ),
        name="gate_up",
    )(*ins)


def down_kernel(distances, kb, ahead, shrink_too, where, hidden, dl, ds, d_held, *refs):
    if shrink_too:
        shrink = refs[0]
        refs = refs[1:]
    mine, theirs = refs[:2]
    refs = refs[2:]
    if ahead:
        d_next = refs[0]
        refs = refs[1:]
    acc, ahead_sems = refs
    depth, width = hidden.shape[1], acc.shape[1]
    half = mine.shape[0]
    steps = depth // kb
    col = pl.multiple_of((where[1] ^ distances[0]) * width, width)

    following = []
    for j in range(ahead):
        next_col = pl.multiple_of((where[1] ^ distances[1]) * width, width)
        source = dl.at[j * kb : (j + 1) * kb, pl.ds(next_col, width)]
        following.append(pltpu.make_async_copy(source, d_next.at[j], ahead_sems.at[j]))

    def add(step):
        block = d_held.at[step]
        parts = []
        for g in range(kb // GROUP):
            row = ds[pl.ds(step * (kb // GROUP) + g, 1), pl.ds(col, width)].astype(jnp.bfloat16)
            parts.append(block[g * GROUP : (g + 1) * GROUP, :] * row)
        weight = jnp.concatenate(parts, axis=0) if len(parts) > 1 else parts[0]
        acc[...] += jnp.dot(
            hidden[:, pl.ds(pl.multiple_of(step * kb, kb), kb)],
            weight,
            preferred_element_type=jnp.float32,
        )

    def project():
        low = jnp.dot(hidden[...], shrink[...], preferred_element_type=jnp.float32)
        mine[:, width:] = low[:half]
        theirs[:, width:] = low[half:].astype(jnp.bfloat16)

    acc[...] = jnp.zeros_like(acc)
    run(steps, add, following)
    if shrink_too:
        project()
    mine[:, :width] = acc[:half, :]
    theirs[:, :width] = acc[half:, :].astype(jnp.bfloat16)


def down(where, distances, hidden, dl, ds, carried, width, shrink, kb, ahead):
    rows, depth = hidden.shape
    wide = width + (0 if shrink is None else shrink.shape[1])
    ins = [where, hidden, dl, ds, carried]
    specs = [smem(), vmem(), hbm(), vmem(), vmem()]
    if shrink is not None:
        ins.append(shrink)
        specs.append(vmem())
    out_shape = [
        jax.ShapeDtypeStruct((rows // 2, wide), jnp.float32),
        jax.ShapeDtypeStruct((rows // 2, wide), jnp.bfloat16),
    ]
    if ahead:
        out_shape.append(pltpu.VMEM((ahead, kb, width), jnp.bfloat16))
    return pl.pallas_call(
        functools.partial(down_kernel, distances, kb, ahead, shrink is not None),
        out_shape=out_shape,
        in_specs=specs,
        out_specs=[vmem()] * len(out_shape),
        scratch_shapes=[
            pltpu.VMEM((rows, width), jnp.float32),
            pltpu.SemaphoreType.DMA((max(1, ahead),)),
        ],
        compiler_params=pltpu.CompilerParams(vmem_limit_bytes=8 * MIB),
        cost_estimate=pl.CostEstimate(
            flops=2 * rows * depth * width, bytes_accessed=2 * depth * width, transcendentals=0
        ),
        name="down",
    )(*ins)


def cost(count):
    return pl.CostEstimate(flops=count, bytes_accessed=4 * count, transcendentals=0)


def pair_kernel(chips, mine, got, own, *send):
    rows = own.shape[0]
    own[...] = mine[:rows, :] + got[:rows, :].astype(jnp.float32)
    for s in range(1, chips):
        at = slice(s * rows, (s + 1) * rows)
        send[s - 1][...] = (mine[at, :] + got[at, :].astype(jnp.float32)).astype(jnp.bfloat16)


def pair_sum(mine, got, chips):
    rows, width = mine.shape[0] // chips, mine.shape[1]
    out_shape = [jax.ShapeDtypeStruct((rows, width), jnp.float32)]
    out_shape += [jax.ShapeDtypeStruct((rows, width), jnp.bfloat16)] * (chips - 1)
    return pl.pallas_call(
        functools.partial(pair_kernel, chips),
        out_shape=out_shape,
        in_specs=[vmem()] * 2,
        out_specs=[vmem()] * chips,
        compiler_params=pltpu.CompilerParams(vmem_limit_bytes=4 * MIB),
        cost_estimate=cost(rows * chips * width),
        name="pair",
    )(mine, got)


def attach_kernel(count, low, *refs):
    parts, out = refs[:count], refs[count]
    width = parts[0].shape[1]
    total = parts[0][...]
    for p in parts[1:]:
        total = total + p[...].astype(jnp.float32)
    out[:, :width] = total.astype(jnp.bfloat16)
    out[:, width:] = low[...]


def attach(parts, low):
    rows, width = parts[0].shape
    return pl.pallas_call(
        functools.partial(attach_kernel, len(parts)),
        out_shape=jax.ShapeDtypeStruct((rows, width + low.shape[1]), jnp.bfloat16),
        in_specs=[vmem()] * (1 + len(parts)),
        out_specs=vmem(),
        compiler_params=pltpu.CompilerParams(vmem_limit_bytes=4 * MIB),
        cost_estimate=cost(rows * width * len(parts)),
        name="attach",
    )(low, *parts)


def fold_matrix(pool_width, rank, lanes, transposed):
    shape = (lanes, pool_width) if transposed else (pool_width, lanes)
    wide = lax.broadcasted_iota(jnp.int32, shape, 1 if transposed else 0)
    slim = lax.broadcasted_iota(jnp.int32, shape, 0 if transposed else 1)
    return (lax.rem(wide, rank) == slim).astype(jnp.float32).astype(jnp.bfloat16)


def pool_mask(pool_row, rows, pool_width, rank):
    column = lax.broadcasted_iota(jnp.int32, (rows, pool_width), 1)
    start = pool_row * rank
    return (column >= start) & (column < start + rank)


def message_kernel(count, width, rank, pool_row, *refs):
    parts, (out, low) = refs[:count], refs[count:]
    total = parts[0][...].astype(jnp.float32)
    for p in parts[1:]:
        total = total + p[...].astype(jnp.float32)
    rows, wide = total.shape
    mask = pool_mask(pool_row[...], rows, wide - width, rank)
    chosen = jnp.where(mask, total[:, width:], 0.0).astype(jnp.bfloat16)
    part = jnp.dot(
        chosen,
        fold_matrix(wide - width, rank, low.shape[1], False),
        preferred_element_type=jnp.float32,
    ).astype(jnp.bfloat16)
    low[...] = part
    out[:, :width] = total[:, :width].astype(jnp.bfloat16)
    out[:, width:] = part


def message(parts, pool_row, width, rank):
    rows = parts[0].shape[0]
    lanes = max(LANES, rank)
    return pl.pallas_call(
        functools.partial(message_kernel, len(parts), width, rank),
        out_shape=[
            jax.ShapeDtypeStruct((rows, width + lanes), jnp.bfloat16),
            jax.ShapeDtypeStruct((rows, lanes), jnp.bfloat16),
        ],
        in_specs=[vmem()] * (1 + len(parts)),
        out_specs=[vmem()] * 2,
        compiler_params=pltpu.CompilerParams(vmem_limit_bytes=6 * MIB),
        cost_estimate=cost(rows * width * len(parts)),
        name="message",
    )(pool_row, *parts)


def final_kernel(count, wides, order, rank, where, pool_row, low, *refs):
    pieces = len(order)
    pool, refs = refs[:pieces], refs[pieces:]
    parts, wide, out = refs[:count], refs[count : count + wides], refs[count + wides]
    rows, width = out.shape
    total_low = low[...].astype(jnp.float32)
    for w in wide:
        total_low = total_low + w[:, width:].astype(jnp.float32)
    total_low = total_low.astype(jnp.bfloat16)
    pool_width = pool[0].shape[0]
    spread = jnp.dot(
        total_low,
        fold_matrix(pool_width, rank, total_low.shape[1], True),
        preferred_element_type=jnp.float32,
    )
    total = jnp.zeros((rows, width), jnp.float32)
    for p in range(pieces):
        held = pool_row[...] - (where[0] ^ order[p]) * (pool_width // rank)
        mask = pool_mask(held, rows, pool_width, rank)
        chosen = jnp.where(mask, spread, 0.0).astype(jnp.bfloat16)
        total = total + jnp.dot(chosen, pool[p][...], preferred_element_type=jnp.float32)
    for p in parts:
        total = total + p[...].astype(jnp.float32)
    for w in wide:
        total = total + w[:, :width].astype(jnp.float32)
    out[...] = total.astype(jnp.bfloat16)


def final(parts, wide, where, order, pool_row, low, pool, rank):
    rows, width = parts[0].shape
    return pl.pallas_call(
        functools.partial(final_kernel, len(parts), len(wide), order, rank),
        out_shape=jax.ShapeDtypeStruct((rows, width), jnp.bfloat16),
        in_specs=[smem()] + [vmem()] * (2 + len(pool) + len(parts) + len(wide)),
        out_specs=vmem(),
        compiler_params=pltpu.CompilerParams(vmem_limit_bytes=4 * MIB),
        name="final",
            cost_estimate=cost(0),
    )(where, pool_row, low, *pool, *parts, *wide)


def nearest_first(count):
    return sorted(range(1, count), key=lambda d: (d.bit_length(), -d))


def local(replicas, tensors, *args):
    (
        act_codes,
        act_scale,
        adapter_ids,
        seg_starts,
        pool_index,
        gate_levels,
        gate_scale,
        up_levels,
        up_scale,
        down_levels,
        down_scale,
        shrink_weight,
        expand_rows,
    ) = args
    replica = lax.axis_index("replica")
    tensor = lax.axis_index("tensor")
    cores = 2
    chips = replicas // cores
    rows, depth = act_codes.shape
    rank, width = expand_rows.shape[1], expand_rows.shape[2]
    hidden_rows = down_levels.shape[0]

    def core_swap(v):
        return lax.ppermute(v, "replica", [(r, r ^ 1) for r in range(replicas)])

    def chip_swap(v, s):
        return lax.ppermute(v, "replica", [(r, r ^ (s * cores)) for r in range(replicas)])

    def tensor_swap(v, d):
        return lax.ppermute(v, "tensor", [(t, t ^ d) for t in range(tensors)])

    order = [s * cores for s in range(chips)] + [s * cores + 1 for s in range(chips)]

    def spread_block(v):
        same = [v] + [chip_swap(v, s) for s in range(1, chips)]
        return same + [core_swap(p) for p in same]

    gate_levels, up_levels, down_levels, gate_scale, up_scale, down_scale = (
        pltpu.with_memory_space_constraint(v, pltpu.HBM)
        for v in (gate_levels, up_levels, down_levels, gate_scale, up_scale, down_scale)
    )
    near = [0] + nearest_first(tensors)
    far = near[1:][::-1] + [0]
    kb = min(BLOCK, depth)
    down_kb = min(BLOCK, hidden_rows)
    where = jnp.stack([replica, tensor]).astype(jnp.int32)

    groups = [near[:1]]
    rest = near[1:]
    if len(rest) <= 3:
        groups += [[d] for d in rest]
    else:
        groups += [rest[: len(rest) // 2], rest[len(rest) // 2 :]]

    moved = {d: tensor_swap(act_codes, d) for d in groups[1]}
    same = [act_codes] + [chip_swap(act_codes, s) for s in range(1, chips)]
    filled = fill(
        where,
        *(
            pltpu.with_memory_space_constraint(v[None, :], pltpu.HBM)
            for v in (pool_index, act_scale, adapter_ids)
        ),
        order,
        depth,
        gate_levels,
        gate_scale,
        up_levels,
        up_scale,
        down_scale,
        kb,
        depth // kb,
    )
    carried = filled[:2]
    gate_scale, up_scale, down_scale, row_scale, pool_row = filled[2:]
    arrived = {0: same + [core_swap(after(p, pool_row)) for p in same]}
    codes_later = after(act_codes, pool_row)
    for d in groups[1]:
        arrived[d] = spread_block(after(moved[d], pool_row))
    for late in groups[2:]:
        for d in late:
            moved[d] = tensor_swap(codes_later, d)
    acc = None
    for i, g in enumerate(groups):
        is_last = i == len(groups) - 1
        following = far[:1] if is_last else groups[i + 1]
        out = gate_up(
            where,
            g,
            following,
            [arrived[d] for d in g],
            gate_levels,
            gate_scale,
            up_levels,
            up_scale,
            carried,
            acc,
            row_scale if is_last else None,
            down_levels,
            kb,
            down_kb,
            hidden_rows // down_kb if is_last else len(following) * depth // kb,
        )
        if is_last:
            hidden, carried = out
        else:
            acc, carried = out[:2], out[2:]
        if i == 0:
            for late in groups[2:]:
                for d in late:
                    arrived[d] = spread_block(after(moved[d], acc[0]))
        if i == 1:
            pool = spread_block(after(expand_rows.reshape(-1, width), acc[0]))

    low = None
    received = []
    sent, sums, messages = [], [], []
    for n, d in enumerate(far):
        more = n + 1 < len(far)
        source = hidden
        if n >= 2:
            source = after(source, sums[n - 2])
        if n >= 3:
            source = after(source, messages[n - 3])
        out = down(
            where,
            [d] + far[n + 1 : n + 2],
            source,
            down_levels,
            down_scale,
            carried,
            width,
            shrink_weight if n == 0 else None,
            down_kb,
            hidden_rows // down_kb if more else 0,
        )
        mine, theirs = out[:2]
        carried = out[2] if more else None
        own, *send = pair_sum(mine, core_swap(theirs), chips)
        sums.append(send[0])
        parts = [own] + [chip_swap(send[s - 1], s) for s in range(1, chips)]
        if n == 0:
            block, low = message(parts, pool_row, width, rank)
        elif d:
            block = attach(parts, low)
        if d:
            messages.append(block)
            received.append(tensor_swap(block, d))
    return final(parts, received, where, order, pool_row, low, pool, rank)


def solution(mesh):
    placed = (
        P(("parts", "replica"), "tensor"),
        P("parts"),
        P(("parts", "replica")),
        P("parts", None),
        P("parts"),
        P(None, ("replica", "tensor")),
        P(None, ("replica", "tensor")),
        P(None, ("replica", "tensor")),
        P(None, ("replica", "tensor")),
        P(("replica", "tensor"), None),
        P(("replica", "tensor"), None),
        P(("replica", "tensor"), None),
        P("replica", None, "tensor"),
    )
    return jax.shard_map(
        functools.partial(local, mesh.shape["replica"], mesh.shape["tensor"]),
        mesh=mesh,
        in_specs=placed,
        out_specs=P(("parts", "replica"), "tensor"),
        check_vma=False,
    )
```

time: 117 us -> 91.5 us (0.78)
  between operations: 13.7 us -> 0.23 us
  waiting for transfers between devices: 25.3 us -> 14.4 us
  local copies, waits for them, and re-layouts: 8.4 us -> 0.01 us
  Pallas kernels: 46.7 us -> 52 us
  starting transfers between devices: 21 us -> 24.6 us
  other arithmetic: 1.89 us -> 0.07 us
    pallas_call x9 -> x16, Pallas kernels: 44.8 us -> 51.8 us  [the longest x4 27.4 us: gate_up(): pl.pallas_call(functools.partial(gate_up_kernel, pieces, distances, comin...]
    unnamed x22 -> x6, local copies, waits for them, and re-layouts: 5.97 us -> 0.01 us
    ppermute x6, waiting for transfers between devices: 14.4 us -> 8.55 us  [tensor_swap(): return lax.ppermute(v, 'tensor', [(t, t ^ d) for t in range(tensors)])]
    ppermute x8 -> x9, waiting for transfers between devices: 10.8 us -> 5.82 us  [chip_swap(): lax.ppermute(v, 'replica', [(r, r ^ s * cores) for r in range(replicas)])]
    ppermute x6, starting transfers between devices: 8.62 us -> 10.7 us  [tensor_swap(): return lax.ppermute(v, 'tensor', [(t, t ^ d) for t in range(tensors)])]
    ppermute x8 -> x9, starting transfers between devices: 9.73 us -> 11.6 us  [chip_swap(): lax.ppermute(v, 'replica', [(r, r ^ s * cores) for r in range(replicas)])]
    pallas_call x1, Pallas kernels: 1.88 us -> 0.19 us  [message(): pl.pallas_call(functools.partial(message_kernel, len(parts), width, rank)...]
    ppermute x12 -> x14, starting transfers between devices: 2.64 us -> 2.39 us  [core_swap(): return lax.ppermute(v, 'replica', [(r, r ^ 1) for r in range(replicas)])]
  transfers between devices with their start and end apart: 27 -> 29, of which waited for: 8 -> 6; matrix products, arithmetic and copies ran while one was open for 4% -> 0% of each run, Pallas kernels for 39% -> 55%
where the time goes in v2:
time: 91.5 us; the launch traced here: 91.4 us
  Pallas kernels  52 us (57%)
  starting transfers between devices  24.6 us (27%)
  waiting for transfers between devices  14.4 us (16%)
    pallas_call x4, Pallas kernels, gate_up(): pl.pallas_call(functools.partial(gate_up_kernel, pieces, distances, comin...  27.4 us
    pallas_call x4, Pallas kernels, down(): pl.pallas_call(functools.partial(down_kernel, distances, kb, ahead, shrin...  15.4 us
    ppermute x9, starting transfers between devices, chip_swap(): lax.ppermute(v, 'replica', [(r, r ^ s * cores) for r in range(replicas)])  11.6 us
    ppermute x6, starting transfers between devices, tensor_swap(): return lax.ppermute(v, 'tensor', [(t, t ^ d) for t in range(tensors)])  10.7 us
    ppermute x6, waiting for transfers between devices, tensor_swap(): return lax.ppermute(v, 'tensor', [(t, t ^ d) for t in range(tensors)])  8.55 us
    pallas_call x1, Pallas kernels, fill(): pl.pallas_call(functools.partial(fill_kernel, kb, count, depth, order), o...  7 us
    ppermute x9, waiting for transfers between devices, chip_swap(): lax.ppermute(v, 'replica', [(r, r ^ s * cores) for r in range(replicas)])  5.82 us
    ppermute x14, starting transfers between devices, core_swap(): return lax.ppermute(v, 'replica', [(r, r ^ 1) for r in range(replicas)])  2.39 us
  transfers between devices with their start and end apart: 29, of which 6 were waited for; matrix products, arithmetic and copies ran while one was open for 0% of the time, Pallas kernels for 55%

profile of v2, /device:TPU:0, one launch (start us, length us, event | category | flops | bytes accessed | tf_op | source)
XLA Modules:
  0.0 91.4 jit_solution(12846046037763627056)
XLA Ops:
  0.0 2.9 %collective-permute-start.1 = (bf16[32,2048]{1,0:T(8,128)(2,1)}, bf16[32,2048]{1,0:T(8,128)(2,1)S(1)}, u32[]{:S(2)}, u32[]{:S(2)}) collective-permute-start(bf16[32,2048]{1,0:T(8,128)(2,1)} %refs_0_.2), channel_id=1, source_target_pairs={{0,8},{4,12},{8,0},{12,4},{1,9},{5,13},{9,1},{13,5},{2,10},{6,14},... | collective-permute-start | bytes 393224 | tf_op jit(solution)/shard_map/ppermute | solution.py:501
  2.9 1.6 %collective-permute-start.11 = (bf16[32,2048]{1,0:T(8,128)(2,1)}, bf16[32,2048]{1,0:T(8,128)(2,1)S(1)}, u32[]{:S(2)}, u32[]{:S(2)}) collective-permute-start(bf16[32,2048]{1,0:T(8,128)(2,1)} %refs_0_.2), channel_id=1, source_target_pairs={{0,1},{1,0},{2,3},{3,2},{4,5},{5,4},{6,7},{7,6},{8,9},{9,8},{10,11... | collective-permute-start | bytes 393224 | tf_op jit(solution)/shard_map/ppermute | solution.py:504
  4.5 0.1 pad_add_fusion.where
  4.6 7.0 %fill.1 = (bf16[4,512,2048]{2,1,0:T(8,128)(2,1)S(1)}, bf16[4,512,2048]{2,1,0:T(8,128)(2,1)S(1)}, f32[64,2048]{1,0:T(8,128)S(1)}, f32[64,2048]{1,0:T(8,128)S(1)},...) custom-call(s32[2]{0:T(128)S(1)} %pad_add_fusion.where, s32[1,8]{1,0:T(1,128)} %bitcast.9, ...), custom_call_target="tpu_custom_call" | custom-call | bytes 16777216 | tf_op jit(solution)/shard_map/fill/pallas_call | solution.py:90
  11.6 0.1 collective-permute-start.2
  11.7 0.0 collective-permute-done.1.refs_1_
  11.7 0.5 collective-permute-start.3
  12.2 2.5 %collective-permute-start.7 = (bf16[32,2048]{1,0:T(8,128)(2,1)S(1)}, bf16[32,2048]{1,0:T(8,128)(2,1)S(1)}, u32[]{:S(2)}, u32[]{:S(2)}) collective-permute-start(bf16[32,2048]{1,0:T(8,128)(2,1)S(1)} %copy-done.2), channel_id=1, source_target_pairs={{0,3},{1,2},{2,1},{3,0},{4,7},{5,6},{6,5},{7,4},{8,11},{9,10},{10,... | collective-permute-start | bytes 393224 | tf_op jit(solution)/shard_map/ppermute | solution.py:504
  14.7 0.1 collective-permute-start
  14.8 0.0 collective-permute-done.11.refs_0_
  14.8 0.0 collective-permute-start.13
  14.8 0.6 collective-permute-start.12
  15.4 7.3 %gate_up.4 = (f32[128,2048]{1,0:T(8,128)S(1)}, f32[128,2048]{1,0:T(8,128)S(1)}, bf16[4,512,2048]{2,1,0:T(8,128)(2,1)S(1)}, bf16[4,512,2048]{2,1,0:T(8,128)(2,1)S(1)}) custom-call(s32[2]{0:T(128)S(1)} %pad_add_fusion.where, bf16[32,2048]{1,0:T(8,128)(2,1)S(1)} %copy-done.2, bf16[32,2048]{1,0:T(8,128)(2,1)S(1)} %collective-permute-done.1.refs_1_, ...), custom_call_target="tpu_custom_call" | custom-call | flops 2147483648 | bytes 16777216 | tf_op jit(solution)/shard_map/gate_up/pallas_call | solution.py:236
  22.7 1.6 %collective-permute-start.8 = (bf16[32,2048]{1,0:T(8,128)(2,1)S(1)}, bf16[32,2048]{1,0:T(8,128)(2,1)S(1)}, u32[]{:S(2)}, u32[]{:S(2)}) collective-permute-start(bf16[32,2048]{1,0:T(8,128)(2,1)S(1)} %collective-permute-done.7.refs_0_), channel_id=1, source_target_pairs={{0,8},{4,12},{8,0},{12,4},{1,9},{5,13},{9,1},{13,5},{2,10},{6,14},... | collective-permute-start | bytes 393224 | tf_op jit(solution)/shard_map/ppermute | solution.py:501
  24.3 2.7 %collective-permute-done.refs_0_ = bf16[32,2048]{1,0:T(8,128)(2,1)S(1)} collective-permute-done((bf16[32,2048]{1,0:T(8,128)(2,1)S(1)}, bf16[32,2048]{1,0:T(8,128)(2,1)S(1)}, u32[]{:S(2)}, u32[]{:S(2)}) %collective-permute-start) | collective-permute-done | bytes 131104 | tf_op jit(solution)/shard_map/ppermute | solution.py:504
  27.0 0.5 collective-permute-start.4
  27.5 0.2 collective-permute-start.9
  27.7 0.6 collective-permute-done.8.refs_1_
  28.4 7.3 %gate_up.5 = (f32[128,2048]{1,0:T(8,128)S(1)}, f32[128,2048]{1,0:T(8,128)S(1)}, bf16[4,512,2048]{2,1,0:T(8,128)(2,1)S(1)}, bf16[4,512,2048]{2,1,0:T(8,128)(2,1)S(1)}) custom-call(s32[2]{0:T(128)S(1)} %pad_add_fusion.where, bf16[32,2048]{1,0:T(8,128)(2,1)S(1)} %collective-permute-done.11.refs_0_, bf16[32,2048]{1,0:T(8,128)(2,1)S(1)} %collective-permute-done.12.refs_1_, ...), custom_call_target="tpu_custom_call" | custom-call | flops 2147483648 | bytes 16777216 | tf_op jit(solution)/shard_map/gate_up/pallas_call | solution.py:236
  35.7 1.6 %collective-permute-start.17 = (bf16[128,2048]{1,0:T(8,128)(2,1)S(1)}, bf16[128,2048]{1,0:T(8,128)(2,1)S(1)}, u32[]{:S(2)}, u32[]{:S(2)}) collective-permute-start(bf16[128,2048]{1,0:T(8,128)(2,1)S(1)} %bitcast.6), channel_id=1, source_target_pairs={{0,8},{4,12},{8,0},{12,4},{1,9},{5,13},{9,1},{13,5},{2,10},{6,14},... | collective-permute-start | bytes 1572872 | tf_op jit(solution)/shard_map/ppermute | solution.py:501
  37.3 0.2 collective-permute-start.6
  37.5 7.3 %gate_up.6 = (f32[128,2048]{1,0:T(8,128)S(1)}, f32[128,2048]{1,0:T(8,128)S(1)}, bf16[4,512,2048]{2,1,0:T(8,128)(2,1)S(1)}, bf16[4,512,2048]{2,1,0:T(8,128)(2,1)S(1)}) custom-call(s32[2]{0:T(128)S(1)} %pad_add_fusion.where, bf16[32,2048]{1,0:T(8,128)(2,1)S(1)} %collective-permute-done.7.refs_0_, bf16[32,2048]{1,0:T(8,128)(2,1)S(1)} %collective-permute-done.8.refs_1_, ...), custom_call_target="tpu_custom_call" | custom-call | flops 2147483648 | bytes 16777216 | tf_op jit(solution)/shard_map/gate_up/pallas_call | solution.py:236
  44.8 0.0 copy-start
  44.8 5.5 %gate_up.7 = (bf16[128,2048]{1,0:T(8,128)(2,1)S(1)}, bf16[4,512,2048]{2,1,0:T(8,128)(2,1)S(1)}) custom-call(s32[2]{0:T(128)S(1)} %pad_add_fusion.where, bf16[32,2048]{1,0:T(8,128)(2,1)S(1)} %collective-permute-done.refs_0_, bf16[32,2048]{1,0:T(8,128)(2,1)S(1)} %collective-permute-done.4.refs_1_, bf16[32,2048]{1,0:T(8,128)(2,1)S(1)} %collective-permute-done.5.refs_2_, ...), custom_call_target="tpu_custom_call" | custom-call | flops 2147483648 | bytes 16777216 | tf_op jit(solution)/shard_map/gate_up/pallas_call | solution.py:236
  50.3 4.6 %down.4 = (f32[64,2560]{1,0:T(8,128)S(1)}, bf16[64,2560]{1,0:T(8,128)(2,1)S(1)}, bf16[4,512,2048]{2,1,0:T(8,128)(2,1)S(1)}) custom-call(s32[2]{0:T(128)S(1)} %pad_add_fusion.where, bf16[128,2048]{1,0:T(8,128)(2,1)S(1)} %get-tuple-element.95.hidden, bf16[2048,8192]{1,0:T(8,128)(2,1)} %dl.7, f32[16,8192]{1,0:T(8,128)S(1)} %get-tuple-element.80.ds, ...), custom_call_target="tpu_custom_call" | custom-call | flops 1073741824 | bytes 8388608 | tf_op jit(solution)/shard_map/down/pallas_call | solution.py:313
  54.9 0.4 collective-permute-start.15
  55.3 4.1 %down.5 = (f32[64,2048]{1,0:T(8,128)S(1)}, bf16[64,2048]{1,0:T(8,128)(2,1)S(1)}, bf16[4,512,2048]{2,1,0:T(8,128)(2,1)S(1)}) custom-call(s32[2]{0:T(128)S(1)} %pad_add_fusion.where, bf16[128,2048]{1,0:T(8,128)(2,1)S(1)} %get-tuple-element.95.hidden, bf16[2048,8192]{1,0:T(8,128)(2,1)} %dl.7, f32[16,8192]{1,0:T(8,128)S(1)} %get-tuple-element.80.ds, ...), custom_call_target="tpu_custom_call" | custom-call | flops 1073741824 | bytes 8388608 | tf_op jit(solution)/shard_map/down/pallas_call | solution.py:313
  59.4 0.3 collective-permute-start.20
  59.7 0.1 pair.4
  59.7 0.6 collective-permute-start.16
  60.4 0.0 collective-permute-start.18
  60.4 4.1 %down.6 = (f32[64,2048]{1,0:T(8,128)S(1)}, bf16[64,2048]{1,0:T(8,128)(2,1)S(1)}, bf16[4,512,2048]{2,1,0:T(8,128)(2,1)S(1)}) custom-call(s32[2]{0:T(128)S(1)} %pad_add_fusion.where, bf16[128,2048]{1,0:T(8,128)(2,1)S(1)} %get-tuple-element.95.hidden, bf16[2048,8192]{1,0:T(8,128)(2,1)} %dl.7, f32[16,8192]{1,0:T(8,128)S(1)} %get-tuple-element.80.ds, ...), custom_call_target="tpu_custom_call" | custom-call | flops 1073741824 | bytes 8388608 | tf_op jit(solution)/shard_map/down/pallas_call | solution.py:313
  64.5 0.6 collective-permute-start.26
  65.1 0.1 collective-permute-start.19
  65.2 1.0 %collective-permute-done.16.refs_1_ = bf16[32,2560]{1,0:T(8,128)(2,1)S(1)} collective-permute-done((bf16[32,2560]{1,0:T(8,128)(2,1)S(1)}, bf16[32,2560]{1,0:T(8,128)(2,1)S(1)}, u32[]{:S(2)}, u32[]{:S(2)}) %collective-permute-start.16) | collective-permute-done | bytes 163872 | tf_op jit(solution)/shard_map/ppermute | solution.py:501
  66.2 0.2 message.1
  66.4 2.6 %down.7 = (f32[64,2048]{1,0:T(8,128)S(1)}, bf16[64,2048]{1,0:T(8,128)(2,1)S(1)}) custom-call(s32[2]{0:T(128)S(1)} %pad_add_fusion.where, bf16[128,2048]{1,0:T(8,128)(2,1)S(1)} %get-tuple-element.95.hidden, bf16[2048,8192]{1,0:T(8,128)(2,1)} %dl.7, f32[16,8192]{1,0:T(8,128)S(1)} %get-tuple-element.80.ds, bf16[4,512,2048]{2,1,0:T(8,128)(2,1)S(1)} %get-tuple-element.97.d_held), custom_call_target="tpu_custom_call" | custom-call | flops 1073741824 | bytes 8388608 | tf_op jit(solution)/shard_map/down/pallas_call | solution.py:313
  69.0 0.1 collective-permute-start.21
  69.1 0.9 collective-permute-start.24
  70.0 1.3 %collective-permute-start.27 = (bf16[32,2048]{1,0:T(8,128)(2,1)S(1)}, bf16[32,2048]{1,0:T(8,128)(2,1)S(1)}, u32[]{:S(2)}, u32[]{:S(2)}) collective-permute-start(bf16[32,2048]{1,0:T(8,128)(2,1)S(1)} %get-tuple-element.106), channel_id=1, source_target_pairs={{0,8},{4,12},{8,0},{12,4},{1,9},{5,13},{9,1},{13,5},{2,10},{6,14},... | collective-permute-start | bytes 393224 | tf_op jit(solution)/shard_map/ppermute | solution.py:501
  71.3 4.2 %collective-permute-done.24.refs_1_ = bf16[32,2048]{1,0:T(8,128)(2,1)S(1)} collective-permute-done((bf16[32,2048]{1,0:T(8,128)(2,1)S(1)}, bf16[32,2048]{1,0:T(8,128)(2,1)S(1)}, u32[]{:S(2)}, u32[]{:S(2)}) %collective-permute-start.24) | collective-permute-done | bytes 131104 | tf_op jit(solution)/shard_map/ppermute | solution.py:501
  75.4 4.0 %collective-permute-start.23 = (bf16[32,2176]{1,0:T(8,128)(2,1)S(1)}, bf16[32,2176]{1,0:T(8,128)(2,1)S(1)}, u32[]{:S(2)}, u32[]{:S(2)}) collective-permute-start(bf16[32,2176]{1,0:T(8,128)(2,1)S(1)} %get-tuple-element.93), channel_id=1, source_target_pairs={{0,2},{1,3},{2,0},{3,1},{4,6},{5,7},{6,4},{7,5},{8,10},{9,11},{10,... | collective-permute-start | bytes 417800 | tf_op jit(solution)/shard_map/ppermute | solution.py:504
  79.5 1.2 %collective-permute-start.25 = (bf16[32,2176]{1,0:T(8,128)(2,1)S(1)}, bf16[32,2176]{1,0:T(8,128)(2,1)S(1)}, u32[]{:S(2)}, u32[]{:S(2)}) collective-permute-start(bf16[32,2176]{1,0:T(8,128)(2,1)S(1)} %attach.2), channel_id=1, source_target_pairs={{0,3},{1,2},{2,1},{3,0},{4,7},{5,6},{6,5},{7,4},{8,11},{9,10},{10,... | collective-permute-start | bytes 417800 | tf_op jit(solution)/shard_map/ppermute | solution.py:504
  80.7 1.3 %collective-permute-start.28 = (bf16[32,2176]{1,0:T(8,128)(2,1)S(1)}, bf16[32,2176]{1,0:T(8,128)(2,1)S(1)}, u32[]{:S(2)}, u32[]{:S(2)}) collective-permute-start(bf16[32,2176]{1,0:T(8,128)(2,1)S(1)} %attach.3), channel_id=1, source_target_pairs={{0,1},{1,0},{2,3},{3,2},{4,5},{5,4},{6,7},{7,6},{8,9},{9,8},{10,11... | collective-permute-start | bytes 417800 | tf_op jit(solution)/shard_map/ppermute | solution.py:504
  82.1 1.6 %collective-permute-start.22 = (bf16[32,2048]{1,0:T(8,128)(2,1)S(1)}, bf16[32,2048]{1,0:T(8,128)(2,1)S(1)}, u32[]{:S(2)}, u32[]{:S(2)}) collective-permute-start(bf16[32,2048]{1,0:T(8,128)(2,1)S(1)} %get-tuple-element.101), channel_id=1, source_target_pairs={{0,8},{4,12},{8,0},{12,4},{1,9},{5,13},{9,1},{13,5},{2,10},{6,14},... | collective-permute-start | bytes 393224 | tf_op jit(solution)/shard_map/ppermute | solution.py:501
  83.7 5.1 %collective-permute-done.23.refs_6_ = bf16[32,2176]{1,0:T(8,128)(2,1)S(1)} collective-permute-done((bf16[32,2176]{1,0:T(8,128)(2,1)S(1)}, bf16[32,2176]{1,0:T(8,128)(2,1)S(1)}, u32[]{:S(2)}, u32[]{:S(2)}) %collective-permute-start.23) | collective-permute-done | bytes 139296 | tf_op jit(solution)/shard_map/ppermute | solution.py:504
  88.8 0.8 collective-permute-done.28.refs_8_
  89.6 1.8 %final.1 = bf16[32,2048]{1,0:T(8,128)(2,1)} custom-call(s32[2]{0:T(128)S(1)} %pad_add_fusion.where, s32[32,1]{1,0:T(8,128)S(1)} %get-tuple-element.56.pool_row, bf16[32,128]{1,0:T(8,128)(2,1)S(1)} %get-tuple-element.86.low, bf16[128,2048]{1,0:T(8,128)(2,1)S(1)} %bitcast.8, bf16[128,2048]{1,0:T(8,128)(2,1)S(1)} %collective-permute-done.17.refs_1_, ...), custom_call_target="tpu_custom_call" | custom-call | tf_op jit(solution)/shard_map/final/pallas_call | solution.py:458
  (34 shorter events, 0.3 us)
Async XLA Ops:
  0.0 11.7 %collective-permute-start.1 = (bf16[32,2048]{1,0:T(8,128)(2,1)}, bf16[32,2048]{1,0:T(8,128)(2,1)S(1)}, u32[]{:S(2)}, u32[]{:S(2)}) collective-permute-start(bf16[32,2048]{1,0:T(8,128)(2,1)} %refs_0_.2), channel_id=1, source_target_pairs={{0,8},{4,12},{8,0},{12,4},{1,9},{5,13},{9,1},{13,5},{2,10},{6,14},... | collective-permute-start | bytes 393224 | tf_op jit(solution)/shard_map/ppermute | solution.py:501
  2.9 11.8 %collective-permute-start.11 = (bf16[32,2048]{1,0:T(8,128)(2,1)}, bf16[32,2048]{1,0:T(8,128)(2,1)S(1)}, u32[]{:S(2)}, u32[]{:S(2)}) collective-permute-start(bf16[32,2048]{1,0:T(8,128)(2,1)} %refs_0_.2), channel_id=1, source_target_pairs={{0,1},{1,0},{2,3},{3,2},{4,5},{5,4},{6,7},{7,6},{8,9},{9,8},{10,11... | collective-permute-start | bytes 393224 | tf_op jit(solution)/shard_map/ppermute | solution.py:504
  4.6 7.0 %copy-start.2 = (bf16[32,2048]{1,0:T(8,128)(2,1)S(1)}, bf16[32,2048]{1,0:T(8,128)(2,1)}, u32[]{:S(2)}) copy-start(bf16[32,2048]{1,0:T(8,128)(2,1)} %refs_0_.2) | copy-start | bytes 393220
  11.6 3.2 %collective-permute-start.2 = (bf16[32,2048]{1,0:T(8,128)(2,1)S(1)}, bf16[32,2048]{1,0:T(8,128)(2,1)S(1)}, u32[]{:S(2)}, u32[]{:S(2)}) collective-permute-start(bf16[32,2048]{1,0:T(8,128)(2,1)S(1)} %copy-done.2), channel_id=1, source_target_pairs={{0,4},{4,0},{8,12},{12,8},{1,5},{5,1},{9,13},{13,9},{2,6},{6,2},{1... | collective-permute-start | bytes 393224 | tf_op jit(solution)/shard_map/ppermute | solution.py:498
  11.7 3.7 %collective-permute-start.3 = (bf16[32,2048]{1,0:T(8,128)(2,1)S(1)}, bf16[32,2048]{1,0:T(8,128)(2,1)S(1)}, u32[]{:S(2)}, u32[]{:S(2)}) collective-permute-start(bf16[32,2048]{1,0:T(8,128)(2,1)S(1)} %collective-permute-done.1.refs_1_), channel_id=1, source_target_pairs={{0,4},{4,0},{8,12},{12,8},{1,5},{5,1},{9,13},{13,9},{2,6},{6,2},{1... | collective-permute-start | bytes 393224 | tf_op jit(solution)/shard_map/ppermute | solution.py:498
  12.2 10.5 %collective-permute-start.7 = (bf16[32,2048]{1,0:T(8,128)(2,1)S(1)}, bf16[32,2048]{1,0:T(8,128)(2,1)S(1)}, u32[]{:S(2)}, u32[]{:S(2)}) collective-permute-start(bf16[32,2048]{1,0:T(8,128)(2,1)S(1)} %copy-done.2), channel_id=1, source_target_pairs={{0,3},{1,2},{2,1},{3,0},{4,7},{5,6},{6,5},{7,4},{8,11},{9,10},{10,... | collective-permute-start | bytes 393224 | tf_op jit(solution)/shard_map/ppermute | solution.py:504
  14.7 12.3 %collective-permute-start = (bf16[32,2048]{1,0:T(8,128)(2,1)S(1)}, bf16[32,2048]{1,0:T(8,128)(2,1)S(1)}, u32[]{:S(2)}, u32[]{:S(2)}) collective-permute-start(bf16[32,2048]{1,0:T(8,128)(2,1)S(1)} %copy-done.2), channel_id=1, source_target_pairs={{0,2},{1,3},{2,0},{3,1},{4,6},{5,7},{6,4},{7,5},{8,10},{9,11},{10,... | collective-permute-start | bytes 393224 | tf_op jit(solution)/shard_map/ppermute | solution.py:504
  14.8 12.7 %collective-permute-start.13 = (bf16[32,2048]{1,0:T(8,128)(2,1)S(1)}, bf16[32,2048]{1,0:T(8,128)(2,1)S(1)}, u32[]{:S(2)}, u32[]{:S(2)}) collective-permute-start(bf16[32,2048]{1,0:T(8,128)(2,1)S(1)} %collective-permute-done.11.refs_0_), channel_id=1, source_target_pairs={{0,4},{4,0},{8,12},{12,8},{1,5},{5,1},{9,13},{13,9},{2,6},{6,2},{1... | collective-permute-start | bytes 393224 | tf_op jit(solution)/shard_map/ppermute | solution.py:498
  14.8 9.5 %collective-permute-start.12 = (bf16[32,2048]{1,0:T(8,128)(2,1)S(1)}, bf16[32,2048]{1,0:T(8,128)(2,1)S(1)}, u32[]{:S(2)}, u32[]{:S(2)}) collective-permute-start(bf16[32,2048]{1,0:T(8,128)(2,1)S(1)} %collective-permute-done.11.refs_0_), channel_id=1, source_target_pairs={{0,8},{4,12},{8,0},{12,4},{1,9},{5,13},{9,1},{13,5},{2,10},{6,14},... | collective-permute-start | bytes 393224 | tf_op jit(solution)/shard_map/ppermute | solution.py:501
  22.7 5.6 %collective-permute-start.8 = (bf16[32,2048]{1,0:T(8,128)(2,1)S(1)}, bf16[32,2048]{1,0:T(8,128)(2,1)S(1)}, u32[]{:S(2)}, u32[]{:S(2)}) collective-permute-start(bf16[32,2048]{1,0:T(8,128)(2,1)S(1)} %collective-permute-done.7.refs_0_), channel_id=1, source_target_pairs={{0,8},{4,12},{8,0},{12,4},{1,9},{5,13},{9,1},{13,5},{2,10},{6,14},... | collective-permute-start | bytes 393224 | tf_op jit(solution)/shard_map/ppermute | solution.py:501
  24.3 4.1 %collective-permute-start.14 = (bf16[32,2048]{1,0:T(8,128)(2,1)S(1)}, bf16[32,2048]{1,0:T(8,128)(2,1)S(1)}, u32[]{:S(2)}, u32[]{:S(2)}) collective-permute-start(bf16[32,2048]{1,0:T(8,128)(2,1)S(1)} %collective-permute-done.12.refs_1_), channel_id=1, source_target_pairs={{0,4},{4,0},{8,12},{12,8},{1,5},{5,1},{9,13},{13,9},{2,6},{6,2},{1... | collective-permute-start | bytes 393224 | tf_op jit(solution)/shard_map/ppermute | solution.py:498
  26.9 17.9 %collective-permute-start.5 = (bf16[32,2048]{1,0:T(8,128)(2,1)S(1)}, bf16[32,2048]{1,0:T(8,128)(2,1)S(1)}, u32[]{:S(2)}, u32[]{:S(2)}) collective-permute-start(bf16[32,2048]{1,0:T(8,128)(2,1)S(1)} %collective-permute-done.refs_0_), channel_id=1, source_target_pairs={{0,4},{4,0},{8,12},{12,8},{1,5},{5,1},{9,13},{13,9},{2,6},{6,2},{1... | collective-permute-start | bytes 393224 | tf_op jit(solution)/shard_map/ppermute | solution.py:498
  27.0 10.3 %collective-permute-start.4 = (bf16[32,2048]{1,0:T(8,128)(2,1)S(1)}, bf16[32,2048]{1,0:T(8,128)(2,1)S(1)}, u32[]{:S(2)}, u32[]{:S(2)}) collective-permute-start(bf16[32,2048]{1,0:T(8,128)(2,1)S(1)} %collective-permute-done.refs_0_), channel_id=1, source_target_pairs={{0,8},{4,12},{8,0},{12,4},{1,9},{5,13},{9,1},{13,5},{2,10},{6,14},... | collective-permute-start | bytes 393224 | tf_op jit(solution)/shard_map/ppermute | solution.py:501
  27.5 10.0 %collective-permute-start.9 = (bf16[32,2048]{1,0:T(8,128)(2,1)S(1)}, bf16[32,2048]{1,0:T(8,128)(2,1)S(1)}, u32[]{:S(2)}, u32[]{:S(2)}) collective-permute-start(bf16[32,2048]{1,0:T(8,128)(2,1)S(1)} %collective-permute-done.7.refs_0_), channel_id=1, source_target_pairs={{0,4},{4,0},{8,12},{12,8},{1,5},{5,1},{9,13},{13,9},{2,6},{6,2},{1... | collective-permute-start | bytes 393224 | tf_op jit(solution)/shard_map/ppermute | solution.py:498
  28.4 9.1 %collective-permute-start.10 = (bf16[32,2048]{1,0:T(8,128)(2,1)S(1)}, bf16[32,2048]{1,0:T(8,128)(2,1)S(1)}, u32[]{:S(2)}, u32[]{:S(2)}) collective-permute-start(bf16[32,2048]{1,0:T(8,128)(2,1)S(1)} %collective-permute-done.8.refs_1_), channel_id=1, source_target_pairs={{0,4},{4,0},{8,12},{12,8},{1,5},{5,1},{9,13},{13,9},{2,6},{6,2},{1... | collective-permute-start | bytes 393224 | tf_op jit(solution)/shard_map/ppermute | solution.py:498
  28.4 7.3 %copy-start.1 = (bf16[2,64,2048]{2,1,0:T(8,128)(2,1)S(1)}, bf16[2,64,2048]{2,1,0:T(8,128)(2,1)}, u32[]{:S(2)}) copy-start(bf16[2,64,2048]{2,1,0:T(8,128)(2,1)} %param.24) | copy-start | bytes 1572868
  35.7 29.3 %collective-permute-start.17 = (bf16[128,2048]{1,0:T(8,128)(2,1)S(1)}, bf16[128,2048]{1,0:T(8,128)(2,1)S(1)}, u32[]{:S(2)}, u32[]{:S(2)}) collective-permute-start(bf16[128,2048]{1,0:T(8,128)(2,1)S(1)} %bitcast.6), channel_id=1, source_target_pairs={{0,8},{4,12},{8,0},{12,4},{1,9},{5,13},{9,1},{13,5},{2,10},{6,14},... | collective-permute-start | bytes 1572872 | tf_op jit(solution)/shard_map/ppermute | solution.py:501
  37.3 7.6 %collective-permute-start.6 = (bf16[32,2048]{1,0:T(8,128)(2,1)S(1)}, bf16[32,2048]{1,0:T(8,128)(2,1)S(1)}, u32[]{:S(2)}, u32[]{:S(2)}) collective-permute-start(bf16[32,2048]{1,0:T(8,128)(2,1)S(1)} %collective-permute-done.4.refs_1_), channel_id=1, source_target_pairs={{0,4},{4,0},{8,12},{12,8},{1,5},{5,1},{9,13},{13,9},{2,6},{6,2},{1... | collective-permute-start | bytes 393224 | tf_op jit(solution)/shard_map/ppermute | solution.py:498
  44.8 5.5 %copy-start = (bf16[2048,512]{1,0:T(8,128)(2,1)S(1)}, bf16[2048,512]{1,0:T(8,128)(2,1)}, u32[]{:S(2)}) copy-start(bf16[2048,512]{1,0:T(8,128)(2,1)} %refs_0_.3) | copy-start | bytes 6291460
  54.9 4.8 %collective-permute-start.15 = (bf16[64,2560]{1,0:T(8,128)(2,1)S(1)}, bf16[64,2560]{1,0:T(8,128)(2,1)S(1)}, u32[]{:S(2)}, u32[]{:S(2)}) collective-permute-start(bf16[64,2560]{1,0:T(8,128)(2,1)S(1)} %get-tuple-element.83), channel_id=1, source_target_pairs={{0,4},{4,0},{8,12},{12,8},{1,5},{5,1},{9,13},{13,9},{2,6},{6,2},{1... | collective-permute-start | bytes 983048 | tf_op jit(solution)/shard_map/ppermute | solution.py:498
  59.4 5.7 %collective-permute-start.20 = (bf16[64,2048]{1,0:T(8,128)(2,1)S(1)}, bf16[64,2048]{1,0:T(8,128)(2,1)S(1)}, u32[]{:S(2)}, u32[]{:S(2)}) collective-permute-start(bf16[64,2048]{1,0:T(8,128)(2,1)S(1)} %get-tuple-element.90), channel_id=1, source_target_pairs={{0,4},{4,0},{8,12},{12,8},{1,5},{5,1},{9,13},{13,9},{2,6},{6,2},{1... | collective-permute-start | bytes 786440 | tf_op jit(solution)/shard_map/ppermute | solution.py:498
  59.7 6.5 %collective-permute-start.16 = (bf16[32,2560]{1,0:T(8,128)(2,1)S(1)}, bf16[32,2560]{1,0:T(8,128)(2,1)S(1)}, u32[]{:S(2)}, u32[]{:S(2)}) collective-permute-start(bf16[32,2560]{1,0:T(8,128)(2,1)S(1)} %get-tuple-element.85), channel_id=1, source_target_pairs={{0,8},{4,12},{8,0},{12,4},{1,9},{5,13},{9,1},{13,5},{2,10},{6,14},... | collective-permute-start | bytes 491528 | tf_op jit(solution)/shard_map/ppermute | solution.py:501
  60.4 21.7 %collective-permute-start.18 = (bf16[128,2048]{1,0:T(8,128)(2,1)S(1)}, bf16[128,2048]{1,0:T(8,128)(2,1)S(1)}, u32[]{:S(2)}, u32[]{:S(2)}) collective-permute-start(bf16[128,2048]{1,0:T(8,128)(2,1)S(1)} %bitcast.7), channel_id=1, source_target_pairs={{0,4},{4,0},{8,12},{12,8},{1,5},{5,1},{9,13},{13,9},{2,6},{6,2},{1... | collective-permute-start | bytes 1572872 | tf_op jit(solution)/shard_map/ppermute | solution.py:498
  64.5 5.5 %collective-permute-start.26 = (bf16[64,2048]{1,0:T(8,128)(2,1)S(1)}, bf16[64,2048]{1,0:T(8,128)(2,1)S(1)}, u32[]{:S(2)}, u32[]{:S(2)}) collective-permute-start(bf16[64,2048]{1,0:T(8,128)(2,1)S(1)} %get-tuple-element.104), channel_id=1, source_target_pairs={{0,4},{4,0},{8,12},{12,8},{1,5},{5,1},{9,13},{13,9},{2,6},{6,2},{1... | collective-permute-start | bytes 786440 | tf_op jit(solution)/shard_map/ppermute | solution.py:498
  65.1 24.6 %collective-permute-start.19 = (bf16[128,2048]{1,0:T(8,128)(2,1)S(1)}, bf16[128,2048]{1,0:T(8,128)(2,1)S(1)}, u32[]{:S(2)}, u32[]{:S(2)}) collective-permute-start(bf16[128,2048]{1,0:T(8,128)(2,1)S(1)} %collective-permute-done.17.refs_1_), channel_id=1, source_target_pairs={{0,4},{4,0},{8,12},{12,8},{1,5},{5,1},{9,13},{13,9},{2,6},{6,2},{1... | collective-permute-start | bytes 1572872 | tf_op jit(solution)/shard_map/ppermute | solution.py:498
  69.0 11.8 %collective-permute-start.21 = (bf16[64,2048]{1,0:T(8,128)(2,1)S(1)}, bf16[64,2048]{1,0:T(8,128)(2,1)S(1)}, u32[]{:S(2)}, u32[]{:S(2)}) collective-permute-start(bf16[64,2048]{1,0:T(8,128)(2,1)S(1)} %get-tuple-element.99), channel_id=1, source_target_pairs={{0,4},{4,0},{8,12},{12,8},{1,5},{5,1},{9,13},{13,9},{2,6},{6,2},{1... | collective-permute-start | bytes 786440 | tf_op jit(solution)/shard_map/ppermute | solution.py:498
  69.1 6.4 %collective-permute-start.24 = (bf16[32,2048]{1,0:T(8,128)(2,1)S(1)}, bf16[32,2048]{1,0:T(8,128)(2,1)S(1)}, u32[]{:S(2)}, u32[]{:S(2)}) collective-permute-start(bf16[32,2048]{1,0:T(8,128)(2,1)S(1)} %get-tuple-element.91), channel_id=1, source_target_pairs={{0,8},{4,12},{8,0},{12,4},{1,9},{5,13},{9,1},{13,5},{2,10},{6,14},... | collective-permute-start | bytes 393224 | tf_op jit(solution)/shard_map/ppermute | solution.py:501
  70.0 9.4 %collective-permute-start.27 = (bf16[32,2048]{1,0:T(8,128)(2,1)S(1)}, bf16[32,2048]{1,0:T(8,128)(2,1)S(1)}, u32[]{:S(2)}, u32[]{:S(2)}) collective-permute-start(bf16[32,2048]{1,0:T(8,128)(2,1)S(1)} %get-tuple-element.106), channel_id=1, source_target_pairs={{0,8},{4,12},{8,0},{12,4},{1,9},{5,13},{9,1},{13,5},{2,10},{6,14},... | collective-permute-start | bytes 393224 | tf_op jit(solution)/shard_map/ppermute | solution.py:501
  75.4 13.4 %collective-permute-start.23 = (bf16[32,2176]{1,0:T(8,128)(2,1)S(1)}, bf16[32,2176]{1,0:T(8,128)(2,1)S(1)}, u32[]{:S(2)}, u32[]{:S(2)}) collective-permute-start(bf16[32,2176]{1,0:T(8,128)(2,1)S(1)} %get-tuple-element.93), channel_id=1, source_target_pairs={{0,2},{1,3},{2,0},{3,1},{4,6},{5,7},{6,4},{7,5},{8,10},{9,11},{10,... | collective-permute-start | bytes 417800 | tf_op jit(solution)/shard_map/ppermute | solution.py:504
  79.5 9.4 %collective-permute-start.25 = (bf16[32,2176]{1,0:T(8,128)(2,1)S(1)}, bf16[32,2176]{1,0:T(8,128)(2,1)S(1)}, u32[]{:S(2)}, u32[]{:S(2)}) collective-permute-start(bf16[32,2176]{1,0:T(8,128)(2,1)S(1)} %attach.2), channel_id=1, source_target_pairs={{0,3},{1,2},{2,1},{3,0},{4,7},{5,6},{6,5},{7,4},{8,11},{9,10},{10,... | collective-permute-start | bytes 417800 | tf_op jit(solution)/shard_map/ppermute | solution.py:504
  80.7 8.9 %collective-permute-start.28 = (bf16[32,2176]{1,0:T(8,128)(2,1)S(1)}, bf16[32,2176]{1,0:T(8,128)(2,1)S(1)}, u32[]{:S(2)}, u32[]{:S(2)}) collective-permute-start(bf16[32,2176]{1,0:T(8,128)(2,1)S(1)} %attach.3), channel_id=1, source_target_pairs={{0,1},{1,0},{2,3},{3,2},{4,5},{5,4},{6,7},{7,6},{8,9},{9,8},{10,11... | collective-permute-start | bytes 417800 | tf_op jit(solution)/shard_map/ppermute | solution.py:504
  82.1 7.5 %collective-permute-start.22 = (bf16[32,2048]{1,0:T(8,128)(2,1)S(1)}, bf16[32,2048]{1,0:T(8,128)(2,1)S(1)}, u32[]{:S(2)}, u32[]{:S(2)}) collective-permute-start(bf16[32,2048]{1,0:T(8,128)(2,1)S(1)} %get-tuple-element.101), channel_id=1, source_target_pairs={{0,8},{4,12},{8,0},{12,4},{1,9},{5,13},{9,1},{13,5},{2,10},{6,14},... | collective-permute-start | bytes 393224 | tf_op jit(solution)/shard_map/ppermute | solution.py:501

commit v3 on v2

--- a/solution.py
+++ b/solution.py
@@ -609,7 +609,10 @@
         )
         mine, theirs = out[:2]
         carried = out[2] if more else None
-        own, *send = pair_sum(mine, core_swap(theirs), chips)
+        got = core_swap(theirs)
+        if not more:
+            got = after(got, *messages, received[0])
+        own, *send = pair_sum(mine, got, chips)
         sums.append(send[0])
         parts = [own] + [chip_swap(send[s - 1], s) for s in range(1, chips)]
         if n == 0:

time: 91.5 us -> 90.4 us (0.988)
    ppermute x9, waiting for transfers between devices: 5.82 us -> 4.47 us  [chip_swap(): lax.ppermute(v, 'replica', [(r, r ^ s * cores) for r in range(replicas)])]
  transfers between devices with their start and end apart: 29 -> 29, of which waited for: 6 -> 6; matrix products, arithmetic and copies ran while one was open for 0% -> 0% of each run, Pallas kernels for 55% -> 56%
where the time goes in v3:
time: 90.4 us; the launch traced here: 90.3 us
  Pallas kernels  52 us (58%)
  starting transfers between devices  24.3 us (27%)
  waiting for transfers between devices  13.7 us (15%)
    pallas_call x4, Pallas kernels, gate_up(): pl.pallas_call(functools.partial(gate_up_kernel, pieces, distances, comin...  27.4 us
    pallas_call x4, Pallas kernels, down(): pl.pallas_call(functools.partial(down_kernel, distances, kb, ahead, shrin...  15.4 us
    ppermute x9, starting transfers between devices, chip_swap(): lax.ppermute(v, 'replica', [(r, r ^ s * cores) for r in range(replicas)])  11.6 us
    ppermute x6, starting transfers between devices, tensor_swap(): return lax.ppermute(v, 'tensor', [(t, t ^ d) for t in range(tensors)])  10.1 us
    ppermute x6, waiting for transfers between devices, tensor_swap(): return lax.ppermute(v, 'tensor', [(t, t ^ d) for t in range(tensors)])  9.21 us
    pallas_call x1, Pallas kernels, fill(): pl.pallas_call(functools.partial(fill_kernel, kb, count, depth, order), o...  7 us
    ppermute x9, waiting for transfers between devices, chip_swap(): lax.ppermute(v, 'replica', [(r, r ^ s * cores) for r in range(replicas)])  4.47 us
    ppermute x14, starting transfers between devices, core_swap(): return lax.ppermute(v, 'replica', [(r, r ^ 1) for r in range(replicas)])  2.54 us
  transfers between devices with their start and end apart: 29, of which 6 were waited for; matrix products, arithmetic and copies ran while one was open for 0% of the time, Pallas kernels for 56%

profile of v3, /device:TPU:0, one launch (start us, length us, event | category | flops | bytes accessed | tf_op | source)
XLA Modules:
  0.0 90.3 jit_solution(3942595013596454960)
XLA Ops:
  0.0 2.9 %collective-permute-start.1 = (bf16[32,2048]{1,0:T(8,128)(2,1)}, bf16[32,2048]{1,0:T(8,128)(2,1)S(1)}, u32[]{:S(2)}, u32[]{:S(2)}) collective-permute-start(bf16[32,2048]{1,0:T(8,128)(2,1)} %refs_0_.2), channel_id=1, source_target_pairs={{0,8},{4,12},{8,0},{12,4},{1,9},{5,13},{9,1},{13,5},{2,10},{6,14},... | collective-permute-start | bytes 393224 | tf_op jit(solution)/shard_map/ppermute | solution.py:501
  2.9 1.6 %collective-permute-start.11 = (bf16[32,2048]{1,0:T(8,128)(2,1)}, bf16[32,2048]{1,0:T(8,128)(2,1)S(1)}, u32[]{:S(2)}, u32[]{:S(2)}) collective-permute-start(bf16[32,2048]{1,0:T(8,128)(2,1)} %refs_0_.2), channel_id=1, source_target_pairs={{0,1},{1,0},{2,3},{3,2},{4,5},{5,4},{6,7},{7,6},{8,9},{9,8},{10,11... | collective-permute-start | bytes 393224 | tf_op jit(solution)/shard_map/ppermute | solution.py:504
  4.5 0.1 pad_add_fusion.where
  4.6 7.0 %fill.1 = (bf16[4,512,2048]{2,1,0:T(8,128)(2,1)S(1)}, bf16[4,512,2048]{2,1,0:T(8,128)(2,1)S(1)}, f32[64,2048]{1,0:T(8,128)S(1)}, f32[64,2048]{1,0:T(8,128)S(1)},...) custom-call(s32[2]{0:T(128)S(1)} %pad_add_fusion.where, s32[1,8]{1,0:T(1,128)} %bitcast.9, ...), custom_call_target="tpu_custom_call" | custom-call | bytes 16777216 | tf_op jit(solution)/shard_map/fill/pallas_call | solution.py:90
  11.6 0.1 collective-permute-start.2
  11.7 0.5 collective-permute-start.3
  12.2 2.5 %collective-permute-start.7 = (bf16[32,2048]{1,0:T(8,128)(2,1)S(1)}, bf16[32,2048]{1,0:T(8,128)(2,1)S(1)}, u32[]{:S(2)}, u32[]{:S(2)}) collective-permute-start(bf16[32,2048]{1,0:T(8,128)(2,1)S(1)} %copy-done.2), channel_id=1, source_target_pairs={{0,3},{1,2},{2,1},{3,0},{4,7},{5,6},{6,5},{7,4},{8,11},{9,10},{10,... | collective-permute-start | bytes 393224 | tf_op jit(solution)/shard_map/ppermute | solution.py:504
  14.7 0.1 collective-permute-start
  14.8 0.0 collective-permute-done.11.refs_0_
  14.8 0.0 collective-permute-start.13
  14.8 0.6 collective-permute-start.12
  15.4 7.3 %gate_up.4 = (f32[128,2048]{1,0:T(8,128)S(1)}, f32[128,2048]{1,0:T(8,128)S(1)}, bf16[4,512,2048]{2,1,0:T(8,128)(2,1)S(1)}, bf16[4,512,2048]{2,1,0:T(8,128)(2,1)S(1)}) custom-call(s32[2]{0:T(128)S(1)} %pad_add_fusion.where, bf16[32,2048]{1,0:T(8,128)(2,1)S(1)} %copy-done.2, bf16[32,2048]{1,0:T(8,128)(2,1)S(1)} %collective-permute-done.1.refs_1_, ...), custom_call_target="tpu_custom_call" | custom-call | flops 2147483648 | bytes 16777216 | tf_op jit(solution)/shard_map/gate_up/pallas_call | solution.py:236
  22.7 0.0 collective-permute-done.7.refs_0_
  22.7 1.6 %collective-permute-start.8 = (bf16[32,2048]{1,0:T(8,128)(2,1)S(1)}, bf16[32,2048]{1,0:T(8,128)(2,1)S(1)}, u32[]{:S(2)}, u32[]{:S(2)}) collective-permute-start(bf16[32,2048]{1,0:T(8,128)(2,1)S(1)} %collective-permute-done.7.refs_0_), channel_id=1, source_target_pairs={{0,8},{4,12},{8,0},{12,4},{1,9},{5,13},{9,1},{13,5},{2,10},{6,14},... | collective-permute-start | bytes 393224 | tf_op jit(solution)/shard_map/ppermute | solution.py:501
  24.3 2.7 %collective-permute-done.refs_0_ = bf16[32,2048]{1,0:T(8,128)(2,1)S(1)} collective-permute-done((bf16[32,2048]{1,0:T(8,128)(2,1)S(1)}, bf16[32,2048]{1,0:T(8,128)(2,1)S(1)}, u32[]{:S(2)}, u32[]{:S(2)}) %collective-permute-start) | collective-permute-done | bytes 131104 | tf_op jit(solution)/shard_map/ppermute | solution.py:504
  27.0 0.5 collective-permute-start.4
  27.5 0.2 collective-permute-start.9
  27.7 0.6 collective-permute-done.8.refs_1_
  28.4 7.3 %gate_up.5 = (f32[128,2048]{1,0:T(8,128)S(1)}, f32[128,2048]{1,0:T(8,128)S(1)}, bf16[4,512,2048]{2,1,0:T(8,128)(2,1)S(1)}, bf16[4,512,2048]{2,1,0:T(8,128)(2,1)S(1)}) custom-call(s32[2]{0:T(128)S(1)} %pad_add_fusion.where, bf16[32,2048]{1,0:T(8,128)(2,1)S(1)} %collective-permute-done.11.refs_0_, bf16[32,2048]{1,0:T(8,128)(2,1)S(1)} %collective-permute-done.12.refs_1_, ...), custom_call_target="tpu_custom_call" | custom-call | flops 2147483648 | bytes 16777216 | tf_op jit(solution)/shard_map/gate_up/pallas_call | solution.py:236
  35.7 1.6 %collective-permute-start.17 = (bf16[128,2048]{1,0:T(8,128)(2,1)S(1)}, bf16[128,2048]{1,0:T(8,128)(2,1)S(1)}, u32[]{:S(2)}, u32[]{:S(2)}) collective-permute-start(bf16[128,2048]{1,0:T(8,128)(2,1)S(1)} %bitcast.6), channel_id=1, source_target_pairs={{0,8},{4,12},{8,0},{12,4},{1,9},{5,13},{9,1},{13,5},{2,10},{6,14},... | collective-permute-start | bytes 1572872 | tf_op jit(solution)/shard_map/ppermute | solution.py:501
  37.3 0.2 collective-permute-start.6
  37.5 7.3 %gate_up.6 = (f32[128,2048]{1,0:T(8,128)S(1)}, f32[128,2048]{1,0:T(8,128)S(1)}, bf16[4,512,2048]{2,1,0:T(8,128)(2,1)S(1)}, bf16[4,512,2048]{2,1,0:T(8,128)(2,1)S(1)}) custom-call(s32[2]{0:T(128)S(1)} %pad_add_fusion.where, bf16[32,2048]{1,0:T(8,128)(2,1)S(1)} %collective-permute-done.7.refs_0_, bf16[32,2048]{1,0:T(8,128)(2,1)S(1)} %collective-permute-done.8.refs_1_, ...), custom_call_target="tpu_custom_call" | custom-call | flops 2147483648 | bytes 16777216 | tf_op jit(solution)/shard_map/gate_up/pallas_call | solution.py:236
  44.8 0.0 copy-start
  44.8 5.5 %gate_up.7 = (bf16[128,2048]{1,0:T(8,128)(2,1)S(1)}, bf16[4,512,2048]{2,1,0:T(8,128)(2,1)S(1)}) custom-call(s32[2]{0:T(128)S(1)} %pad_add_fusion.where, bf16[32,2048]{1,0:T(8,128)(2,1)S(1)} %collective-permute-done.refs_0_, bf16[32,2048]{1,0:T(8,128)(2,1)S(1)} %collective-permute-done.4.refs_1_, bf16[32,2048]{1,0:T(8,128)(2,1)S(1)} %collective-permute-done.5.refs_2_, ...), custom_call_target="tpu_custom_call" | custom-call | flops 2147483648 | bytes 16777216 | tf_op jit(solution)/shard_map/gate_up/pallas_call | solution.py:236
  50.3 4.6 %down.4 = (f32[64,2560]{1,0:T(8,128)S(1)}, bf16[64,2560]{1,0:T(8,128)(2,1)S(1)}, bf16[4,512,2048]{2,1,0:T(8,128)(2,1)S(1)}) custom-call(s32[2]{0:T(128)S(1)} %pad_add_fusion.where, bf16[128,2048]{1,0:T(8,128)(2,1)S(1)} %get-tuple-element.96.hidden, bf16[2048,8192]{1,0:T(8,128)(2,1)} %dl.7, f32[16,8192]{1,0:T(8,128)S(1)} %get-tuple-element.81.ds, ...), custom_call_target="tpu_custom_call" | custom-call | flops 1073741824 | bytes 8388608 | tf_op jit(solution)/shard_map/down/pallas_call | solution.py:313
  54.9 0.4 collective-permute-start.15
  55.3 4.1 %down.5 = (f32[64,2048]{1,0:T(8,128)S(1)}, bf16[64,2048]{1,0:T(8,128)(2,1)S(1)}, bf16[4,512,2048]{2,1,0:T(8,128)(2,1)S(1)}) custom-call(s32[2]{0:T(128)S(1)} %pad_add_fusion.where, bf16[128,2048]{1,0:T(8,128)(2,1)S(1)} %get-tuple-element.96.hidden, bf16[2048,8192]{1,0:T(8,128)(2,1)} %dl.7, f32[16,8192]{1,0:T(8,128)S(1)} %get-tuple-element.81.ds, ...), custom_call_target="tpu_custom_call" | custom-call | flops 1073741824 | bytes 8388608 | tf_op jit(solution)/shard_map/down/pallas_call | solution.py:313
  59.4 0.3 collective-permute-start.20
  59.7 0.1 pair.4
  59.7 0.6 collective-permute-start.16
  60.4 4.1 %down.6 = (f32[64,2048]{1,0:T(8,128)S(1)}, bf16[64,2048]{1,0:T(8,128)(2,1)S(1)}, bf16[4,512,2048]{2,1,0:T(8,128)(2,1)S(1)}) custom-call(s32[2]{0:T(128)S(1)} %pad_add_fusion.where, bf16[128,2048]{1,0:T(8,128)(2,1)S(1)} %get-tuple-element.96.hidden, bf16[2048,8192]{1,0:T(8,128)(2,1)} %dl.7, f32[16,8192]{1,0:T(8,128)S(1)} %get-tuple-element.81.ds, ...), custom_call_target="tpu_custom_call" | custom-call | flops 1073741824 | bytes 8388608 | tf_op jit(solution)/shard_map/down/pallas_call | solution.py:313
  64.5 0.1 collective-permute-start.23
  64.6 0.5 collective-permute-start.18
  65.1 0.1 collective-permute-start.19
  65.2 1.6 %collective-permute-start.22 = (bf16[32,2048]{1,0:T(8,128)(2,1)S(1)}, bf16[32,2048]{1,0:T(8,128)(2,1)S(1)}, u32[]{:S(2)}, u32[]{:S(2)}) collective-permute-start(bf16[32,2048]{1,0:T(8,128)(2,1)S(1)} %get-tuple-element.92), channel_id=1, source_target_pairs={{0,8},{4,12},{8,0},{12,4},{1,9},{5,13},{9,1},{13,5},{2,10},{6,14},... | collective-permute-start | bytes 393224 | tf_op jit(solution)/shard_map/ppermute | solution.py:501
  66.7 0.2 message.1
  66.9 2.6 %down.7 = (f32[64,2048]{1,0:T(8,128)S(1)}, bf16[64,2048]{1,0:T(8,128)(2,1)S(1)}) custom-call(s32[2]{0:T(128)S(1)} %pad_add_fusion.where, bf16[128,2048]{1,0:T(8,128)(2,1)S(1)} %get-tuple-element.96.hidden, bf16[2048,8192]{1,0:T(8,128)(2,1)} %dl.7, f32[16,8192]{1,0:T(8,128)S(1)} %get-tuple-element.81.ds, bf16[4,512,2048]{2,1,0:T(8,128)(2,1)S(1)} %get-tuple-element.98.d_held), custom_call_target="tpu_custom_call" | custom-call | flops 1073741824 | bytes 8388608 | tf_op jit(solution)/shard_map/down/pallas_call | solution.py:313
  69.5 0.2 collective-permute-start.21
  69.7 3.5 %collective-permute-start.25 = (bf16[32,2176]{1,0:T(8,128)(2,1)S(1)}, bf16[32,2176]{1,0:T(8,128)(2,1)S(1)}, u32[]{:S(2)}, u32[]{:S(2)}) collective-permute-start(bf16[32,2176]{1,0:T(8,128)(2,1)S(1)} %get-tuple-element.94), channel_id=1, source_target_pairs={{0,2},{1,3},{2,0},{3,1},{4,6},{5,7},{6,4},{7,5},{8,10},{9,11},{10,... | collective-permute-start | bytes 417800 | tf_op jit(solution)/shard_map/ppermute | solution.py:504
  73.3 1.7 %collective-permute-start.24 = (bf16[32,2048]{1,0:T(8,128)(2,1)S(1)}, bf16[32,2048]{1,0:T(8,128)(2,1)S(1)}, u32[]{:S(2)}, u32[]{:S(2)}) collective-permute-start(bf16[32,2048]{1,0:T(8,128)(2,1)S(1)} %get-tuple-element.105), channel_id=1, source_target_pairs={{0,8},{4,12},{8,0},{12,4},{1,9},{5,13},{9,1},{13,5},{2,10},{6,14},... | collective-permute-start | bytes 393224 | tf_op jit(solution)/shard_map/ppermute | solution.py:501
  75.0 3.8 %collective-permute-done.24.refs_1_ = bf16[32,2048]{1,0:T(8,128)(2,1)S(1)} collective-permute-done((bf16[32,2048]{1,0:T(8,128)(2,1)S(1)}, bf16[32,2048]{1,0:T(8,128)(2,1)S(1)}, u32[]{:S(2)}, u32[]{:S(2)}) %collective-permute-start.24) | collective-permute-done | bytes 131104 | tf_op jit(solution)/shard_map/ppermute | solution.py:501
  78.8 1.4 %collective-permute-start.27 = (bf16[32,2176]{1,0:T(8,128)(2,1)S(1)}, bf16[32,2176]{1,0:T(8,128)(2,1)S(1)}, u32[]{:S(2)}, u32[]{:S(2)}) collective-permute-start(bf16[32,2176]{1,0:T(8,128)(2,1)S(1)} %attach.2), channel_id=1, source_target_pairs={{0,3},{1,2},{2,1},{3,0},{4,7},{5,6},{6,5},{7,4},{8,11},{9,10},{10,... | collective-permute-start | bytes 417800 | tf_op jit(solution)/shard_map/ppermute | solution.py:504
  80.3 0.1 collective-permute-done.25.refs_6_
  80.4 1.0 %collective-permute-start.28 = (bf16[32,2176]{1,0:T(8,128)(2,1)S(1)}, bf16[32,2176]{1,0:T(8,128)(2,1)S(1)}, u32[]{:S(2)}, u32[]{:S(2)}) collective-permute-start(bf16[32,2176]{1,0:T(8,128)(2,1)S(1)} %attach.3), channel_id=1, source_target_pairs={{0,1},{1,0},{2,3},{3,2},{4,5},{5,4},{6,7},{7,6},{8,9},{9,8},{10,11... | collective-permute-start | bytes 417800 | tf_op jit(solution)/shard_map/ppermute | solution.py:504
  81.5 0.6 collective-permute-start.26
  82.1 4.9 %collective-permute-done.27.refs_7_ = bf16[32,2176]{1,0:T(8,128)(2,1)S(1)} collective-permute-done((bf16[32,2176]{1,0:T(8,128)(2,1)S(1)}, bf16[32,2176]{1,0:T(8,128)(2,1)S(1)}, u32[]{:S(2)}, u32[]{:S(2)}) %collective-permute-start.27) | collective-permute-done | bytes 139296 | tf_op jit(solution)/shard_map/ppermute | solution.py:504
  87.0 1.5 %collective-permute-done.28.refs_8_ = bf16[32,2176]{1,0:T(8,128)(2,1)S(1)} collective-permute-done((bf16[32,2176]{1,0:T(8,128)(2,1)S(1)}, bf16[32,2176]{1,0:T(8,128)(2,1)S(1)}, u32[]{:S(2)}, u32[]{:S(2)}) %collective-permute-start.28) | collective-permute-done | bytes 139296 | tf_op jit(solution)/shard_map/ppermute | solution.py:504
  88.5 1.8 %final.1 = bf16[32,2048]{1,0:T(8,128)(2,1)} custom-call(s32[2]{0:T(128)S(1)} %pad_add_fusion.where, s32[32,1]{1,0:T(8,128)S(1)} %get-tuple-element.57.pool_row, bf16[32,128]{1,0:T(8,128)(2,1)S(1)} %get-tuple-element.87.low, bf16[128,2048]{1,0:T(8,128)(2,1)S(1)} %bitcast.8, bf16[128,2048]{1,0:T(8,128)(2,1)S(1)} %collective-permute-done.17.refs_1_, ...), custom_call_target="tpu_custom_call" | custom-call | tf_op jit(solution)/shard_map/final/pallas_call | solution.py:458
  (34 shorter events, 0.3 us)
Async XLA Ops:
  0.0 11.7 %collective-permute-start.1 = (bf16[32,2048]{1,0:T(8,128)(2,1)}, bf16[32,2048]{1,0:T(8,128)(2,1)S(1)}, u32[]{:S(2)}, u32[]{:S(2)}) collective-permute-start(bf16[32,2048]{1,0:T(8,128)(2,1)} %refs_0_.2), channel_id=1, source_target_pairs={{0,8},{4,12},{8,0},{12,4},{1,9},{5,13},{9,1},{13,5},{2,10},{6,14},... | collective-permute-start | bytes 393224 | tf_op jit(solution)/shard_map/ppermute | solution.py:501
  2.9 11.8 %collective-permute-start.11 = (bf16[32,2048]{1,0:T(8,128)(2,1)}, bf16[32,2048]{1,0:T(8,128)(2,1)S(1)}, u32[]{:S(2)}, u32[]{:S(2)}) collective-permute-start(bf16[32,2048]{1,0:T(8,128)(2,1)} %refs_0_.2), channel_id=1, source_target_pairs={{0,1},{1,0},{2,3},{3,2},{4,5},{5,4},{6,7},{7,6},{8,9},{9,8},{10,11... | collective-permute-start | bytes 393224 | tf_op jit(solution)/shard_map/ppermute | solution.py:504
  4.6 7.0 %copy-start.2 = (bf16[32,2048]{1,0:T(8,128)(2,1)S(1)}, bf16[32,2048]{1,0:T(8,128)(2,1)}, u32[]{:S(2)}) copy-start(bf16[32,2048]{1,0:T(8,128)(2,1)} %refs_0_.2) | copy-start | bytes 393220
  11.6 3.2 %collective-permute-start.2 = (bf16[32,2048]{1,0:T(8,128)(2,1)S(1)}, bf16[32,2048]{1,0:T(8,128)(2,1)S(1)}, u32[]{:S(2)}, u32[]{:S(2)}) collective-permute-start(bf16[32,2048]{1,0:T(8,128)(2,1)S(1)} %copy-done.2), channel_id=1, source_target_pairs={{0,4},{4,0},{8,12},{12,8},{1,5},{5,1},{9,13},{13,9},{2,6},{6,2},{1... | collective-permute-start | bytes 393224 | tf_op jit(solution)/shard_map/ppermute | solution.py:498
  11.7 3.7 %collective-permute-start.3 = (bf16[32,2048]{1,0:T(8,128)(2,1)S(1)}, bf16[32,2048]{1,0:T(8,128)(2,1)S(1)}, u32[]{:S(2)}, u32[]{:S(2)}) collective-permute-start(bf16[32,2048]{1,0:T(8,128)(2,1)S(1)} %collective-permute-done.1.refs_1_), channel_id=1, source_target_pairs={{0,4},{4,0},{8,12},{12,8},{1,5},{5,1},{9,13},{13,9},{2,6},{6,2},{1... | collective-permute-start | bytes 393224 | tf_op jit(solution)/shard_map/ppermute | solution.py:498
  12.2 10.5 %collective-permute-start.7 = (bf16[32,2048]{1,0:T(8,128)(2,1)S(1)}, bf16[32,2048]{1,0:T(8,128)(2,1)S(1)}, u32[]{:S(2)}, u32[]{:S(2)}) collective-permute-start(bf16[32,2048]{1,0:T(8,128)(2,1)S(1)} %copy-done.2), channel_id=1, source_target_pairs={{0,3},{1,2},{2,1},{3,0},{4,7},{5,6},{6,5},{7,4},{8,11},{9,10},{10,... | collective-permute-start | bytes 393224 | tf_op jit(solution)/shard_map/ppermute | solution.py:504
  14.7 12.3 %collective-permute-start = (bf16[32,2048]{1,0:T(8,128)(2,1)S(1)}, bf16[32,2048]{1,0:T(8,128)(2,1)S(1)}, u32[]{:S(2)}, u32[]{:S(2)}) collective-permute-start(bf16[32,2048]{1,0:T(8,128)(2,1)S(1)} %copy-done.2), channel_id=1, source_target_pairs={{0,2},{1,3},{2,0},{3,1},{4,6},{5,7},{6,4},{7,5},{8,10},{9,11},{10,... | collective-permute-start | bytes 393224 | tf_op jit(solution)/shard_map/ppermute | solution.py:504
  14.8 12.7 %collective-permute-start.13 = (bf16[32,2048]{1,0:T(8,128)(2,1)S(1)}, bf16[32,2048]{1,0:T(8,128)(2,1)S(1)}, u32[]{:S(2)}, u32[]{:S(2)}) collective-permute-start(bf16[32,2048]{1,0:T(8,128)(2,1)S(1)} %collective-permute-done.11.refs_0_), channel_id=1, source_target_pairs={{0,4},{4,0},{8,12},{12,8},{1,5},{5,1},{9,13},{13,9},{2,6},{6,2},{1... | collective-permute-start | bytes 393224 | tf_op jit(solution)/shard_map/ppermute | solution.py:498
  14.8 9.5 %collective-permute-start.12 = (bf16[32,2048]{1,0:T(8,128)(2,1)S(1)}, bf16[32,2048]{1,0:T(8,128)(2,1)S(1)}, u32[]{:S(2)}, u32[]{:S(2)}) collective-permute-start(bf16[32,2048]{1,0:T(8,128)(2,1)S(1)} %collective-permute-done.11.refs_0_), channel_id=1, source_target_pairs={{0,8},{4,12},{8,0},{12,4},{1,9},{5,13},{9,1},{13,5},{2,10},{6,14},... | collective-permute-start | bytes 393224 | tf_op jit(solution)/shard_map/ppermute | solution.py:501
  22.7 5.6 %collective-permute-start.8 = (bf16[32,2048]{1,0:T(8,128)(2,1)S(1)}, bf16[32,2048]{1,0:T(8,128)(2,1)S(1)}, u32[]{:S(2)}, u32[]{:S(2)}) collective-permute-start(bf16[32,2048]{1,0:T(8,128)(2,1)S(1)} %collective-permute-done.7.refs_0_), channel_id=1, source_target_pairs={{0,8},{4,12},{8,0},{12,4},{1,9},{5,13},{9,1},{13,5},{2,10},{6,14},... | collective-permute-start | bytes 393224 | tf_op jit(solution)/shard_map/ppermute | solution.py:501
  24.3 4.1 %collective-permute-start.14 = (bf16[32,2048]{1,0:T(8,128)(2,1)S(1)}, bf16[32,2048]{1,0:T(8,128)(2,1)S(1)}, u32[]{:S(2)}, u32[]{:S(2)}) collective-permute-start(bf16[32,2048]{1,0:T(8,128)(2,1)S(1)} %collective-permute-done.12.refs_1_), channel_id=1, source_target_pairs={{0,4},{4,0},{8,12},{12,8},{1,5},{5,1},{9,13},{13,9},{2,6},{6,2},{1... | collective-permute-start | bytes 393224 | tf_op jit(solution)/shard_map/ppermute | solution.py:498
  26.9 17.9 %collective-permute-start.5 = (bf16[32,2048]{1,0:T(8,128)(2,1)S(1)}, bf16[32,2048]{1,0:T(8,128)(2,1)S(1)}, u32[]{:S(2)}, u32[]{:S(2)}) collective-permute-start(bf16[32,2048]{1,0:T(8,128)(2,1)S(1)} %collective-permute-done.refs_0_), channel_id=1, source_target_pairs={{0,4},{4,0},{8,12},{12,8},{1,5},{5,1},{9,13},{13,9},{2,6},{6,2},{1... | collective-permute-start | bytes 393224 | tf_op jit(solution)/shard_map/ppermute | solution.py:498
  27.0 10.3 %collective-permute-start.4 = (bf16[32,2048]{1,0:T(8,128)(2,1)S(1)}, bf16[32,2048]{1,0:T(8,128)(2,1)S(1)}, u32[]{:S(2)}, u32[]{:S(2)}) collective-permute-start(bf16[32,2048]{1,0:T(8,128)(2,1)S(1)} %collective-permute-done.refs_0_), channel_id=1, source_target_pairs={{0,8},{4,12},{8,0},{12,4},{1,9},{5,13},{9,1},{13,5},{2,10},{6,14},... | collective-permute-start | bytes 393224 | tf_op jit(solution)/shard_map/ppermute | solution.py:501
  27.5 10.0 %collective-permute-start.9 = (bf16[32,2048]{1,0:T(8,128)(2,1)S(1)}, bf16[32,2048]{1,0:T(8,128)(2,1)S(1)}, u32[]{:S(2)}, u32[]{:S(2)}) collective-permute-start(bf16[32,2048]{1,0:T(8,128)(2,1)S(1)} %collective-permute-done.7.refs_0_), channel_id=1, source_target_pairs={{0,4},{4,0},{8,12},{12,8},{1,5},{5,1},{9,13},{13,9},{2,6},{6,2},{1... | collective-permute-start | bytes 393224 | tf_op jit(solution)/shard_map/ppermute | solution.py:498
  28.4 9.1 %collective-permute-start.10 = (bf16[32,2048]{1,0:T(8,128)(2,1)S(1)}, bf16[32,2048]{1,0:T(8,128)(2,1)S(1)}, u32[]{:S(2)}, u32[]{:S(2)}) collective-permute-start(bf16[32,2048]{1,0:T(8,128)(2,1)S(1)} %collective-permute-done.8.refs_1_), channel_id=1, source_target_pairs={{0,4},{4,0},{8,12},{12,8},{1,5},{5,1},{9,13},{13,9},{2,6},{6,2},{1... | collective-permute-start | bytes 393224 | tf_op jit(solution)/shard_map/ppermute | solution.py:498
  28.4 7.3 %copy-start.1 = (bf16[2,64,2048]{2,1,0:T(8,128)(2,1)S(1)}, bf16[2,64,2048]{2,1,0:T(8,128)(2,1)}, u32[]{:S(2)}) copy-start(bf16[2,64,2048]{2,1,0:T(8,128)(2,1)} %param.24) | copy-start | bytes 1572868
  35.7 29.3 %collective-permute-start.17 = (bf16[128,2048]{1,0:T(8,128)(2,1)S(1)}, bf16[128,2048]{1,0:T(8,128)(2,1)S(1)}, u32[]{:S(2)}, u32[]{:S(2)}) collective-permute-start(bf16[128,2048]{1,0:T(8,128)(2,1)S(1)} %bitcast.6), channel_id=1, source_target_pairs={{0,8},{4,12},{8,0},{12,4},{1,9},{5,13},{9,1},{13,5},{2,10},{6,14},... | collective-permute-start | bytes 1572872 | tf_op jit(solution)/shard_map/ppermute | solution.py:501
  37.3 7.6 %collective-permute-start.6 = (bf16[32,2048]{1,0:T(8,128)(2,1)S(1)}, bf16[32,2048]{1,0:T(8,128)(2,1)S(1)}, u32[]{:S(2)}, u32[]{:S(2)}) collective-permute-start(bf16[32,2048]{1,0:T(8,128)(2,1)S(1)} %collective-permute-done.4.refs_1_), channel_id=1, source_target_pairs={{0,4},{4,0},{8,12},{12,8},{1,5},{5,1},{9,13},{13,9},{2,6},{6,2},{1... | collective-permute-start | bytes 393224 | tf_op jit(solution)/shard_map/ppermute | solution.py:498
  44.8 5.5 %copy-start = (bf16[2048,512]{1,0:T(8,128)(2,1)S(1)}, bf16[2048,512]{1,0:T(8,128)(2,1)}, u32[]{:S(2)}) copy-start(bf16[2048,512]{1,0:T(8,128)(2,1)} %refs_0_.3) | copy-start | bytes 6291460
  54.9 4.8 %collective-permute-start.15 = (bf16[64,2560]{1,0:T(8,128)(2,1)S(1)}, bf16[64,2560]{1,0:T(8,128)(2,1)S(1)}, u32[]{:S(2)}, u32[]{:S(2)}) collective-permute-start(bf16[64,2560]{1,0:T(8,128)(2,1)S(1)} %get-tuple-element.84), channel_id=1, source_target_pairs={{0,4},{4,0},{8,12},{12,8},{1,5},{5,1},{9,13},{13,9},{2,6},{6,2},{1... | collective-permute-start | bytes 983048 | tf_op jit(solution)/shard_map/ppermute | solution.py:498
  59.4 5.7 %collective-permute-start.20 = (bf16[64,2048]{1,0:T(8,128)(2,1)S(1)}, bf16[64,2048]{1,0:T(8,128)(2,1)S(1)}, u32[]{:S(2)}, u32[]{:S(2)}) collective-permute-start(bf16[64,2048]{1,0:T(8,128)(2,1)S(1)} %get-tuple-element.91), channel_id=1, source_target_pairs={{0,4},{4,0},{8,12},{12,8},{1,5},{5,1},{9,13},{13,9},{2,6},{6,2},{1... | collective-permute-start | bytes 786440 | tf_op jit(solution)/shard_map/ppermute | solution.py:498
  59.7 7.0 %collective-permute-start.16 = (bf16[32,2560]{1,0:T(8,128)(2,1)S(1)}, bf16[32,2560]{1,0:T(8,128)(2,1)S(1)}, u32[]{:S(2)}, u32[]{:S(2)}) collective-permute-start(bf16[32,2560]{1,0:T(8,128)(2,1)S(1)} %get-tuple-element.86), channel_id=1, source_target_pairs={{0,8},{4,12},{8,0},{12,4},{1,9},{5,13},{9,1},{13,5},{2,10},{6,14},... | collective-permute-start | bytes 491528 | tf_op jit(solution)/shard_map/ppermute | solution.py:501
  64.5 5.3 %collective-permute-start.23 = (bf16[64,2048]{1,0:T(8,128)(2,1)S(1)}, bf16[64,2048]{1,0:T(8,128)(2,1)S(1)}, u32[]{:S(2)}, u32[]{:S(2)}) collective-permute-start(bf16[64,2048]{1,0:T(8,128)(2,1)S(1)} %get-tuple-element.103), channel_id=1, source_target_pairs={{0,4},{4,0},{8,12},{12,8},{1,5},{5,1},{9,13},{13,9},{2,6},{6,2},{1... | collective-permute-start | bytes 786440 | tf_op jit(solution)/shard_map/ppermute | solution.py:498
  64.6 17.5 %collective-permute-start.18 = (bf16[128,2048]{1,0:T(8,128)(2,1)S(1)}, bf16[128,2048]{1,0:T(8,128)(2,1)S(1)}, u32[]{:S(2)}, u32[]{:S(2)}) collective-permute-start(bf16[128,2048]{1,0:T(8,128)(2,1)S(1)} %bitcast.7), channel_id=1, source_target_pairs={{0,4},{4,0},{8,12},{12,8},{1,5},{5,1},{9,13},{13,9},{2,6},{6,2},{1... | collective-permute-start | bytes 1572872 | tf_op jit(solution)/shard_map/ppermute | solution.py:498
  65.1 23.5 %collective-permute-start.19 = (bf16[128,2048]{1,0:T(8,128)(2,1)S(1)}, bf16[128,2048]{1,0:T(8,128)(2,1)S(1)}, u32[]{:S(2)}, u32[]{:S(2)}) collective-permute-start(bf16[128,2048]{1,0:T(8,128)(2,1)S(1)} %collective-permute-done.17.refs_1_), channel_id=1, source_target_pairs={{0,4},{4,0},{8,12},{12,8},{1,5},{5,1},{9,13},{13,9},{2,6},{6,2},{1... | collective-permute-start | bytes 1572872 | tf_op jit(solution)/shard_map/ppermute | solution.py:498
  65.2 8.1 %collective-permute-start.22 = (bf16[32,2048]{1,0:T(8,128)(2,1)S(1)}, bf16[32,2048]{1,0:T(8,128)(2,1)S(1)}, u32[]{:S(2)}, u32[]{:S(2)}) collective-permute-start(bf16[32,2048]{1,0:T(8,128)(2,1)S(1)} %get-tuple-element.92), channel_id=1, source_target_pairs={{0,8},{4,12},{8,0},{12,4},{1,9},{5,13},{9,1},{13,5},{2,10},{6,14},... | collective-permute-start | bytes 393224 | tf_op jit(solution)/shard_map/ppermute | solution.py:501
  69.5 11.9 %collective-permute-start.21 = (bf16[64,2048]{1,0:T(8,128)(2,1)S(1)}, bf16[64,2048]{1,0:T(8,128)(2,1)S(1)}, u32[]{:S(2)}, u32[]{:S(2)}) collective-permute-start(bf16[64,2048]{1,0:T(8,128)(2,1)S(1)} %get-tuple-element.100), channel_id=1, source_target_pairs={{0,4},{4,0},{8,12},{12,8},{1,5},{5,1},{9,13},{13,9},{2,6},{6,2},{1... | collective-permute-start | bytes 786440 | tf_op jit(solution)/shard_map/ppermute | solution.py:498
  69.7 10.7 %collective-permute-start.25 = (bf16[32,2176]{1,0:T(8,128)(2,1)S(1)}, bf16[32,2176]{1,0:T(8,128)(2,1)S(1)}, u32[]{:S(2)}, u32[]{:S(2)}) collective-permute-start(bf16[32,2176]{1,0:T(8,128)(2,1)S(1)} %get-tuple-element.94), channel_id=1, source_target_pairs={{0,2},{1,3},{2,0},{3,1},{4,6},{5,7},{6,4},{7,5},{8,10},{9,11},{10,... | collective-permute-start | bytes 417800 | tf_op jit(solution)/shard_map/ppermute | solution.py:504
  73.3 5.5 %collective-permute-start.24 = (bf16[32,2048]{1,0:T(8,128)(2,1)S(1)}, bf16[32,2048]{1,0:T(8,128)(2,1)S(1)}, u32[]{:S(2)}, u32[]{:S(2)}) collective-permute-start(bf16[32,2048]{1,0:T(8,128)(2,1)S(1)} %get-tuple-element.105), channel_id=1, source_target_pairs={{0,8},{4,12},{8,0},{12,4},{1,9},{5,13},{9,1},{13,5},{2,10},{6,14},... | collective-permute-start | bytes 393224 | tf_op jit(solution)/shard_map/ppermute | solution.py:501
  78.8 8.2 %collective-permute-start.27 = (bf16[32,2176]{1,0:T(8,128)(2,1)S(1)}, bf16[32,2176]{1,0:T(8,128)(2,1)S(1)}, u32[]{:S(2)}, u32[]{:S(2)}) collective-permute-start(bf16[32,2176]{1,0:T(8,128)(2,1)S(1)} %attach.2), channel_id=1, source_target_pairs={{0,3},{1,2},{2,1},{3,0},{4,7},{5,6},{6,5},{7,4},{8,11},{9,10},{10,... | collective-permute-start | bytes 417800 | tf_op jit(solution)/shard_map/ppermute | solution.py:504
  80.4 8.1 %collective-permute-start.28 = (bf16[32,2176]{1,0:T(8,128)(2,1)S(1)}, bf16[32,2176]{1,0:T(8,128)(2,1)S(1)}, u32[]{:S(2)}, u32[]{:S(2)}) collective-permute-start(bf16[32,2176]{1,0:T(8,128)(2,1)S(1)} %attach.3), channel_id=1, source_target_pairs={{0,1},{1,0},{2,3},{3,2},{4,5},{5,4},{6,7},{7,6},{8,9},{9,8},{10,11... | collective-permute-start | bytes 417800 | tf_op jit(solution)/shard_map/ppermute | solution.py:504
  81.5 7.0 %collective-permute-start.26 = (bf16[32,2048]{1,0:T(8,128)(2,1)S(1)}, bf16[32,2048]{1,0:T(8,128)(2,1)S(1)}, u32[]{:S(2)}, u32[]{:S(2)}) collective-permute-start(bf16[32,2048]{1,0:T(8,128)(2,1)S(1)} %get-tuple-element.108), channel_id=1, source_target_pairs={{0,8},{4,12},{8,0},{12,4},{1,9},{5,13},{9,1},{13,5},{2,10},{6,14},... | collective-permute-start | bytes 393224 | tf_op jit(solution)/shard_map/ppermute | solution.py:501

commit v4 on v3

--- a/solution.py
+++ b/solution.py
@@ -109,9 +109,6 @@
 
 
 def run(steps, stage, ahead):
-    for c in ahead:
-        c.start()
-
     def body(step, carry):
         stage(step)
         return carry
@@ -188,6 +185,8 @@
             preferred_element_type=jnp.float32,
         )
 
+    for c in following:
+        c.start()
     if first:
         gate[...] = jnp.zeros_like(gate)
         up[...] = jnp.zeros_like(up)
@@ -288,6 +287,8 @@
         mine[:, width:] = low[:half]
         theirs[:, width:] = low[half:].astype(jnp.bfloat16)
 
+    for c in following:
+        c.start()
     acc[...] = jnp.zeros_like(acc)
     run(steps, add, following)
     if shrink_too:

time: 90.4 us -> 90 us (level)
  transfers between devices with their start and end apart: 29 -> 29, of which waited for: 6 -> 6; matrix products, arithmetic and copies ran while one was open for 0% -> 0% of each run, Pallas kernels for 56% -> 55%
where the time goes in v4:
time: 90 us; the launch traced here: 89.9 us
  Pallas kernels  51.4 us (57%)
  starting transfers between devices  24.2 us (27%)
  waiting for transfers between devices  13.9 us (15%)
    pallas_call x4, Pallas kernels, gate_up(): pl.pallas_call(functools.partial(gate_up_kernel, pieces, distances, comin...  26.9 us
    pallas_call x4, Pallas kernels, down(): pl.pallas_call(functools.partial(down_kernel, distances, kb, ahead, shrin...  15.4 us
    ppermute x9, starting transfers between devices, chip_swap(): lax.ppermute(v, 'replica', [(r, r ^ s * cores) for r in range(replicas)])  11.5 us
    ppermute x6, starting transfers between devices, tensor_swap(): return lax.ppermute(v, 'tensor', [(t, t ^ d) for t in range(tensors)])  10.2 us
    ppermute x6, waiting for transfers between devices, tensor_swap(): return lax.ppermute(v, 'tensor', [(t, t ^ d) for t in range(tensors)])  9.56 us
    pallas_call x1, Pallas kernels, fill(): pl.pallas_call(functools.partial(fill_kernel, kb, count, depth, order), o...  7 us
    ppermute x9, waiting for transfers between devices, chip_swap(): lax.ppermute(v, 'replica', [(r, r ^ s * cores) for r in range(replicas)])  4.29 us
    ppermute x14, starting transfers between devices, core_swap(): return lax.ppermute(v, 'replica', [(r, r ^ 1) for r in range(replicas)])  2.54 us
  transfers between devices with their start and end apart: 29, of which 6 were waited for; matrix products, arithmetic and copies ran while one was open for 0% of the time, Pallas kernels for 55%

profile of v4, /device:TPU:0, one launch (start us, length us, event | category | flops | bytes accessed | tf_op | source)
XLA Modules:
  0.0 89.9 jit_solution(3954915384142906196)
XLA Ops:
  0.0 2.9 %collective-permute-start.1 = (bf16[32,2048]{1,0:T(8,128)(2,1)}, bf16[32,2048]{1,0:T(8,128)(2,1)S(1)}, u32[]{:S(2)}, u32[]{:S(2)}) collective-permute-start(bf16[32,2048]{1,0:T(8,128)(2,1)} %refs_0_.2), channel_id=1, source_target_pairs={{0,8},{4,12},{8,0},{12,4},{1,9},{5,13},{9,1},{13,5},{2,10},{6,14},... | collective-permute-start | bytes 393224 | tf_op jit(solution)/shard_map/ppermute | solution.py:502
  2.9 1.6 %collective-permute-start.11 = (bf16[32,2048]{1,0:T(8,128)(2,1)}, bf16[32,2048]{1,0:T(8,128)(2,1)S(1)}, u32[]{:S(2)}, u32[]{:S(2)}) collective-permute-start(bf16[32,2048]{1,0:T(8,128)(2,1)} %refs_0_.2), channel_id=1, source_target_pairs={{0,1},{1,0},{2,3},{3,2},{4,5},{5,4},{6,7},{7,6},{8,9},{9,8},{10,11... | collective-permute-start | bytes 393224 | tf_op jit(solution)/shard_map/ppermute | solution.py:505
  4.5 0.1 pad_add_fusion.where
  4.6 7.0 %fill.1 = (bf16[4,512,2048]{2,1,0:T(8,128)(2,1)S(1)}, bf16[4,512,2048]{2,1,0:T(8,128)(2,1)S(1)}, f32[64,2048]{1,0:T(8,128)S(1)}, f32[64,2048]{1,0:T(8,128)S(1)},...) custom-call(s32[2]{0:T(128)S(1)} %pad_add_fusion.where, s32[1,8]{1,0:T(1,128)} %bitcast.9, ...), custom_call_target="tpu_custom_call" | custom-call | bytes 16777216 | tf_op jit(solution)/shard_map/fill/pallas_call | solution.py:90
  11.6 0.1 collective-permute-start.2
  11.7 0.0 collective-permute-done.1.refs_1_
  11.7 0.5 collective-permute-start.3
  12.2 2.5 %collective-permute-start.7 = (bf16[32,2048]{1,0:T(8,128)(2,1)S(1)}, bf16[32,2048]{1,0:T(8,128)(2,1)S(1)}, u32[]{:S(2)}, u32[]{:S(2)}) collective-permute-start(bf16[32,2048]{1,0:T(8,128)(2,1)S(1)} %copy-done.2), channel_id=1, source_target_pairs={{0,3},{1,2},{2,1},{3,0},{4,7},{5,6},{6,5},{7,4},{8,11},{9,10},{10,... | collective-permute-start | bytes 393224 | tf_op jit(solution)/shard_map/ppermute | solution.py:505
  14.7 0.1 collective-permute-start
  14.8 0.0 collective-permute-done.11.refs_0_
  14.8 0.0 collective-permute-start.13
  14.8 0.6 collective-permute-start.12
  15.4 7.2 %gate_up.4 = (f32[128,2048]{1,0:T(8,128)S(1)}, f32[128,2048]{1,0:T(8,128)S(1)}, bf16[4,512,2048]{2,1,0:T(8,128)(2,1)S(1)}, bf16[4,512,2048]{2,1,0:T(8,128)(2,1)S(1)}) custom-call(s32[2]{0:T(128)S(1)} %pad_add_fusion.where, bf16[32,2048]{1,0:T(8,128)(2,1)S(1)} %copy-done.2, bf16[32,2048]{1,0:T(8,128)(2,1)S(1)} %collective-permute-done.1.refs_1_, ...), custom_call_target="tpu_custom_call" | custom-call | flops 2147483648 | bytes 16777216 | tf_op jit(solution)/shard_map/gate_up/pallas_call | solution.py:235
  22.6 1.6 %collective-permute-start.8 = (bf16[32,2048]{1,0:T(8,128)(2,1)S(1)}, bf16[32,2048]{1,0:T(8,128)(2,1)S(1)}, u32[]{:S(2)}, u32[]{:S(2)}) collective-permute-start(bf16[32,2048]{1,0:T(8,128)(2,1)S(1)} %collective-permute-done.7.refs_0_), channel_id=1, source_target_pairs={{0,8},{4,12},{8,0},{12,4},{1,9},{5,13},{9,1},{13,5},{2,10},{6,14},... | collective-permute-start | bytes 393224 | tf_op jit(solution)/shard_map/ppermute | solution.py:502
  24.2 2.8 %collective-permute-done.refs_0_ = bf16[32,2048]{1,0:T(8,128)(2,1)S(1)} collective-permute-done((bf16[32,2048]{1,0:T(8,128)(2,1)S(1)}, bf16[32,2048]{1,0:T(8,128)(2,1)S(1)}, u32[]{:S(2)}, u32[]{:S(2)}) %collective-permute-start) | collective-permute-done | bytes 131104 | tf_op jit(solution)/shard_map/ppermute | solution.py:505
  27.0 0.5 collective-permute-start.4
  27.5 0.2 collective-permute-start.9
  27.7 0.5 collective-permute-done.8.refs_1_
  28.2 7.2 %gate_up.5 = (f32[128,2048]{1,0:T(8,128)S(1)}, f32[128,2048]{1,0:T(8,128)S(1)}, bf16[4,512,2048]{2,1,0:T(8,128)(2,1)S(1)}, bf16[4,512,2048]{2,1,0:T(8,128)(2,1)S(1)}) custom-call(s32[2]{0:T(128)S(1)} %pad_add_fusion.where, bf16[32,2048]{1,0:T(8,128)(2,1)S(1)} %collective-permute-done.11.refs_0_, bf16[32,2048]{1,0:T(8,128)(2,1)S(1)} %collective-permute-done.12.refs_1_, ...), custom_call_target="tpu_custom_call" | custom-call | flops 2147483648 | bytes 16777216 | tf_op jit(solution)/shard_map/gate_up/pallas_call | solution.py:235
  35.4 1.6 %collective-permute-start.17 = (bf16[128,2048]{1,0:T(8,128)(2,1)S(1)}, bf16[128,2048]{1,0:T(8,128)(2,1)S(1)}, u32[]{:S(2)}, u32[]{:S(2)}) collective-permute-start(bf16[128,2048]{1,0:T(8,128)(2,1)S(1)} %bitcast.6), channel_id=1, source_target_pairs={{0,8},{4,12},{8,0},{12,4},{1,9},{5,13},{9,1},{13,5},{2,10},{6,14},... | collective-permute-start | bytes 1572872 | tf_op jit(solution)/shard_map/ppermute | solution.py:502
  37.0 0.2 collective-permute-start.6
  37.2 7.2 %gate_up.6 = (f32[128,2048]{1,0:T(8,128)S(1)}, f32[128,2048]{1,0:T(8,128)S(1)}, bf16[4,512,2048]{2,1,0:T(8,128)(2,1)S(1)}, bf16[4,512,2048]{2,1,0:T(8,128)(2,1)S(1)}) custom-call(s32[2]{0:T(128)S(1)} %pad_add_fusion.where, bf16[32,2048]{1,0:T(8,128)(2,1)S(1)} %collective-permute-done.7.refs_0_, bf16[32,2048]{1,0:T(8,128)(2,1)S(1)} %collective-permute-done.8.refs_1_, ...), custom_call_target="tpu_custom_call" | custom-call | flops 2147483648 | bytes 16777216 | tf_op jit(solution)/shard_map/gate_up/pallas_call | solution.py:235
  44.4 0.0 copy-start
  44.4 5.3 %gate_up.7 = (bf16[128,2048]{1,0:T(8,128)(2,1)S(1)}, bf16[4,512,2048]{2,1,0:T(8,128)(2,1)S(1)}) custom-call(s32[2]{0:T(128)S(1)} %pad_add_fusion.where, bf16[32,2048]{1,0:T(8,128)(2,1)S(1)} %collective-permute-done.refs_0_, bf16[32,2048]{1,0:T(8,128)(2,1)S(1)} %collective-permute-done.4.refs_1_, bf16[32,2048]{1,0:T(8,128)(2,1)S(1)} %collective-permute-done.5.refs_2_, ...), custom_call_target="tpu_custom_call" | custom-call | flops 2147483648 | bytes 16777216 | tf_op jit(solution)/shard_map/gate_up/pallas_call | solution.py:235
  49.8 4.6 %down.4 = (f32[64,2560]{1,0:T(8,128)S(1)}, bf16[64,2560]{1,0:T(8,128)(2,1)S(1)}, bf16[4,512,2048]{2,1,0:T(8,128)(2,1)S(1)}) custom-call(s32[2]{0:T(128)S(1)} %pad_add_fusion.where, bf16[128,2048]{1,0:T(8,128)(2,1)S(1)} %get-tuple-element.96.hidden, bf16[2048,8192]{1,0:T(8,128)(2,1)} %dl.7, f32[16,8192]{1,0:T(8,128)S(1)} %get-tuple-element.81.ds, ...), custom_call_target="tpu_custom_call" | custom-call | flops 1073741824 | bytes 8388608 | tf_op jit(solution)/shard_map/down/pallas_call | solution.py:314
  54.4 0.4 collective-permute-start.15
  54.7 4.1 %down.5 = (f32[64,2048]{1,0:T(8,128)S(1)}, bf16[64,2048]{1,0:T(8,128)(2,1)S(1)}, bf16[4,512,2048]{2,1,0:T(8,128)(2,1)S(1)}) custom-call(s32[2]{0:T(128)S(1)} %pad_add_fusion.where, bf16[128,2048]{1,0:T(8,128)(2,1)S(1)} %get-tuple-element.96.hidden, bf16[2048,8192]{1,0:T(8,128)(2,1)} %dl.7, f32[16,8192]{1,0:T(8,128)S(1)} %get-tuple-element.81.ds, ...), custom_call_target="tpu_custom_call" | custom-call | flops 1073741824 | bytes 8388608 | tf_op jit(solution)/shard_map/down/pallas_call | solution.py:314
  58.9 0.3 collective-permute-start.20
  59.1 0.1 pair.4
  59.2 0.6 collective-permute-start.16
  59.8 4.1 %down.6 = (f32[64,2048]{1,0:T(8,128)S(1)}, bf16[64,2048]{1,0:T(8,128)(2,1)S(1)}, bf16[4,512,2048]{2,1,0:T(8,128)(2,1)S(1)}) custom-call(s32[2]{0:T(128)S(1)} %pad_add_fusion.where, bf16[128,2048]{1,0:T(8,128)(2,1)S(1)} %get-tuple-element.96.hidden, bf16[2048,8192]{1,0:T(8,128)(2,1)} %dl.7, f32[16,8192]{1,0:T(8,128)S(1)} %get-tuple-element.81.ds, ...), custom_call_target="tpu_custom_call" | custom-call | flops 1073741824 | bytes 8388608 | tf_op jit(solution)/shard_map/down/pallas_call | solution.py:314
  63.9 0.1 collective-permute-start.23
  64.0 0.5 collective-permute-start.18
  64.5 0.1 collective-permute-start.19
  64.6 1.6 %collective-permute-start.22 = (bf16[32,2048]{1,0:T(8,128)(2,1)S(1)}, bf16[32,2048]{1,0:T(8,128)(2,1)S(1)}, u32[]{:S(2)}, u32[]{:S(2)}) collective-permute-start(bf16[32,2048]{1,0:T(8,128)(2,1)S(1)} %get-tuple-element.92), channel_id=1, source_target_pairs={{0,8},{4,12},{8,0},{12,4},{1,9},{5,13},{9,1},{13,5},{2,10},{6,14},... | collective-permute-start | bytes 393224 | tf_op jit(solution)/shard_map/ppermute | solution.py:502
  66.2 0.2 message.1
  66.4 2.6 %down.7 = (f32[64,2048]{1,0:T(8,128)S(1)}, bf16[64,2048]{1,0:T(8,128)(2,1)S(1)}) custom-call(s32[2]{0:T(128)S(1)} %pad_add_fusion.where, bf16[128,2048]{1,0:T(8,128)(2,1)S(1)} %get-tuple-element.96.hidden, bf16[2048,8192]{1,0:T(8,128)(2,1)} %dl.7, f32[16,8192]{1,0:T(8,128)S(1)} %get-tuple-element.81.ds, bf16[4,512,2048]{2,1,0:T(8,128)(2,1)S(1)} %get-tuple-element.98.d_held), custom_call_target="tpu_custom_call" | custom-call | flops 1073741824 | bytes 8388608 | tf_op jit(solution)/shard_map/down/pallas_call | solution.py:314
  69.0 0.2 collective-permute-start.21
  69.2 3.6 %collective-permute-start.25 = (bf16[32,2176]{1,0:T(8,128)(2,1)S(1)}, bf16[32,2176]{1,0:T(8,128)(2,1)S(1)}, u32[]{:S(2)}, u32[]{:S(2)}) collective-permute-start(bf16[32,2176]{1,0:T(8,128)(2,1)S(1)} %get-tuple-element.94), channel_id=1, source_target_pairs={{0,2},{1,3},{2,0},{3,1},{4,6},{5,7},{6,4},{7,5},{8,10},{9,11},{10,... | collective-permute-start | bytes 417800 | tf_op jit(solution)/shard_map/ppermute | solution.py:505
  72.9 1.7 %collective-permute-start.24 = (bf16[32,2048]{1,0:T(8,128)(2,1)S(1)}, bf16[32,2048]{1,0:T(8,128)(2,1)S(1)}, u32[]{:S(2)}, u32[]{:S(2)}) collective-permute-start(bf16[32,2048]{1,0:T(8,128)(2,1)S(1)} %get-tuple-element.105), channel_id=1, source_target_pairs={{0,8},{4,12},{8,0},{12,4},{1,9},{5,13},{9,1},{13,5},{2,10},{6,14},... | collective-permute-start | bytes 393224 | tf_op jit(solution)/shard_map/ppermute | solution.py:502
  74.6 3.8 %collective-permute-done.24.refs_1_ = bf16[32,2048]{1,0:T(8,128)(2,1)S(1)} collective-permute-done((bf16[32,2048]{1,0:T(8,128)(2,1)S(1)}, bf16[32,2048]{1,0:T(8,128)(2,1)S(1)}, u32[]{:S(2)}, u32[]{:S(2)}) %collective-permute-start.24) | collective-permute-done | bytes 131104 | tf_op jit(solution)/shard_map/ppermute | solution.py:502
  78.4 1.3 %collective-permute-start.27 = (bf16[32,2176]{1,0:T(8,128)(2,1)S(1)}, bf16[32,2176]{1,0:T(8,128)(2,1)S(1)}, u32[]{:S(2)}, u32[]{:S(2)}) collective-permute-start(bf16[32,2176]{1,0:T(8,128)(2,1)S(1)} %attach.2), channel_id=1, source_target_pairs={{0,3},{1,2},{2,1},{3,0},{4,7},{5,6},{6,5},{7,4},{8,11},{9,10},{10,... | collective-permute-start | bytes 417800 | tf_op jit(solution)/shard_map/ppermute | solution.py:505
  79.8 0.2 collective-permute-done.25.refs_6_
  80.0 1.1 %collective-permute-start.28 = (bf16[32,2176]{1,0:T(8,128)(2,1)S(1)}, bf16[32,2176]{1,0:T(8,128)(2,1)S(1)}, u32[]{:S(2)}, u32[]{:S(2)}) collective-permute-start(bf16[32,2176]{1,0:T(8,128)(2,1)S(1)} %attach.3), channel_id=1, source_target_pairs={{0,1},{1,0},{2,3},{3,2},{4,5},{5,4},{6,7},{7,6},{8,9},{9,8},{10,11... | collective-permute-start | bytes 417800 | tf_op jit(solution)/shard_map/ppermute | solution.py:505
  81.1 0.5 collective-permute-start.26
  81.5 5.0 %collective-permute-done.27.refs_7_ = bf16[32,2176]{1,0:T(8,128)(2,1)S(1)} collective-permute-done((bf16[32,2176]{1,0:T(8,128)(2,1)S(1)}, bf16[32,2176]{1,0:T(8,128)(2,1)S(1)}, u32[]{:S(2)}, u32[]{:S(2)}) %collective-permute-start.27) | collective-permute-done | bytes 139296 | tf_op jit(solution)/shard_map/ppermute | solution.py:505
  86.6 1.5 %collective-permute-done.28.refs_8_ = bf16[32,2176]{1,0:T(8,128)(2,1)S(1)} collective-permute-done((bf16[32,2176]{1,0:T(8,128)(2,1)S(1)}, bf16[32,2176]{1,0:T(8,128)(2,1)S(1)}, u32[]{:S(2)}, u32[]{:S(2)}) %collective-permute-start.28) | collective-permute-done | bytes 139296 | tf_op jit(solution)/shard_map/ppermute | solution.py:505
  88.1 1.8 %final.1 = bf16[32,2048]{1,0:T(8,128)(2,1)} custom-call(s32[2]{0:T(128)S(1)} %pad_add_fusion.where, s32[32,1]{1,0:T(8,128)S(1)} %get-tuple-element.57.pool_row, bf16[32,128]{1,0:T(8,128)(2,1)S(1)} %get-tuple-element.87.low, bf16[128,2048]{1,0:T(8,128)(2,1)S(1)} %bitcast.8, bf16[128,2048]{1,0:T(8,128)(2,1)S(1)} %collective-permute-done.17.refs_1_, ...), custom_call_target="tpu_custom_call" | custom-call | tf_op jit(solution)/shard_map/final/pallas_call | solution.py:459
  (34 shorter events, 0.3 us)
Async XLA Ops:
  0.0 11.7 %collective-permute-start.1 = (bf16[32,2048]{1,0:T(8,128)(2,1)}, bf16[32,2048]{1,0:T(8,128)(2,1)S(1)}, u32[]{:S(2)}, u32[]{:S(2)}) collective-permute-start(bf16[32,2048]{1,0:T(8,128)(2,1)} %refs_0_.2), channel_id=1, source_target_pairs={{0,8},{4,12},{8,0},{12,4},{1,9},{5,13},{9,1},{13,5},{2,10},{6,14},... | collective-permute-start | bytes 393224 | tf_op jit(solution)/shard_map/ppermute | solution.py:502
  2.9 11.8 %collective-permute-start.11 = (bf16[32,2048]{1,0:T(8,128)(2,1)}, bf16[32,2048]{1,0:T(8,128)(2,1)S(1)}, u32[]{:S(2)}, u32[]{:S(2)}) collective-permute-start(bf16[32,2048]{1,0:T(8,128)(2,1)} %refs_0_.2), channel_id=1, source_target_pairs={{0,1},{1,0},{2,3},{3,2},{4,5},{5,4},{6,7},{7,6},{8,9},{9,8},{10,11... | collective-permute-start | bytes 393224 | tf_op jit(solution)/shard_map/ppermute | solution.py:505
  4.6 7.0 %copy-start.2 = (bf16[32,2048]{1,0:T(8,128)(2,1)S(1)}, bf16[32,2048]{1,0:T(8,128)(2,1)}, u32[]{:S(2)}) copy-start(bf16[32,2048]{1,0:T(8,128)(2,1)} %refs_0_.2) | copy-start | bytes 393220
  11.6 3.2 %collective-permute-start.2 = (bf16[32,2048]{1,0:T(8,128)(2,1)S(1)}, bf16[32,2048]{1,0:T(8,128)(2,1)S(1)}, u32[]{:S(2)}, u32[]{:S(2)}) collective-permute-start(bf16[32,2048]{1,0:T(8,128)(2,1)S(1)} %copy-done.2), channel_id=1, source_target_pairs={{0,4},{4,0},{8,12},{12,8},{1,5},{5,1},{9,13},{13,9},{2,6},{6,2},{1... | collective-permute-start | bytes 393224 | tf_op jit(solution)/shard_map/ppermute | solution.py:499
  11.7 3.7 %collective-permute-start.3 = (bf16[32,2048]{1,0:T(8,128)(2,1)S(1)}, bf16[32,2048]{1,0:T(8,128)(2,1)S(1)}, u32[]{:S(2)}, u32[]{:S(2)}) collective-permute-start(bf16[32,2048]{1,0:T(8,128)(2,1)S(1)} %collective-permute-done.1.refs_1_), channel_id=1, source_target_pairs={{0,4},{4,0},{8,12},{12,8},{1,5},{5,1},{9,13},{13,9},{2,6},{6,2},{1... | collective-permute-start | bytes 393224 | tf_op jit(solution)/shard_map/ppermute | solution.py:499
  12.2 10.4 %collective-permute-start.7 = (bf16[32,2048]{1,0:T(8,128)(2,1)S(1)}, bf16[32,2048]{1,0:T(8,128)(2,1)S(1)}, u32[]{:S(2)}, u32[]{:S(2)}) collective-permute-start(bf16[32,2048]{1,0:T(8,128)(2,1)S(1)} %copy-done.2), channel_id=1, source_target_pairs={{0,3},{1,2},{2,1},{3,0},{4,7},{5,6},{6,5},{7,4},{8,11},{9,10},{10,... | collective-permute-start | bytes 393224 | tf_op jit(solution)/shard_map/ppermute | solution.py:505
  14.7 12.3 %collective-permute-start = (bf16[32,2048]{1,0:T(8,128)(2,1)S(1)}, bf16[32,2048]{1,0:T(8,128)(2,1)S(1)}, u32[]{:S(2)}, u32[]{:S(2)}) collective-permute-start(bf16[32,2048]{1,0:T(8,128)(2,1)S(1)} %copy-done.2), channel_id=1, source_target_pairs={{0,2},{1,3},{2,0},{3,1},{4,6},{5,7},{6,4},{7,5},{8,10},{9,11},{10,... | collective-permute-start | bytes 393224 | tf_op jit(solution)/shard_map/ppermute | solution.py:505
  14.8 12.7 %collective-permute-start.13 = (bf16[32,2048]{1,0:T(8,128)(2,1)S(1)}, bf16[32,2048]{1,0:T(8,128)(2,1)S(1)}, u32[]{:S(2)}, u32[]{:S(2)}) collective-permute-start(bf16[32,2048]{1,0:T(8,128)(2,1)S(1)} %collective-permute-done.11.refs_0_), channel_id=1, source_target_pairs={{0,4},{4,0},{8,12},{12,8},{1,5},{5,1},{9,13},{13,9},{2,6},{6,2},{1... | collective-permute-start | bytes 393224 | tf_op jit(solution)/shard_map/ppermute | solution.py:499
  14.8 9.4 %collective-permute-start.12 = (bf16[32,2048]{1,0:T(8,128)(2,1)S(1)}, bf16[32,2048]{1,0:T(8,128)(2,1)S(1)}, u32[]{:S(2)}, u32[]{:S(2)}) collective-permute-start(bf16[32,2048]{1,0:T(8,128)(2,1)S(1)} %collective-permute-done.11.refs_0_), channel_id=1, source_target_pairs={{0,8},{4,12},{8,0},{12,4},{1,9},{5,13},{9,1},{13,5},{2,10},{6,14},... | collective-permute-start | bytes 393224 | tf_op jit(solution)/shard_map/ppermute | solution.py:502
  22.6 5.6 %collective-permute-start.8 = (bf16[32,2048]{1,0:T(8,128)(2,1)S(1)}, bf16[32,2048]{1,0:T(8,128)(2,1)S(1)}, u32[]{:S(2)}, u32[]{:S(2)}) collective-permute-start(bf16[32,2048]{1,0:T(8,128)(2,1)S(1)} %collective-permute-done.7.refs_0_), channel_id=1, source_target_pairs={{0,8},{4,12},{8,0},{12,4},{1,9},{5,13},{9,1},{13,5},{2,10},{6,14},... | collective-permute-start | bytes 393224 | tf_op jit(solution)/shard_map/ppermute | solution.py:502
  24.2 4.1 %collective-permute-start.14 = (bf16[32,2048]{1,0:T(8,128)(2,1)S(1)}, bf16[32,2048]{1,0:T(8,128)(2,1)S(1)}, u32[]{:S(2)}, u32[]{:S(2)}) collective-permute-start(bf16[32,2048]{1,0:T(8,128)(2,1)S(1)} %collective-permute-done.12.refs_1_), channel_id=1, source_target_pairs={{0,4},{4,0},{8,12},{12,8},{1,5},{5,1},{9,13},{13,9},{2,6},{6,2},{1... | collective-permute-start | bytes 393224 | tf_op jit(solution)/shard_map/ppermute | solution.py:499
  26.9 17.5 %collective-permute-start.5 = (bf16[32,2048]{1,0:T(8,128)(2,1)S(1)}, bf16[32,2048]{1,0:T(8,128)(2,1)S(1)}, u32[]{:S(2)}, u32[]{:S(2)}) collective-permute-start(bf16[32,2048]{1,0:T(8,128)(2,1)S(1)} %collective-permute-done.refs_0_), channel_id=1, source_target_pairs={{0,4},{4,0},{8,12},{12,8},{1,5},{5,1},{9,13},{13,9},{2,6},{6,2},{1... | collective-permute-start | bytes 393224 | tf_op jit(solution)/shard_map/ppermute | solution.py:499
  27.0 10.0 %collective-permute-start.4 = (bf16[32,2048]{1,0:T(8,128)(2,1)S(1)}, bf16[32,2048]{1,0:T(8,128)(2,1)S(1)}, u32[]{:S(2)}, u32[]{:S(2)}) collective-permute-start(bf16[32,2048]{1,0:T(8,128)(2,1)S(1)} %collective-permute-done.refs_0_), channel_id=1, source_target_pairs={{0,8},{4,12},{8,0},{12,4},{1,9},{5,13},{9,1},{13,5},{2,10},{6,14},... | collective-permute-start | bytes 393224 | tf_op jit(solution)/shard_map/ppermute | solution.py:502
  27.5 9.7 %collective-permute-start.9 = (bf16[32,2048]{1,0:T(8,128)(2,1)S(1)}, bf16[32,2048]{1,0:T(8,128)(2,1)S(1)}, u32[]{:S(2)}, u32[]{:S(2)}) collective-permute-start(bf16[32,2048]{1,0:T(8,128)(2,1)S(1)} %collective-permute-done.7.refs_0_), channel_id=1, source_target_pairs={{0,4},{4,0},{8,12},{12,8},{1,5},{5,1},{9,13},{13,9},{2,6},{6,2},{1... | collective-permute-start | bytes 393224 | tf_op jit(solution)/shard_map/ppermute | solution.py:499
  28.2 9.0 %collective-permute-start.10 = (bf16[32,2048]{1,0:T(8,128)(2,1)S(1)}, bf16[32,2048]{1,0:T(8,128)(2,1)S(1)}, u32[]{:S(2)}, u32[]{:S(2)}) collective-permute-start(bf16[32,2048]{1,0:T(8,128)(2,1)S(1)} %collective-permute-done.8.refs_1_), channel_id=1, source_target_pairs={{0,4},{4,0},{8,12},{12,8},{1,5},{5,1},{9,13},{13,9},{2,6},{6,2},{1... | collective-permute-start | bytes 393224 | tf_op jit(solution)/shard_map/ppermute | solution.py:499
  28.2 7.2 %copy-start.1 = (bf16[2,64,2048]{2,1,0:T(8,128)(2,1)S(1)}, bf16[2,64,2048]{2,1,0:T(8,128)(2,1)}, u32[]{:S(2)}) copy-start(bf16[2,64,2048]{2,1,0:T(8,128)(2,1)} %param.24) | copy-start | bytes 1572868
  35.4 29.1 %collective-permute-start.17 = (bf16[128,2048]{1,0:T(8,128)(2,1)S(1)}, bf16[128,2048]{1,0:T(8,128)(2,1)S(1)}, u32[]{:S(2)}, u32[]{:S(2)}) collective-permute-start(bf16[128,2048]{1,0:T(8,128)(2,1)S(1)} %bitcast.6), channel_id=1, source_target_pairs={{0,8},{4,12},{8,0},{12,4},{1,9},{5,13},{9,1},{13,5},{2,10},{6,14},... | collective-permute-start | bytes 1572872 | tf_op jit(solution)/shard_map/ppermute | solution.py:502
  37.0 7.4 %collective-permute-start.6 = (bf16[32,2048]{1,0:T(8,128)(2,1)S(1)}, bf16[32,2048]{1,0:T(8,128)(2,1)S(1)}, u32[]{:S(2)}, u32[]{:S(2)}) collective-permute-start(bf16[32,2048]{1,0:T(8,128)(2,1)S(1)} %collective-permute-done.4.refs_1_), channel_id=1, source_target_pairs={{0,4},{4,0},{8,12},{12,8},{1,5},{5,1},{9,13},{13,9},{2,6},{6,2},{1... | collective-permute-start | bytes 393224 | tf_op jit(solution)/shard_map/ppermute | solution.py:499
  44.4 5.4 %copy-start = (bf16[2048,512]{1,0:T(8,128)(2,1)S(1)}, bf16[2048,512]{1,0:T(8,128)(2,1)}, u32[]{:S(2)}) copy-start(bf16[2048,512]{1,0:T(8,128)(2,1)} %refs_0_.3) | copy-start | bytes 6291460
  54.4 4.8 %collective-permute-start.15 = (bf16[64,2560]{1,0:T(8,128)(2,1)S(1)}, bf16[64,2560]{1,0:T(8,128)(2,1)S(1)}, u32[]{:S(2)}, u32[]{:S(2)}) collective-permute-start(bf16[64,2560]{1,0:T(8,128)(2,1)S(1)} %get-tuple-element.84), channel_id=1, source_target_pairs={{0,4},{4,0},{8,12},{12,8},{1,5},{5,1},{9,13},{13,9},{2,6},{6,2},{1... | collective-permute-start | bytes 983048 | tf_op jit(solution)/shard_map/ppermute | solution.py:499
  58.9 5.7 %collective-permute-start.20 = (bf16[64,2048]{1,0:T(8,128)(2,1)S(1)}, bf16[64,2048]{1,0:T(8,128)(2,1)S(1)}, u32[]{:S(2)}, u32[]{:S(2)}) collective-permute-start(bf16[64,2048]{1,0:T(8,128)(2,1)S(1)} %get-tuple-element.91), channel_id=1, source_target_pairs={{0,4},{4,0},{8,12},{12,8},{1,5},{5,1},{9,13},{13,9},{2,6},{6,2},{1... | collective-permute-start | bytes 786440 | tf_op jit(solution)/shard_map/ppermute | solution.py:499
  59.2 7.0 %collective-permute-start.16 = (bf16[32,2560]{1,0:T(8,128)(2,1)S(1)}, bf16[32,2560]{1,0:T(8,128)(2,1)S(1)}, u32[]{:S(2)}, u32[]{:S(2)}) collective-permute-start(bf16[32,2560]{1,0:T(8,128)(2,1)S(1)} %get-tuple-element.86), channel_id=1, source_target_pairs={{0,8},{4,12},{8,0},{12,4},{1,9},{5,13},{9,1},{13,5},{2,10},{6,14},... | collective-permute-start | bytes 491528 | tf_op jit(solution)/shard_map/ppermute | solution.py:502
  63.9 5.3 %collective-permute-start.23 = (bf16[64,2048]{1,0:T(8,128)(2,1)S(1)}, bf16[64,2048]{1,0:T(8,128)(2,1)S(1)}, u32[]{:S(2)}, u32[]{:S(2)}) collective-permute-start(bf16[64,2048]{1,0:T(8,128)(2,1)S(1)} %get-tuple-element.103), channel_id=1, source_target_pairs={{0,4},{4,0},{8,12},{12,8},{1,5},{5,1},{9,13},{13,9},{2,6},{6,2},{1... | collective-permute-start | bytes 786440 | tf_op jit(solution)/shard_map/ppermute | solution.py:499
  64.0 17.5 %collective-permute-start.18 = (bf16[128,2048]{1,0:T(8,128)(2,1)S(1)}, bf16[128,2048]{1,0:T(8,128)(2,1)S(1)}, u32[]{:S(2)}, u32[]{:S(2)}) collective-permute-start(bf16[128,2048]{1,0:T(8,128)(2,1)S(1)} %bitcast.7), channel_id=1, source_target_pairs={{0,4},{4,0},{8,12},{12,8},{1,5},{5,1},{9,13},{13,9},{2,6},{6,2},{1... | collective-permute-start | bytes 1572872 | tf_op jit(solution)/shard_map/ppermute | solution.py:499
  64.5 23.6 %collective-permute-start.19 = (bf16[128,2048]{1,0:T(8,128)(2,1)S(1)}, bf16[128,2048]{1,0:T(8,128)(2,1)S(1)}, u32[]{:S(2)}, u32[]{:S(2)}) collective-permute-start(bf16[128,2048]{1,0:T(8,128)(2,1)S(1)} %collective-permute-done.17.refs_1_), channel_id=1, source_target_pairs={{0,4},{4,0},{8,12},{12,8},{1,5},{5,1},{9,13},{13,9},{2,6},{6,2},{1... | collective-permute-start | bytes 1572872 | tf_op jit(solution)/shard_map/ppermute | solution.py:499
  64.6 8.2 %collective-permute-start.22 = (bf16[32,2048]{1,0:T(8,128)(2,1)S(1)}, bf16[32,2048]{1,0:T(8,128)(2,1)S(1)}, u32[]{:S(2)}, u32[]{:S(2)}) collective-permute-start(bf16[32,2048]{1,0:T(8,128)(2,1)S(1)} %get-tuple-element.92), channel_id=1, source_target_pairs={{0,8},{4,12},{8,0},{12,4},{1,9},{5,13},{9,1},{13,5},{2,10},{6,14},... | collective-permute-start | bytes 393224 | tf_op jit(solution)/shard_map/ppermute | solution.py:502
  69.0 12.1 %collective-permute-start.21 = (bf16[64,2048]{1,0:T(8,128)(2,1)S(1)}, bf16[64,2048]{1,0:T(8,128)(2,1)S(1)}, u32[]{:S(2)}, u32[]{:S(2)}) collective-permute-start(bf16[64,2048]{1,0:T(8,128)(2,1)S(1)} %get-tuple-element.100), channel_id=1, source_target_pairs={{0,4},{4,0},{8,12},{12,8},{1,5},{5,1},{9,13},{13,9},{2,6},{6,2},{1... | collective-permute-start | bytes 786440 | tf_op jit(solution)/shard_map/ppermute | solution.py:499
  69.2 10.8 %collective-permute-start.25 = (bf16[32,2176]{1,0:T(8,128)(2,1)S(1)}, bf16[32,2176]{1,0:T(8,128)(2,1)S(1)}, u32[]{:S(2)}, u32[]{:S(2)}) collective-permute-start(bf16[32,2176]{1,0:T(8,128)(2,1)S(1)} %get-tuple-element.94), channel_id=1, source_target_pairs={{0,2},{1,3},{2,0},{3,1},{4,6},{5,7},{6,4},{7,5},{8,10},{9,11},{10,... | collective-permute-start | bytes 417800 | tf_op jit(solution)/shard_map/ppermute | solution.py:505
  72.9 5.5 %collective-permute-start.24 = (bf16[32,2048]{1,0:T(8,128)(2,1)S(1)}, bf16[32,2048]{1,0:T(8,128)(2,1)S(1)}, u32[]{:S(2)}, u32[]{:S(2)}) collective-permute-start(bf16[32,2048]{1,0:T(8,128)(2,1)S(1)} %get-tuple-element.105), channel_id=1, source_target_pairs={{0,8},{4,12},{8,0},{12,4},{1,9},{5,13},{9,1},{13,5},{2,10},{6,14},... | collective-permute-start | bytes 393224 | tf_op jit(solution)/shard_map/ppermute | solution.py:502
  78.4 8.2 %collective-permute-start.27 = (bf16[32,2176]{1,0:T(8,128)(2,1)S(1)}, bf16[32,2176]{1,0:T(8,128)(2,1)S(1)}, u32[]{:S(2)}, u32[]{:S(2)}) collective-permute-start(bf16[32,2176]{1,0:T(8,128)(2,1)S(1)} %attach.2), channel_id=1, source_target_pairs={{0,3},{1,2},{2,1},{3,0},{4,7},{5,6},{6,5},{7,4},{8,11},{9,10},{10,... | collective-permute-start | bytes 417800 | tf_op jit(solution)/shard_map/ppermute | solution.py:505
  80.0 8.1 %collective-permute-start.28 = (bf16[32,2176]{1,0:T(8,128)(2,1)S(1)}, bf16[32,2176]{1,0:T(8,128)(2,1)S(1)}, u32[]{:S(2)}, u32[]{:S(2)}) collective-permute-start(bf16[32,2176]{1,0:T(8,128)(2,1)S(1)} %attach.3), channel_id=1, source_target_pairs={{0,1},{1,0},{2,3},{3,2},{4,5},{5,4},{6,7},{7,6},{8,9},{9,8},{10,11... | collective-permute-start | bytes 417800 | tf_op jit(solution)/shard_map/ppermute | solution.py:505
  81.1 7.0 %collective-permute-start.26 = (bf16[32,2048]{1,0:T(8,128)(2,1)S(1)}, bf16[32,2048]{1,0:T(8,128)(2,1)S(1)}, u32[]{:S(2)}, u32[]{:S(2)}) collective-permute-start(bf16[32,2048]{1,0:T(8,128)(2,1)S(1)} %get-tuple-element.108), channel_id=1, source_target_pairs={{0,8},{4,12},{8,0},{12,4},{1,9},{5,13},{9,1},{13,5},{2,10},{6,14},... | collective-permute-start | bytes 393224 | tf_op jit(solution)/shard_map/ppermute | solution.py:502
